TPU v7x, 512 devices: a whole 4x4x16 slice. The times are simulated.
512 devices in a mesh: pipe: 64 (over x_lo, z, core), tp: 8 (over x_hi, y).
Axes of the slice: x: 4 (x_hi: 2, x_lo: 2; x = x_hi * 2 + x_lo), y: 4, z: 16, core: 2. Of those that a mesh axis runs over, the one named last changes fastest.
Arguments:
- carried: bfloat16 [64, 256, 4096], P('pipe', None, 'tp'), may hold values from -8 to 8
- fresh: bfloat16 [2, 256, 4096], P(None, None, 'tp'), may hold values from -8 to 8
- gains: bfloat16 [64, 4096], P('pipe', 'tp'), may hold values from 0.25 to 1.75
- qkv_weight: bfloat16 [64, 4096, 2304], P('pipe', 'tp'), may hold values from -1 to 1
- out_weight: bfloat16 [64, 2048, 4096], P('pipe', None, 'tp'), may hold values from -0.125 to 0.125
- segments: int32 [66, 256], replicated, may hold values from 0 to 15, never falling along the last dimension, each value on 1 to 128 neighbouring positions
- evict_tick: int32 [64], P('pipe'), may hold values from 0 to 2
Outputs:
- section_out: bfloat16 [64, 256, 4096], P('pipe', None, 'tp')
- evicted: bfloat16 [64, 256, 4096], P('pipe', None, 'tp')
Inputs may be any that keep to these rules, and one draw needn't show every extreme that they name: `segments`: segment ids never fall along a row.
All inputs are finite; a program needn't handle non-finite values.
Results may differ from a plain program's by a relative error of at most 0.015.
Values may be sent and summed in bfloat16 or wider, within the bound.
No kernel may reach another device: no remote copies, remote signals or barrier semaphores. Data moves between devices by JAX's collectives and lax.ppermute only.
A program may use at most 64 MiB of HBM per device.

v0:
```python
import jax
import jax.numpy as jnp
from jax import lax
from jax.sharding import PartitionSpec as P

HEAD_DIM = 128
KV_HEADS = 1
Q_HEADS = 16


norm_eps = 1e-05


def from_behind(value, axis, by):
    length = lax.axis_size(axis)
    pairs = [(i, i + by) for i in range(length) if 0 <= i + by < length]
    return lax.ppermute(value, axis, pairs)


def attend(queries, keys, values, query_pos, key_pos, query_seg, key_seg):
    row_count = queries.shape[0]
    length = keys.shape[0]
    kv_count = keys.shape[1] // HEAD_DIM
    group_size = queries.shape[1] // HEAD_DIM // kv_count
    query_blocks = queries.reshape(row_count, kv_count, group_size, HEAD_DIM)
    key_blocks = keys.reshape(length, kv_count, HEAD_DIM)
    value_blocks = values.reshape(length, kv_count, HEAD_DIM)
    scores = jnp.einsum(
        "rkgd,tkd->kgrt", query_blocks, key_blocks, preferred_element_type=jnp.float32
    ) * HEAD_DIM ** (-0.5)
    visible = (query_seg[:, None] == key_seg[None, :]) & (query_pos[:, None] >= key_pos[None, :])
    scores = jnp.where(visible, scores, jnp.float32(-1e30))
    highest = jnp.max(scores, axis=-1, keepdims=True)
    exponentials = jnp.where(visible, jnp.exp(scores - highest), jnp.float32(0.0))
    totals = jnp.sum(exponentials, axis=-1, keepdims=True)
    attention = (exponentials / totals).astype(jnp.bfloat16)
    mixed = jnp.einsum(
        "kgrt,tkd->rkgd", attention, value_blocks, preferred_element_type=jnp.float32
    )
    return mixed.reshape(row_count, kv_count * group_size * HEAD_DIM).astype(jnp.bfloat16)


def section_layer(current, gain, qkv_weight, out_weight, section_segments):
    wide_input = current.astype(jnp.float32)
    total_width = current.shape[1] * lax.axis_size("tp")
    square_sums = lax.psum(jnp.sum(wide_input * wide_input, axis=1), "tp")
    scale = lax.rsqrt(square_sums / total_width + norm_eps)
    normed = (wide_input * scale[:, None] * gain.astype(jnp.float32)).astype(jnp.bfloat16)
    partial_proj = jnp.dot(normed, qkv_weight, preferred_element_type=jnp.float32)
    query_width = Q_HEADS * HEAD_DIM
    key_width = KV_HEADS * HEAD_DIM
    positions = jnp.arange(current.shape[0], dtype=jnp.int32)
    projected = lax.psum(partial_proj, "tp").astype(jnp.bfloat16)
    mixed = attend(
        projected[:, :query_width],
        projected[:, query_width : query_width + key_width],
        projected[:, query_width + key_width :],
        positions,
        positions,
        section_segments,
        section_segments,
    )
    return (wide_input + jnp.dot(mixed, out_weight, preferred_element_type=jnp.float32)).astype(
        jnp.bfloat16
    )


def shards(carried, fresh, gains, qkv_weight, out_weight, segments, evict_tick):
    section_index = lax.axis_index("pipe")
    pipe_count = lax.axis_size("pipe")
    tick_total = fresh.shape[0] + 1
    current = carried[0]
    chosen = jnp.zeros_like(current)
    result = current
    for tick_index in range(tick_total):
        if tick_index > 0:
            arrived = from_behind(result, "pipe", 1)
            current = jnp.where(section_index == 0, fresh[tick_index - 1], arrived)
        item_index = section_index - tick_index + tick_total - 1
        section_segments = lax.dynamic_slice_in_dim(segments, item_index, 1, 0)[0]
        chosen = jnp.where(evict_tick[0] == tick_index, current, chosen)
        result = section_layer(current, gains[0], qkv_weight[0], out_weight[0], section_segments)
    outgoing = jnp.where(section_index < pipe_count // 2, chosen, jnp.zeros_like(chosen))
    pieces = outgoing.reshape(pipe_count, -1)
    spread = lax.all_to_all(pieces, "pipe", split_axis=0, concat_axis=0, tiled=True)
    landed = lax.all_to_all(spread[::-1], "pipe", split_axis=0, concat_axis=0, tiled=True)
    outgoing = landed.reshape(chosen.shape)
    return (result[None], outgoing[None])


def solution(mesh):
    placed = (
        P("pipe", None, "tp"),
        P(None, None, "tp"),
        P("pipe", "tp"),
        P("pipe", "tp", None),
        P("pipe", None, "tp"),
        P(),
        P("pipe"),
    )
    return jax.shard_map(
        shards,
        mesh=mesh,
        in_specs=placed,
        out_specs=(P("pipe", None, "tp"), P("pipe", None, "tp")),
        check_vma=False,
    )
```

profile of v0, /device:TPU:1, one launch (start us, length us, event | category | flops | bytes accessed | tf_op | source)
XLA Modules:
  0.0 430.8 jit_solution(15935677250914513631)
XLA Ops:
  0.6 1.2 fusion.67
  1.9 21.5 %psum.42 = f32[256]{0:T(256)S(1)} all-reduce(f32[256]{0:T(256)S(1)} %fusion.67), channel_id=1, replica_groups=mesh['pipe'=64,'tp'=8] {'tp'}, use_global_device_ids=true, to_apply=%region_1.2 | all-reduce | flops 256 | bytes 2048 | tf_op jit(solution)/shard_map/psum | solution.py:46
  23.4 0.7 mul.113
  24.1 0.8 constant_dynamic-slice_fusion
  24.9 0.7 fusion.88
  25.6 3.2 fusion.10
  28.8 71.6 %all-reduce.3 = bf16[256,2304]{1,0:T(8,128)(2,1)S(1)} all-reduce(f32[256,2304]{1,0:T(8,128)} %fusion.10), channel_id=1, replica_groups=mesh['pipe'=64,'tp'=8] {'tp'}, use_global_device_ids=true, to_apply=%region_2.3 | all-reduce | flops 589824 | bytes 3538944 | tf_op jit(solution)/shard_map/psum | solution.py:53
  100.4 1.8 fusion
  102.2 1.0 fusion.3
  103.3 2.4 fusion.27
  105.8 0.7 fusion.51
  106.5 15.9 %collective-permute-start = (bf16[256,512]{1,0:T(8,128)(2,1)S(1)}, bf16[256,512]{1,0:T(8,128)(2,1)S(1)}, u32[]{:S(2)}, u32[]{:S(2)}) collective-permute-start(bf16[256,512]{1,0:T(8,128)(2,1)S(1)} %fusion.51), channel_id=1, source_target_pairs={{0,8},{8,16},{16,24},{24,32},{32,40},{40,48},{48,56},{56,64},{64,7... | collective-permute-start | bytes 786440 | tf_op jit(solution)/shard_map/ppermute | solution.py:17
  122.6 3.7 collective-permute-done
  126.3 1.1 fusion.70
  127.4 19.4 %psum.44 = f32[256]{0:T(256)S(1)} all-reduce(f32[256]{0:T(256)S(1)} %get-tuple-element.4), channel_id=1, replica_groups=mesh['pipe'=64,'tp'=8] {'tp'}, use_global_device_ids=true, to_apply=%region_6.7 | all-reduce | flops 256 | bytes 2048 | tf_op jit(solution)/shard_map/psum | solution.py:46
  146.8 2.2 fusion.8
  149.0 71.8 %all-reduce.4 = bf16[256,2304]{1,0:T(8,128)(2,1)} all-reduce(f32[256,2304]{1,0:T(8,128)} %fusion.8), channel_id=1, replica_groups=mesh['pipe'=64,'tp'=8] {'tp'}, use_global_device_ids=true, to_apply=%region_7.8 | all-reduce | flops 589824 | bytes 3538944 | tf_op jit(solution)/shard_map/psum | solution.py:53
  220.8 2.1 fusion.1
  222.9 1.0 fusion.4
  223.9 2.4 fusion.30
  226.4 0.7 fusion.48
  227.1 17.0 %collective-permute-start.1 = (bf16[256,512]{1,0:T(8,128)(2,1)S(1)}, bf16[256,512]{1,0:T(8,128)(2,1)S(1)}, u32[]{:S(2)}, u32[]{:S(2)}) collective-permute-start(bf16[256,512]{1,0:T(8,128)(2,1)S(1)} %fusion.48), channel_id=1, source_target_pairs={{0,8},{8,16},{16,24},{24,32},{32,40},{40,48},{48,56},{56,64},{64,7... | collective-permute-start | bytes 786440 | tf_op jit(solution)/shard_map/ppermute | solution.py:17
  244.9 2.5 collective-permute-done.1
  247.4 1.7 fusion.81
  249.1 0.1 fusion.73
  249.3 19.2 %psum.46 = f32[256]{0:T(256)S(1)} all-reduce(f32[256]{0:T(256)S(1)} %fusion.73), channel_id=1, replica_groups=mesh['pipe'=64,'tp'=8] {'tp'}, use_global_device_ids=true, to_apply=%region_11.12 | all-reduce | flops 256 | bytes 2048 | tf_op jit(solution)/shard_map/psum | solution.py:46
  268.5 2.0 all_to_all.19
  270.5 0.5 broadcast.90
  271.0 2.2 reduce.7
  273.2 0.9 reshape.149
  274.1 25.2 %all-to-all-start = ((bf16[64,2,1024]{2,1,0:T(2,128)(2,1)}), bf16[64,2,1024]{2,1,0:T(2,128)(2,1)S(1)}, u32[]{:S(2)}, u32[]{:S(2)}) async-start(bf16[64,2,1024]{2,1,0:T(2,128)(2,1)} %reshape.149), calls=%async_computation | async-start | bytes 524288 | tf_op jit(solution)/shard_map/all_to_all | solution.py:85
  299.3 2.2 fusion.6
  301.5 73.8 %all-reduce.5 = bf16[256,2304]{1,0:T(8,128)(2,1)} all-reduce(f32[256,2304]{1,0:T(8,128)} %fusion.6), channel_id=1, replica_groups=mesh['pipe'=64,'tp'=8] {'tp'}, use_global_device_ids=true, to_apply=%region_12.13 | all-reduce | flops 589824 | bytes 3538944 | tf_op jit(solution)/shard_map/psum | solution.py:53
  375.3 2.1 fusion.2
  377.4 1.9 copy-done.1
  379.3 1.0 fusion.5
  380.3 0.2 reshape.150
  380.6 0.2 copy.72
  380.7 0.5 rev.3
  381.2 0.8 reduce.8
  382.0 0.9 reshape.151
  382.8 23.1 %all-to-all-start.1 = ((bf16[64,2,1024]{2,1,0:T(2,128)(2,1)}), bf16[64,2,1024]{2,1,0:T(2,128)(2,1)S(1)}, u32[]{:S(2)}, u32[]{:S(2)}) async-start(bf16[64,2,1024]{2,1,0:T(2,128)(2,1)} %reshape.151), calls=%async_computation.1 | async-start | bytes 524288 | tf_op jit(solution)/shard_map/all_to_all | solution.py:86
  406.0 3.8 fusion.33
  409.8 1.4 fusion.54
  411.2 17.0 %all-to-all-done.1 = bf16[64,2,1024]{2,1,0:T(2,128)(2,1)S(1)} async-done(((bf16[64,2,1024]{2,1,0:T(2,128)(2,1)}), bf16[64,2,1024]{2,1,0:T(2,128)(2,1)S(1)}, u32[]{:S(2)}, u32[]{:S(2)}) %all-to-all-start.1) | async-done | bytes 262176 | tf_op jit(solution)/shard_map/all_to_all | solution.py:86
  428.2 0.2 reshape.152
  428.4 1.5 reduce.6
  430.0 0.9 broadcast_in_dim_reshape.3
  (21 shorter events, 0.3 us)
Async XLA Ops:
  0.6 25.0 %copy-start = (bf16[1,512,2304]{2,1,0:T(8,128)(2,1)S(1)}, bf16[1,512,2304]{2,1,0:T(8,128)(2,1)}, u32[]{:S(2)}) copy-start(bf16[1,512,2304]{2,1,0:T(8,128)(2,1)} %param.10) | copy-start | bytes 7077892
  100.4 1.8 copy-start.3
  100.4 1.8 copy-start.4
  103.3 2.5 copy-start.2
  103.3 2.5 copy-start.5
  106.5 19.8 %collective-permute-start = (bf16[256,512]{1,0:T(8,128)(2,1)S(1)}, bf16[256,512]{1,0:T(8,128)(2,1)S(1)}, u32[]{:S(2)}, u32[]{:S(2)}) collective-permute-start(bf16[256,512]{1,0:T(8,128)(2,1)S(1)} %fusion.51), channel_id=1, source_target_pairs={{0,8},{8,16},{16,24},{24,32},{32,40},{40,48},{48,56},{56,64},{64,7... | collective-permute-start | bytes 786440 | tf_op jit(solution)/shard_map/ppermute | solution.py:17
  223.9 2.5 copy-start.6
  227.1 20.3 %collective-permute-start.1 = (bf16[256,512]{1,0:T(8,128)(2,1)S(1)}, bf16[256,512]{1,0:T(8,128)(2,1)S(1)}, u32[]{:S(2)}, u32[]{:S(2)}) collective-permute-start(bf16[256,512]{1,0:T(8,128)(2,1)S(1)} %fusion.48), channel_id=1, source_target_pairs={{0,8},{8,16},{16,24},{24,32},{32,40},{40,48},{48,56},{56,64},{64,7... | collective-permute-start | bytes 786440 | tf_op jit(solution)/shard_map/ppermute | solution.py:17
  274.1 106.2 %all-to-all-start = ((bf16[64,2,1024]{2,1,0:T(2,128)(2,1)}), bf16[64,2,1024]{2,1,0:T(2,128)(2,1)S(1)}, u32[]{:S(2)}, u32[]{:S(2)}) async-start(bf16[64,2,1024]{2,1,0:T(2,128)(2,1)} %reshape.149), calls=%async_computation | async-start | bytes 524288 | tf_op jit(solution)/shard_map/all_to_all | solution.py:85
  377.3 1.9 copy-start.1
  382.8 45.4 %all-to-all-start.1 = ((bf16[64,2,1024]{2,1,0:T(2,128)(2,1)}), bf16[64,2,1024]{2,1,0:T(2,128)(2,1)S(1)}, u32[]{:S(2)}, u32[]{:S(2)}) async-start(bf16[64,2,1024]{2,1,0:T(2,128)(2,1)} %reshape.151), calls=%async_computation.1 | async-start | bytes 524288 | tf_op jit(solution)/shard_map/all_to_all | solution.py:86
  406.0 3.8 copy-start.7
where the time goes:
time: 432 us; the launch traced here: 431 us
  blocking collectives  277 us (64%)
  starting transfers between devices  81.3 us (19%)
  matrix products  25.2 us (6%)
  waiting for transfers between devices  23.2 us (5%)
  other arithmetic  13.3 us (3%)
  local copies, waits for them, and re-layouts  9.03 us (2%)
    psum x3, blocking collectives, section_layer(): projected = lax.psum(partial_proj, 'tp').astype(jnp.bfloat16)  217 us
    psum x3, blocking collectives, section_layer(): square_sums = lax.psum(jnp.sum(wide_input * wide_input, axis=1), 'tp')  60 us
    ppermute x2, starting transfers between devices, from_behind(): return lax.ppermute(value, axis, pairs)  33 us
    all_to_all x1, starting transfers between devices, shards(): lax.all_to_all(pieces, 'pipe', split_axis=0, concat_axis=0, tiled=True)  25.2 us
    all_to_all x1, starting transfers between devices, shards(): lax.all_to_all(spread[::-1], 'pipe', split_axis=0, concat_axis=0, tiled=T...  23.1 us
    all_to_all x1, waiting for transfers between devices, shards(): lax.all_to_all(spread[::-1], 'pipe', split_axis=0, concat_axis=0, tiled=T...  17 us
    dot_general x3, matrix products, attend(): jnp.einsum('kgrt,tkd->rkgd', attention, value_blocks, preferred_element_t...  8.69 us
  transfers between devices with their start and end apart: 4, of which 3 were waited for; matrix products, arithmetic and copies ran while one was open for 2% of the time, Pallas kernels for 0%

commit v1 on v0

v1 whole, which is shorter than its diff:
```python
import functools

import jax
import jax.numpy as jnp
from jax import lax
from jax.experimental import pallas as pl
from jax.experimental.pallas import tpu as pltpu
from jax.sharding import PartitionSpec as P

HEAD_DIM = 128
Q_HEADS = 16
Q_COLS = Q_HEADS * HEAD_DIM
KV_COLS = 2 * HEAD_DIM
LONGEST_SEGMENT = 128
NORM_EPS = 1e-05
F32 = jnp.float32
BF16 = jnp.bfloat16


def window_blocks(rows):
    return (LONGEST_SEGMENT + rows - 2) // rows + 1


def project_kernel(parts, x_ref, gain_ref, weight_ref, out_ref):
    tokens = x_ref.shape[0]
    rows = tokens // parts
    blocks = window_blocks(rows)
    wide = x_ref[...].astype(F32)
    scaled = (wide * gain_ref[...].astype(F32)).astype(BF16)
    squares = jnp.sum(wide * wide, axis=1, keepdims=True)
    high = squares.astype(BF16).astype(F32)
    low = squares - high
    lane = lax.broadcasted_iota(jnp.int32, (rows, 128), 1)
    step = 256
    for start in range(0, Q_COLS, step):
        tile = jnp.dot(scaled, weight_ref[:, start : start + step], preferred_element_type=F32)
        out_ref[:, :, start : start + step] = tile.astype(BF16).reshape(parts, rows, step)
    tile = jnp.dot(scaled, weight_ref[:, Q_COLS:], preferred_element_type=F32).astype(BF16)
    last = Q_COLS + blocks * KV_COLS
    for j in range(parts):
        sums = jnp.zeros((rows, 128), F32)
        for b in range(blocks):
            at = max(j - blocks + 1 + b, 0) * rows
            start = Q_COLS + b * KV_COLS
            out_ref[j, :, start : start + KV_COLS] = tile[at : at + rows]
            sums = jnp.where(lane == 2 * b, high[at : at + rows], sums)
            sums = jnp.where(lane == 2 * b + 1, low[at : at + rows], sums)
        out_ref[j, :, last:] = sums.astype(BF16)


def attend_kernel(parts, width, place_ref, segments_ref, got_ref, out_ref):
    rows = got_ref.shape[1]
    tokens = rows * parts
    blocks = window_blocks(rows)
    span = blocks * rows
    before = span - rows
    rank = place_ref[0]
    item = place_ref[1]

    def total(start, size):
        value = got_ref[0, :, start : start + size].astype(F32)
        for j in range(1, parts):
            value = value + got_ref[j, :, start : start + size].astype(F32)
        return value

    last = Q_COLS + blocks * KV_COLS
    sums = total(last, 128)
    scales = []
    for b in range(blocks):
        squares = sums[:, 2 * b : 2 * b + 1] + sums[:, 2 * b + 1 : 2 * b + 2]
        scales.append(lax.rsqrt(squares / width + NORM_EPS))
    keys, values = [], []
    for b in range(blocks):
        both = (total(Q_COLS + b * KV_COLS, KV_COLS) * scales[b]).astype(BF16)
        keys.append(both[:, :HEAD_DIM])
        values.append(both[:, HEAD_DIM:])
    keys = jnp.concatenate(keys, axis=0)
    values = jnp.concatenate(values, axis=0)
    queries = []
    for h in range(Q_HEADS):
        queries.append((total(h * HEAD_DIM, HEAD_DIM) * scales[-1]).astype(BF16))
    queries = jnp.concatenate(queries, axis=0)

    first = rank * rows - before
    segment_row = segments_ref[pl.ds(item, 1), :]
    segment_row = pltpu.roll(segment_row, lax.rem(tokens - first, tokens), 1)
    segment_rows = jnp.broadcast_to(segment_row, (rows, tokens))
    column = lax.broadcasted_iota(jnp.int32, (rows, tokens), 1)
    own = lax.broadcasted_iota(jnp.int32, (rows, tokens), 0) + before
    own_segment = jnp.sum(jnp.where(column == own, segment_rows, 0), axis=1, keepdims=True)
    visible = (segment_rows == own_segment) & (column <= own) & (column + first >= 0)
    visible = visible[:, :span]

    scores = lax.dot_general(
        queries, keys, (((1,), (1,)), ((), ())), preferred_element_type=F32
    ) * HEAD_DIM ** (-0.5)
    scores = scores.reshape(Q_HEADS, rows, span)
    scores = jnp.where(visible[None], scores, F32(-1e30))
    highest = jnp.max(scores, axis=-1, keepdims=True)
    exponentials = jnp.where(visible[None], jnp.exp(scores - highest), F32(0.0))
    totals = jnp.sum(exponentials, axis=-1, keepdims=True)
    attention = (exponentials / totals).astype(BF16).reshape(Q_HEADS * rows, span)
    mixed = jnp.dot(attention, values, preferred_element_type=F32).astype(BF16)
    for h in range(Q_HEADS):
        piece = mixed[h * rows : (h + 1) * rows]
        for j in range(parts):
            out_ref[j, :, h * HEAD_DIM : (h + 1) * HEAD_DIM] = piece


def output_kernel(x_ref, mixed_ref, weight_ref, out_ref):
    product = jnp.dot(mixed_ref[...], weight_ref[...], preferred_element_type=F32)
    out_ref[...] = (x_ref[...].astype(F32) + product).astype(BF16)


VMEM = pl.BlockSpec(memory_space=pltpu.VMEM)
SMEM = pl.BlockSpec(memory_space=pltpu.SMEM)
PARAMS = pltpu.CompilerParams(vmem_limit_bytes=24 * 1024 * 1024)


def section_layer(current, gain, qkv_weight, out_weight, segments, place):
    parts = lax.axis_size("tp")
    tokens, width = current.shape
    rows = tokens // parts
    columns = Q_COLS + window_blocks(rows) * KV_COLS + 128
    partial_proj = pl.pallas_call(
        functools.partial(project_kernel, parts),
        out_shape=jax.ShapeDtypeStruct((parts, rows, columns), BF16),
        in_specs=[VMEM] * 3,
        out_specs=VMEM,
        compiler_params=PARAMS,
        name="project",
    )(current, gain, qkv_weight)
    got = lax.all_to_all(partial_proj, "tp", split_axis=0, concat_axis=0, tiled=True)
    mixed = pl.pallas_call(
        functools.partial(attend_kernel, parts, width * parts),
        out_shape=jax.ShapeDtypeStruct((parts, rows, Q_COLS), BF16),
        in_specs=[SMEM, VMEM, VMEM],
        out_specs=VMEM,
        compiler_params=PARAMS,
        name="attend",
    )(place, segments, got)
    mixed = lax.all_to_all(mixed, "tp", split_axis=0, concat_axis=0, tiled=True)
    return pl.pallas_call(
        output_kernel,
        out_shape=jax.ShapeDtypeStruct((tokens, width), BF16),
        in_specs=[VMEM] * 3,
        out_specs=VMEM,
        compiler_params=PARAMS,
        name="project_out",
    )(current, mixed.reshape(tokens, Q_COLS), out_weight)


def shards(carried, fresh, gains, qkv_weight, out_weight, segments, evict_tick):
    section = lax.axis_index("pipe")
    rank = lax.axis_index("tp")
    sections = lax.axis_size("pipe")
    ticks = fresh.shape[0] + 1
    current = carried[0]
    chosen = current
    result = current
    for tick in range(ticks):
        if tick > 0:
            pairs = [(i, i + 1) for i in range(sections - 1)]
            arrived = lax.ppermute(result, "pipe", pairs)
            current = jnp.where(section == 0, fresh[tick - 1], arrived)
            chosen = jnp.where(evict_tick[0] == tick, current, chosen)
        place = jnp.stack([rank, section - tick + ticks - 1]).astype(jnp.int32)
        result = section_layer(current, gains, qkv_weight[0], out_weight[0], segments, place)
    pairs = [(i, sections - 1 - i) for i in range(sections // 2)]
    evicted = lax.ppermute(chosen, "pipe", pairs)
    return (result[None], evicted[None])


def solution(mesh):
    placed = (
        P("pipe", None, "tp"),
        P(None, None, "tp"),
        P("pipe", "tp"),
        P("pipe", "tp", None),
        P("pipe", None, "tp"),
        P(),
        P("pipe"),
    )
    return jax.shard_map(
        shards,
        mesh=mesh,
        in_specs=placed,
        out_specs=(P("pipe", None, "tp"), P("pipe", None, "tp")),
        check_vma=False,
    )
```

time: 432 us -> 201 us (0.47)
  the two profiles are of different devices: /device:TPU:1 before, /device:TPU:231 now
where the time goes in v1:
time: 201 us
  waiting for transfers between devices  101 us (50%)
  starting transfers between devices  38 us (19%)
  blocking collectives  37.9 us (19%)
  Pallas kernels  11.6 us (6%)
  local copies, waits for them, and re-layouts  8.18 us (4%)
    all_to_all x3, waiting for transfers between devices, section_layer(): lax.all_to_all(partial_proj, 'tp', split_axis=0, concat_axis=0, tiled=True)  67.1 us
    all_to_all x2, blocking collectives, section_layer(): mixed = lax.all_to_all(mixed, 'tp', split_axis=0, concat_axis=0, tiled=True)  37.9 us
    ppermute x1, waiting for transfers between devices, shards(): evicted = lax.ppermute(chosen, 'pipe', pairs)  28.4 us
    all_to_all x3, starting transfers between devices, section_layer(): lax.all_to_all(partial_proj, 'tp', split_axis=0, concat_axis=0, tiled=True)  20.2 us
    ppermute x2, starting transfers between devices, shards(): arrived = lax.ppermute(result, 'pipe', pairs)  10.9 us
    unnamed x35, local copies, waits for them, and re-layouts  8.18 us
    ppermute x2, waiting for transfers between devices, shards(): arrived = lax.ppermute(result, 'pipe', pairs)  5.93 us
    all_to_all x1, starting transfers between devices, section_layer(): mixed = lax.all_to_all(mixed, 'tp', split_axis=0, concat_axis=0, tiled=True)  5.59 us
  transfers between devices with their start and end apart: 7, of which 6 were waited for; matrix products, arithmetic and copies ran while one was open for 0% of the time, Pallas kernels for 0%

profile of v1, /device:TPU:231, one launch (start us, length us, event | category | flops | bytes accessed | tf_op | source)
XLA Modules:
  0.0 200.6 jit_solution(12788772225991108270)
XLA Ops:
  0.6 0.0 copy-start
  0.6 1.7 copy-done
  2.3 0.9 copy-done.8
  3.2 0.7 copy-done.11
  3.9 2.0 %project.3 = bf16[8,32,3456]{2,1,0:T(8,128)(2,1)} custom-call(bf16[256,512]{1,0:T(8,128)(2,1)S(1)} %bitcast.29, bf16[1,512]{1,0:T(2,128)(2,1)S(1)} %copy-done.11, bf16[512,2304]{1,0:T(8,128)(2,1)S(1)} %bitcast.20), custom_call_target="tpu_custom_call" | custom-call | tf_op jit(solution)/shard_map/project/pallas_call | solution.py:125
  6.0 7.0 %all-to-all-start = ((bf16[8,32,3456]{2,1,0:T(8,128)(2,1)}), bf16[8,32,3456]{2,1,0:T(8,128)(2,1)S(1)}, u32[]{:S(2)}, u32[]{:S(2)}) async-start(bf16[8,32,3456]{2,1,0:T(8,128)(2,1)} %project.3), calls=%async_computation | async-start | bytes 3538944 | tf_op jit(solution)/shard_map/all_to_all | solution.py:133
  13.0 0.1 pad_add_fusion.place_ref
  13.0 22.3 %all-to-all-done.got_ref = bf16[8,32,3456]{2,1,0:T(8,128)(2,1)S(1)} async-done(((bf16[8,32,3456]{2,1,0:T(8,128)(2,1)}), bf16[8,32,3456]{2,1,0:T(8,128)(2,1)S(1)}, u32[]{:S(2)}, u32[]{:S(2)}) %all-to-all-start) | async-done | bytes 1769504 | tf_op jit(solution)/shard_map/all_to_all | solution.py:133
  35.3 0.0 copy-done.10
  35.3 1.4 attend.3
  36.8 0.0 copy-start.2
  36.8 19.0 %all_to_all.30 = bf16[8,32,2048]{2,1,0:T(8,128)(2,1)S(1)} all-to-all(bf16[8,32,2048]{2,1,0:T(8,128)(2,1)S(1)} %attend.3), channel_id=1, replica_groups=mesh['pipe'=64,'tp'=8] {'tp'}, dimensions={0} | all-to-all | bytes 2097152 | tf_op jit(solution)/shard_map/all_to_all | solution.py:142
  55.8 0.0 copy-done.9
  55.8 0.0 copy-done.2
  55.8 0.0 copy-start.12
  55.8 0.7 project_out.3
  56.5 6.7 %collective-permute-start = (bf16[256,512]{1,0:T(8,128)(2,1)S(1)}, bf16[256,512]{1,0:T(8,128)(2,1)}, u32[]{:S(2)}, u32[]{:S(2)}) collective-permute-start(bf16[256,512]{1,0:T(8,128)(2,1)S(1)} %project_out.3), channel_id=1, source_target_pairs={{0,8},{8,16},{16,24},{24,32},{32,40},{40,48},{48,56},{56,64},{64,7... | collective-permute-start | bytes 786440 | tf_op jit(solution)/shard_map/ppermute | solution.py:164
  63.2 3.3 %collective-permute-done = bf16[256,512]{1,0:T(8,128)(2,1)} collective-permute-done((bf16[256,512]{1,0:T(8,128)(2,1)S(1)}, bf16[256,512]{1,0:T(8,128)(2,1)}, u32[]{:S(2)}, u32[]{:S(2)}) %collective-permute-start) | collective-permute-done | bytes 262176 | tf_op jit(solution)/shard_map/ppermute | solution.py:164
  66.5 0.0 copy-done.13
  66.5 1.0 bitcast_select_fusion.x_ref
  67.5 0.0 copy-done.1
  67.5 0.0 copy-done.12
  67.5 0.8 project.4
  68.3 1.2 copy-done.5
  69.5 6.9 %all-to-all-start.2 = ((bf16[8,32,3456]{2,1,0:T(8,128)(2,1)}), bf16[8,32,3456]{2,1,0:T(8,128)(2,1)}, u32[]{:S(2)}, u32[]{:S(2)}) async-start(bf16[8,32,3456]{2,1,0:T(8,128)(2,1)} %copy-done.5), calls=%async_computation.2 | async-start | bytes 3538944 | tf_op jit(solution)/shard_map/all_to_all | solution.py:133
  76.4 0.1 pad_add_fusion.1.place_ref
  76.5 22.5 %all-to-all-done.2.got_ref = bf16[8,32,3456]{2,1,0:T(8,128)(2,1)} async-done(((bf16[8,32,3456]{2,1,0:T(8,128)(2,1)}), bf16[8,32,3456]{2,1,0:T(8,128)(2,1)}, u32[]{:S(2)}, u32[]{:S(2)}) %all-to-all-start.2) | async-done | bytes 1769504 | tf_op jit(solution)/shard_map/all_to_all | solution.py:133
  99.0 2.4 %attend.4 = bf16[8,32,2048]{2,1,0:T(8,128)(2,1)S(1)} custom-call(s32[2]{0:T(128)S(1)} %pad_add_fusion.1.place_ref, s32[66,256]{1,0:T(8,128)S(1)} %copy-done.10, bf16[8,32,3456]{2,1,0:T(8,128)(2,1)} %all-to-all-done.2.got_ref), custom_call_target="tpu_custom_call" | custom-call | tf_op jit(solution)/shard_map/attend/pallas_call | solution.py:134
  101.4 0.0 copy-start.3
  101.4 18.9 %all_to_all.31 = bf16[8,32,2048]{2,1,0:T(8,128)(2,1)S(1)} all-to-all(bf16[8,32,2048]{2,1,0:T(8,128)(2,1)S(1)} %attend.4), channel_id=1, replica_groups=mesh['pipe'=64,'tp'=8] {'tp'}, dimensions={0} | all-to-all | bytes 2097152 | tf_op jit(solution)/shard_map/all_to_all | solution.py:142
  120.3 0.7 project_out.4
  121.1 4.3 %collective-permute-start.1 = (bf16[256,512]{1,0:T(8,128)(2,1)S(1)}, bf16[256,512]{1,0:T(8,128)(2,1)S(1)}, u32[]{:S(2)}, u32[]{:S(2)}) collective-permute-start(bf16[256,512]{1,0:T(8,128)(2,1)S(1)} %project_out.4), channel_id=1, source_target_pairs={{0,8},{8,16},{16,24},{24,32},{32,40},{40,48},{48,56},{56,64},{64,7... | collective-permute-start | bytes 786440 | tf_op jit(solution)/shard_map/ppermute | solution.py:164
  126.0 2.6 %collective-permute-done.1 = bf16[256,512]{1,0:T(8,128)(2,1)S(1)} collective-permute-done((bf16[256,512]{1,0:T(8,128)(2,1)S(1)}, bf16[256,512]{1,0:T(8,128)(2,1)S(1)}, u32[]{:S(2)}, u32[]{:S(2)}) %collective-permute-start.1) | collective-permute-done | bytes 262176 | tf_op jit(solution)/shard_map/ppermute | solution.py:164
  128.7 0.8 select_select_fusion
  129.4 0.8 project.5
  130.2 1.2 copy-done.6
  131.5 6.2 %all-to-all-start.4 = ((bf16[8,32,3456]{2,1,0:T(8,128)(2,1)}), bf16[8,32,3456]{2,1,0:T(8,128)(2,1)S(1)}, u32[]{:S(2)}, u32[]{:S(2)}) async-start(bf16[8,32,3456]{2,1,0:T(8,128)(2,1)} %copy-done.6), calls=%async_computation.4 | async-start | bytes 3538944 | tf_op jit(solution)/shard_map/all_to_all | solution.py:133
  137.7 0.1 pad_add_fusion.2.place_ref
  137.8 22.3 %all-to-all-done.4.got_ref = bf16[8,32,3456]{2,1,0:T(8,128)(2,1)S(1)} async-done(((bf16[8,32,3456]{2,1,0:T(8,128)(2,1)}), bf16[8,32,3456]{2,1,0:T(8,128)(2,1)S(1)}, u32[]{:S(2)}, u32[]{:S(2)}) %all-to-all-start.4) | async-done | bytes 1769504 | tf_op jit(solution)/shard_map/all_to_all | solution.py:133
  160.1 1.4 attend.5
  161.5 1.0 copy-done.7
  162.5 5.6 %all-to-all-start.5 = ((bf16[8,32,2048]{2,1,0:T(8,128)(2,1)}), bf16[8,32,2048]{2,1,0:T(8,128)(2,1)S(1)}, u32[]{:S(2)}, u32[]{:S(2)}) async-start(bf16[8,32,2048]{2,1,0:T(8,128)(2,1)} %copy-done.7), calls=%async_computation.5 | async-start | bytes 2097152 | tf_op jit(solution)/shard_map/all_to_all | solution.py:142
  168.1 1.3 collective-permute-start.2
  169.4 28.4 %collective-permute-done.2 = bf16[256,512]{1,0:T(8,128)(2,1)S(1)} collective-permute-done((bf16[256,512]{1,0:T(8,128)(2,1)}, bf16[256,512]{1,0:T(8,128)(2,1)S(1)}, u32[]{:S(2)}, u32[]{:S(2)}) %collective-permute-start.2) | collective-permute-done | bytes 262176 | tf_op jit(solution)/shard_map/ppermute | solution.py:170
  197.8 0.7 copy-done.15
  198.5 0.0 all-to-all-done.5
  198.5 1.4 project_out.5
  199.9 0.7 copy.11
  (17 shorter events, 0.0 us)
Async XLA Ops:
  0.6 1.7 copy-start
  2.3 0.9 copy-start.8
  3.2 0.7 copy-start.11
  6.0 29.4 %copy-start.10 = (s32[66,256]{1,0:T(8,128)S(1)}, s32[66,256]{1,0:T(8,128)}, u32[]{:S(2)}) copy-start(s32[66,256]{1,0:T(8,128)} %segments_ref.5) | copy-start | bytes 202756
  6.0 29.4 %all-to-all-start = ((bf16[8,32,3456]{2,1,0:T(8,128)(2,1)}), bf16[8,32,3456]{2,1,0:T(8,128)(2,1)S(1)}, u32[]{:S(2)}, u32[]{:S(2)}) async-start(bf16[8,32,3456]{2,1,0:T(8,128)(2,1)} %project.3), calls=%async_computation | async-start | bytes 3538944 | tf_op jit(solution)/shard_map/all_to_all | solution.py:133
  35.3 20.5 %copy-start.9 = (bf16[1,256,512]{2,1,0:T(8,128)(2,1)S(1)}, bf16[1,256,512]{2,1,0:T(8,128)(2,1)}, u32[]{:S(2)}) copy-start(bf16[1,256,512]{2,1,0:T(8,128)(2,1)} %param.7) | copy-start | bytes 786436
  36.8 19.0 %copy-start.2 = (bf16[1,2048,512]{2,1,0:T(8,128)(2,1)S(1)}, bf16[1,2048,512]{2,1,0:T(8,128)(2,1)}, u32[]{:S(2)}) copy-start(bf16[1,2048,512]{2,1,0:T(8,128)(2,1)} %param.11) | copy-start | bytes 6291460
  55.8 10.7 %copy-start.13 = (bf16[2,256,512]{2,1,0:T(8,128)(2,1)S(1)}, bf16[2,256,512]{2,1,0:T(8,128)(2,1)}, u32[]{:S(2)}) copy-start(bf16[2,256,512]{2,1,0:T(8,128)(2,1)} %param.8) | copy-start | bytes 1572868
  55.8 11.7 %copy-start.1 = (bf16[1,512,2304]{2,1,0:T(8,128)(2,1)S(1)}, bf16[1,512,2304]{2,1,0:T(8,128)(2,1)}, u32[]{:S(2)}) copy-start(bf16[1,512,2304]{2,1,0:T(8,128)(2,1)} %param.10) | copy-start | bytes 7077892
  55.8 11.7 %copy-start.12 = (bf16[1,512]{1,0:T(2,128)(2,1)S(1)}, bf16[1,512]{1,0:T(2,128)(2,1)}, u32[]{:S(2)}) copy-start(bf16[1,512]{1,0:T(2,128)(2,1)} %gain_ref.5) | copy-start | bytes 3076
  56.5 10.0 %collective-permute-start = (bf16[256,512]{1,0:T(8,128)(2,1)S(1)}, bf16[256,512]{1,0:T(8,128)(2,1)}, u32[]{:S(2)}, u32[]{:S(2)}) collective-permute-start(bf16[256,512]{1,0:T(8,128)(2,1)S(1)} %project_out.3), channel_id=1, source_target_pairs={{0,8},{8,16},{16,24},{24,32},{32,40},{40,48},{48,56},{56,64},{64,7... | collective-permute-start | bytes 786440 | tf_op jit(solution)/shard_map/ppermute | solution.py:164
  68.3 1.2 copy-start.5
  69.5 29.6 %all-to-all-start.2 = ((bf16[8,32,3456]{2,1,0:T(8,128)(2,1)}), bf16[8,32,3456]{2,1,0:T(8,128)(2,1)}, u32[]{:S(2)}, u32[]{:S(2)}) async-start(bf16[8,32,3456]{2,1,0:T(8,128)(2,1)} %copy-done.5), calls=%async_computation.2 | async-start | bytes 3538944 | tf_op jit(solution)/shard_map/all_to_all | solution.py:133
  101.4 18.9 %copy-start.3 = (bf16[1,2048,512]{2,1,0:T(8,128)(2,1)S(1)}, bf16[1,2048,512]{2,1,0:T(8,128)(2,1)}, u32[]{:S(2)}) copy-start(bf16[1,2048,512]{2,1,0:T(8,128)(2,1)} %param.11) | copy-start | bytes 6291460
  120.3 8.3 %copy-start.14 = (bf16[2,256,512]{2,1,0:T(8,128)(2,1)S(1)}, bf16[2,256,512]{2,1,0:T(8,128)(2,1)}, u32[]{:S(2)}) copy-start(bf16[2,256,512]{2,1,0:T(8,128)(2,1)} %param.8) | copy-start | bytes 1572868
  121.1 7.6 %collective-permute-start.1 = (bf16[256,512]{1,0:T(8,128)(2,1)S(1)}, bf16[256,512]{1,0:T(8,128)(2,1)S(1)}, u32[]{:S(2)}, u32[]{:S(2)}) collective-permute-start(bf16[256,512]{1,0:T(8,128)(2,1)S(1)} %project_out.4), channel_id=1, source_target_pairs={{0,8},{8,16},{16,24},{24,32},{32,40},{40,48},{48,56},{56,64},{64,7... | collective-permute-start | bytes 786440 | tf_op jit(solution)/shard_map/ppermute | solution.py:164
  130.2 1.2 copy-start.6
  131.5 28.6 %all-to-all-start.4 = ((bf16[8,32,3456]{2,1,0:T(8,128)(2,1)}), bf16[8,32,3456]{2,1,0:T(8,128)(2,1)S(1)}, u32[]{:S(2)}, u32[]{:S(2)}) async-start(bf16[8,32,3456]{2,1,0:T(8,128)(2,1)} %copy-done.6), calls=%async_computation.4 | async-start | bytes 3538944 | tf_op jit(solution)/shard_map/all_to_all | solution.py:133
  161.5 1.0 copy-start.7
  162.5 36.0 %copy-start.4 = (bf16[1,2048,512]{2,1,0:T(8,128)(2,1)S(1)}, bf16[1,2048,512]{2,1,0:T(8,128)(2,1)}, u32[]{:S(2)}) copy-start(bf16[1,2048,512]{2,1,0:T(8,128)(2,1)} %param.11) | copy-start | bytes 6291460
  162.5 36.0 %all-to-all-start.5 = ((bf16[8,32,2048]{2,1,0:T(8,128)(2,1)}), bf16[8,32,2048]{2,1,0:T(8,128)(2,1)S(1)}, u32[]{:S(2)}, u32[]{:S(2)}) async-start(bf16[8,32,2048]{2,1,0:T(8,128)(2,1)} %copy-done.7), calls=%async_computation.5 | async-start | bytes 2097152 | tf_op jit(solution)/shard_map/all_to_all | solution.py:142
  168.1 29.7 %collective-permute-start.2 = (bf16[256,512]{1,0:T(8,128)(2,1)}, bf16[256,512]{1,0:T(8,128)(2,1)S(1)}, u32[]{:S(2)}, u32[]{:S(2)}) collective-permute-start(bf16[256,512]{1,0:T(8,128)(2,1)} %get-tuple-element.2), channel_id=1, source_target_pairs={{0,504},{8,496},{16,488},{24,480},{32,472},{40,464},{48,456},{56,4... | collective-permute-start | bytes 786440 | tf_op jit(solution)/shard_map/ppermute | solution.py:170
  197.8 0.7 copy-start.15
  198.5 1.4 copy-start.16

commit v2 on v1

--- a/solution.py
+++ b/solution.py
@@ -21,12 +21,9 @@
     return (LONGEST_SEGMENT + rows - 2) // rows + 1
 
 
-def project_kernel(parts, x_ref, gain_ref, weight_ref, out_ref):
-    tokens = x_ref.shape[0]
-    rows = tokens // parts
+def project_rows(parts, wide, scaled, weight_ref, out_ref):
+    rows = wide.shape[0] // parts
     blocks = window_blocks(rows)
-    wide = x_ref[...].astype(F32)
-    scaled = (wide * gain_ref[...].astype(F32)).astype(BF16)
     squares = jnp.sum(wide * wide, axis=1, keepdims=True)
     high = squares.astype(BF16).astype(F32)
     low = squares - high
@@ -48,7 +45,29 @@
         out_ref[j, :, last:] = sums.astype(BF16)
 
 
-def attend_kernel(parts, width, place_ref, segments_ref, got_ref, out_ref):
+def project_kernel(parts, tick, stash, flags_ref, *refs):
+    earlier, refs = (refs[:tick], refs[tick:]) if stash else ((), refs)
+    if tick > 0:
+        arrived_ref, fresh_ref, gain_ref, weight_ref, out_ref, current_ref = refs[:6]
+        current = jnp.where(flags_ref[0] == 1, fresh_ref[tick - 1], arrived_ref[...])
+        current_ref[...] = current
+    else:
+        arrived_ref, gain_ref, weight_ref, out_ref = refs
+        current = arrived_ref[...]
+    if earlier:
+        chosen = current
+        for at, earlier_ref in enumerate(earlier):
+            chosen = jnp.where(flags_ref[1] == at, earlier_ref[...], chosen)
+        half = chosen.shape[0] // 2
+        refs[6][...] = chosen[:half]
+        refs[7][...] = chosen[half:]
+    wide = current.astype(F32)
+    scaled = (wide * gain_ref[...].astype(F32)).astype(BF16)
+    project_rows(parts, wide, scaled, weight_ref, out_ref)
+
+
+def attend_kernel(parts, width, place_ref, segments_ref, got_ref, *refs):
+    out_ref = refs[-1]
     rows = got_ref.shape[1]
     tokens = rows * parts
     blocks = window_blocks(rows)
@@ -114,60 +133,91 @@
 
 VMEM = pl.BlockSpec(memory_space=pltpu.VMEM)
 SMEM = pl.BlockSpec(memory_space=pltpu.SMEM)
+ANY = pl.BlockSpec(memory_space=pl.ANY)
 PARAMS = pltpu.CompilerParams(vmem_limit_bytes=24 * 1024 * 1024)
 
 
-def section_layer(current, gain, qkv_weight, out_weight, segments, place):
-    parts = lax.axis_size("tp")
-    tokens, width = current.shape
-    rows = tokens // parts
-    columns = Q_COLS + window_blocks(rows) * KV_COLS + 128
-    partial_proj = pl.pallas_call(
-        functools.partial(project_kernel, parts),
-        out_shape=jax.ShapeDtypeStruct((parts, rows, columns), BF16),
-        in_specs=[VMEM] * 3,
-        out_specs=VMEM,
-        compiler_params=PARAMS,
-        name="project",
-    )(current, gain, qkv_weight)
-    got = lax.all_to_all(partial_proj, "tp", split_axis=0, concat_axis=0, tiled=True)
-    mixed = pl.pallas_call(
-        functools.partial(attend_kernel, parts, width * parts),
-        out_shape=jax.ShapeDtypeStruct((parts, rows, Q_COLS), BF16),
-        in_specs=[SMEM, VMEM, VMEM],
+def shard(shape):
+    return jax.ShapeDtypeStruct(shape, BF16)
+
+
+def exchange(value):
+    return lax.all_to_all(value, "tp", split_axis=0, concat_axis=0, tiled=True)
+
+
+def attend(place, segments, got, width, waited=()):
+    parts, rows, _ = got.shape
+    return pl.pallas_call(
+        functools.partial(attend_kernel, parts, width),
+        out_shape=shard((parts, rows, Q_COLS)),
+        in_specs=[SMEM, VMEM, VMEM] + [ANY] * len(waited),
         out_specs=VMEM,
         compiler_params=PARAMS,
         name="attend",
-    )(place, segments, got)
-    mixed = lax.all_to_all(mixed, "tp", split_axis=0, concat_axis=0, tiled=True)
+    )(place, segments, got, *waited)
+
+
+def project_out(current, mixed, out_weight):
     return pl.pallas_call(
         output_kernel,
-        out_shape=jax.ShapeDtypeStruct((tokens, width), BF16),
+        out_shape=shard(current.shape),
         in_specs=[VMEM] * 3,
         out_specs=VMEM,
         compiler_params=PARAMS,
         name="project_out",
-    )(current, mixed.reshape(tokens, Q_COLS), out_weight)
+    )(current, mixed.reshape(current.shape[0], Q_COLS), out_weight)
 
 
 def shards(carried, fresh, gains, qkv_weight, out_weight, segments, evict_tick):
     section = lax.axis_index("pipe")
     rank = lax.axis_index("tp")
     sections = lax.axis_size("pipe")
+    parts = lax.axis_size("tp")
     ticks = fresh.shape[0] + 1
-    current = carried[0]
-    chosen = current
-    result = current
+    tokens, width = carried.shape[1:]
+    rows = tokens // parts
+    columns = Q_COLS + window_blocks(rows) * KV_COLS + 128
+    flags = jnp.stack([(section == 0).astype(jnp.int32), evict_tick[0]])
+    following = [(i, i + 1) for i in range(sections - 1)]
+    half = sections // 2
+    across = [(i, i + half) for i in range(half)]
+    turned = [(i, half - 1 - i) for i in range(half)]
+    turned_across = [(half + i, sections - 1 - i) for i in range(half)]
+    inputs = [carried[0]]
     for tick in range(ticks):
+        outs = [shard((parts, rows, columns))]
+        operands = [flags, inputs[0], gains, qkv_weight[0]]
+        specs = [SMEM, VMEM, VMEM, VMEM]
         if tick > 0:
-            pairs = [(i, i + 1) for i in range(sections - 1)]
-            arrived = lax.ppermute(result, "pipe", pairs)
-            current = jnp.where(section == 0, fresh[tick - 1], arrived)
-            chosen = jnp.where(evict_tick[0] == tick, current, chosen)
+            arrived = lax.ppermute(result, "pipe", following)
+            operands = [flags, arrived, fresh, gains, qkv_weight[0]]
+            specs = [SMEM, VMEM, VMEM, VMEM, VMEM]
+            outs.append(shard((tokens, width)))
+        if tick == ticks - 1:
+            operands[1:1] = inputs
+            specs[1:1] = [VMEM] * tick
+            outs += [shard((tokens // 2, width))] * 2
+        got = pl.pallas_call(
+            functools.partial(project_kernel, parts, tick, tick == ticks - 1),
+            out_shape=outs,
+            in_specs=specs,
+            out_specs=[VMEM] * len(outs),
+            compiler_params=PARAMS,
+            name="project",
+        )(*operands)
+        partial_proj = got[0]
+        if tick > 0:
+            inputs.append(got[1])
+        sums = exchange(partial_proj)
         place = jnp.stack([rank, section - tick + ticks - 1]).astype(jnp.int32)
-        result = section_layer(current, gains, qkv_weight[0], out_weight[0], segments, place)
-    pairs = [(i, sections - 1 - i) for i in range(sections // 2)]
-    evicted = lax.ppermute(chosen, "pipe", pairs)
+        waited = ()
+        if tick == ticks - 1:
+            waited = (lax.ppermute(got[2], "pipe", across), lax.ppermute(got[3], "pipe", turned))
+        mixed = exchange(attend(place, segments, sums, width * parts, waited))
+        result = project_out(inputs[tick], mixed, out_weight[0])
+    top = lax.ppermute(waited[0], "pipe", turned_across)
+    low = lax.ppermute(waited[1], "pipe", across)
+    evicted = jnp.concatenate([top, low], axis=0)
     return (result[None], evicted[None])
 
 

time: 201 us -> 194 us (0.965)
  the two profiles are of different devices: /device:TPU:231 before, /device:TPU:71 now
where the time goes in v2:
time: 194 us; the launch traced here: 193 us
  waiting for transfers between devices  78.5 us (40%)
  starting transfers between devices  51.2 us (26%)
  blocking collectives  38 us (20%)
  Pallas kernels  13.3 us (7%)
  local copies, waits for them, and re-layouts  9.39 us (5%)
    all_to_all x4, waiting for transfers between devices, exchange(): return lax.all_to_all(value, 'tp', split_axis=0, concat_axis=0, tiled=True)  44.7 us
    all_to_all x2, blocking collectives, exchange(): return lax.all_to_all(value, 'tp', split_axis=0, concat_axis=0, tiled=True)  38 us
    all_to_all x4, starting transfers between devices, exchange(): return lax.all_to_all(value, 'tp', split_axis=0, concat_axis=0, tiled=True)  27.1 us
    ppermute x1, waiting for transfers between devices, shards(): lax.ppermute(got[2], 'pipe', across)  21.5 us
    ppermute x2, starting transfers between devices, shards(): arrived = lax.ppermute(result, 'pipe', following)  12 us
    unnamed x42, local copies, waits for them, and re-layouts  9.39 us
    ppermute x1, starting transfers between devices, shards(): top = lax.ppermute(waited[0], 'pipe', turned_across)  8.88 us
    ppermute x2, waiting for transfers between devices, shards(): arrived = lax.ppermute(result, 'pipe', following)  6.59 us
  transfers between devices with their start and end apart: 10, of which 6 were waited for; matrix products, arithmetic and copies ran while one was open for 0% of the time, Pallas kernels for 0%

profile of v2, /device:TPU:71, one launch (start us, length us, event | category | flops | bytes accessed | tf_op | source)
XLA Modules:
  0.0 192.9 jit_solution(11552082262783462718)
XLA Ops:
  1.3 0.1 pad_add_fusion.flags_ref
  1.4 1.7 copy-done
  3.0 0.9 copy-done.6
  4.0 0.7 copy-done.15
  4.7 2.6 %project.3 = bf16[8,32,3456]{2,1,0:T(8,128)(2,1)} custom-call(s32[2]{0:T(128)S(1)} %pad_add_fusion.flags_ref, bf16[256,512]{1,0:T(8,128)(2,1)S(1)} %bitcast.23, bf16[1,512]{1,0:T(2,128)(2,1)S(1)} %copy-done.15, bf16[512,2304]{1,0:T(8,128)(2,1)S(1)} %bitcast.14), custom_call_target="tpu_custom_call" | custom-call | tf_op jit(solution)/shard_map/project/pallas_call | solution.py:200
  7.2 7.0 %all-to-all-start = ((bf16[8,32,3456]{2,1,0:T(8,128)(2,1)}), bf16[8,32,3456]{2,1,0:T(8,128)(2,1)S(1)}, u32[]{:S(2)}, u32[]{:S(2)}) async-start(bf16[8,32,3456]{2,1,0:T(8,128)(2,1)} %project.3), calls=%async_computation | async-start | bytes 3538944 | tf_op jit(solution)/shard_map/all_to_all | solution.py:145
  14.2 0.1 pad_add_fusion.1.place_ref
  14.3 22.3 %all-to-all-done.got_ref = bf16[8,32,3456]{2,1,0:T(8,128)(2,1)S(1)} async-done(((bf16[8,32,3456]{2,1,0:T(8,128)(2,1)}), bf16[8,32,3456]{2,1,0:T(8,128)(2,1)S(1)}, u32[]{:S(2)}, u32[]{:S(2)}) %all-to-all-start) | async-done | bytes 1769504 | tf_op jit(solution)/shard_map/all_to_all | solution.py:145
  36.6 1.4 attend.3
  38.0 0.0 copy-start.2
  38.0 19.0 %all_to_all.30 = bf16[8,32,2048]{2,1,0:T(8,128)(2,1)S(1)} all-to-all(bf16[8,32,2048]{2,1,0:T(8,128)(2,1)S(1)} %attend.3), channel_id=1, replica_groups=mesh['pipe'=64,'tp'=8] {'tp'}, dimensions={0} | all-to-all | bytes 2097152 | tf_op jit(solution)/shard_map/all_to_all | solution.py:145
  57.1 0.0 copy-start.16
  57.1 0.7 project_out.3
  57.8 5.4 %collective-permute-start = (bf16[256,512]{1,0:T(8,128)(2,1)S(1)}, bf16[256,512]{1,0:T(8,128)(2,1)S(1)}, u32[]{:S(2)}, u32[]{:S(2)}) collective-permute-start(bf16[256,512]{1,0:T(8,128)(2,1)S(1)} %project_out.3), channel_id=1, source_target_pairs={{0,8},{8,16},{16,24},{24,32},{32,40},{40,48},{48,56},{56,64},{64,7... | collective-permute-start | bytes 786440 | tf_op jit(solution)/shard_map/ppermute | solution.py:192
  63.2 3.3 %collective-permute-done.refs_0_ = bf16[256,512]{1,0:T(8,128)(2,1)S(1)} collective-permute-done((bf16[256,512]{1,0:T(8,128)(2,1)S(1)}, bf16[256,512]{1,0:T(8,128)(2,1)S(1)}, u32[]{:S(2)}, u32[]{:S(2)}) %collective-permute-start) | collective-permute-done | bytes 262176 | tf_op jit(solution)/shard_map/ppermute | solution.py:192
  66.5 1.3 project.4
  67.9 1.2 copy-done.10
  69.1 6.9 %all-to-all-start.2 = ((bf16[8,32,3456]{2,1,0:T(8,128)(2,1)}), bf16[8,32,3456]{2,1,0:T(8,128)(2,1)}, u32[]{:S(2)}, u32[]{:S(2)}) async-start(bf16[8,32,3456]{2,1,0:T(8,128)(2,1)} %copy-done.10), calls=%async_computation.2 | async-start | bytes 3538944 | tf_op jit(solution)/shard_map/all_to_all | solution.py:145
  76.0 0.1 pad_add_fusion.2.place_ref
  76.1 22.4 %all-to-all-done.2.got_ref = bf16[8,32,3456]{2,1,0:T(8,128)(2,1)} async-done(((bf16[8,32,3456]{2,1,0:T(8,128)(2,1)}), bf16[8,32,3456]{2,1,0:T(8,128)(2,1)}, u32[]{:S(2)}, u32[]{:S(2)}) %all-to-all-start.2) | async-done | bytes 1769504 | tf_op jit(solution)/shard_map/all_to_all | solution.py:145
  98.5 2.4 %attend.4 = bf16[8,32,2048]{2,1,0:T(8,128)(2,1)S(1)} custom-call(s32[2]{0:T(128)S(1)} %pad_add_fusion.2.place_ref, s32[66,256]{1,0:T(8,128)S(1)} %copy-done.11, bf16[8,32,3456]{2,1,0:T(8,128)(2,1)} %all-to-all-done.2.got_ref), custom_call_target="tpu_custom_call" | custom-call | tf_op jit(solution)/shard_map/attend/pallas_call | solution.py:150
  100.9 0.0 copy-start.3
  100.9 19.0 %all_to_all.31 = bf16[8,32,2048]{2,1,0:T(8,128)(2,1)S(1)} all-to-all(bf16[8,32,2048]{2,1,0:T(8,128)(2,1)S(1)} %attend.4), channel_id=1, replica_groups=mesh['pipe'=64,'tp'=8] {'tp'}, dimensions={0} | all-to-all | bytes 2097152 | tf_op jit(solution)/shard_map/all_to_all | solution.py:145
  119.9 0.7 project_out.4
  120.6 6.6 %collective-permute-start.1 = (bf16[256,512]{1,0:T(8,128)(2,1)S(1)}, bf16[256,512]{1,0:T(8,128)(2,1)S(1)}, u32[]{:S(2)}, u32[]{:S(2)}) collective-permute-start(bf16[256,512]{1,0:T(8,128)(2,1)S(1)} %project_out.4), channel_id=1, source_target_pairs={{0,8},{8,16},{16,24},{24,32},{32,40},{40,48},{48,56},{56,64},{64,7... | collective-permute-start | bytes 786440 | tf_op jit(solution)/shard_map/ppermute | solution.py:192
  127.2 3.3 %collective-permute-done.1.refs_2_ = bf16[256,512]{1,0:T(8,128)(2,1)S(1)} collective-permute-done((bf16[256,512]{1,0:T(8,128)(2,1)S(1)}, bf16[256,512]{1,0:T(8,128)(2,1)S(1)}, u32[]{:S(2)}, u32[]{:S(2)}) %collective-permute-start.1) | collective-permute-done | bytes 262176 | tf_op jit(solution)/shard_map/ppermute | solution.py:192
  130.5 1.4 project.5
  131.8 1.2 copy-done.9
  133.1 0.7 copy-done.12
  133.8 0.6 copy-done.17
  134.4 0.7 copy-done.19
  135.1 6.3 %all-to-all-start.4 = ((bf16[8,32,3456]{2,1,0:T(8,128)(2,1)}), bf16[8,32,3456]{2,1,0:T(8,128)(2,1)S(1)}, u32[]{:S(2)}, u32[]{:S(2)}) async-start(bf16[8,32,3456]{2,1,0:T(8,128)(2,1)} %copy-done.9), calls=%async_computation.4 | async-start | bytes 3538944 | tf_op jit(solution)/shard_map/all_to_all | solution.py:145
  141.4 1.3 collective-permute-start.2
  142.7 0.7 collective-permute-start.3
  143.3 0.1 pad_add_fusion.3.place_ref
  143.4 21.5 %collective-permute-done.2.refs_0_ = bf16[128,512]{1,0:T(8,128)(2,1)S(1)} collective-permute-done((bf16[128,512]{1,0:T(8,128)(2,1)S(1)}, bf16[128,512]{1,0:T(8,128)(2,1)S(1)}, u32[]{:S(2)}, u32[]{:S(2)}) %collective-permute-start.2) | collective-permute-done | bytes 131104 | tf_op jit(solution)/shard_map/ppermute | solution.py:215
  164.9 0.0 collective-permute-done.3.refs_1_
  164.9 0.0 all-to-all-done.4.got_ref
  164.9 1.4 attend.5
  166.4 1.0 copy-done.5
  167.3 0.7 copy-done.14
  168.0 6.8 %all-to-all-start.5 = ((bf16[8,32,2048]{2,1,0:T(8,128)(2,1)}), bf16[8,32,2048]{2,1,0:T(8,128)(2,1)S(1)}, u32[]{:S(2)}, u32[]{:S(2)}) async-start(bf16[8,32,2048]{2,1,0:T(8,128)(2,1)} %copy-done.5), calls=%async_computation.5 | async-start | bytes 2097152 | tf_op jit(solution)/shard_map/all_to_all | solution.py:145
  174.8 8.9 %collective-permute-start.4 = (bf16[128,512]{1,0:T(8,128)(2,1)S(1)}, bf16[128,512]{1,0:T(8,128)(2,1)S(1)}, u32[]{:S(2)}, u32[]{:S(2)}) collective-permute-start(bf16[128,512]{1,0:T(8,128)(2,1)S(1)} %collective-permute-done.2.refs_0_), channel_id=1, source_target_pairs={{256,504},{264,496},{272,488},{280,480},{288,472},{296,464},{304,4... | collective-permute-start | bytes 393224 | tf_op jit(solution)/shard_map/ppermute | solution.py:218
  183.7 1.3 collective-permute-start.5
  185.0 5.7 %collective-permute-done.4 = bf16[128,512]{1,0:T(8,128)(2,1)S(1)} collective-permute-done((bf16[128,512]{1,0:T(8,128)(2,1)S(1)}, bf16[128,512]{1,0:T(8,128)(2,1)S(1)}, u32[]{:S(2)}, u32[]{:S(2)}) %collective-permute-start.4) | collective-permute-done | bytes 131104 | tf_op jit(solution)/shard_map/ppermute | solution.py:218
  190.8 0.0 collective-permute-done.5
  190.8 0.7 maximum_bitcast_fusion
  191.5 1.4 project_out.5
  (30 shorter events, 0.1 us)
Async XLA Ops:
  1.4 1.7 copy-start
  3.0 0.9 copy-start.6
  4.0 0.7 copy-start.15
  7.2 29.4 %copy-start.11 = (s32[66,256]{1,0:T(8,128)S(1)}, s32[66,256]{1,0:T(8,128)}, u32[]{:S(2)}) copy-start(s32[66,256]{1,0:T(8,128)} %segments_ref.5) | copy-start | bytes 202756
  7.2 29.4 %all-to-all-start = ((bf16[8,32,3456]{2,1,0:T(8,128)(2,1)}), bf16[8,32,3456]{2,1,0:T(8,128)(2,1)S(1)}, u32[]{:S(2)}, u32[]{:S(2)}) async-start(bf16[8,32,3456]{2,1,0:T(8,128)(2,1)} %project.3), calls=%async_computation | async-start | bytes 3538944 | tf_op jit(solution)/shard_map/all_to_all | solution.py:145
  36.6 20.5 %copy-start.7 = (bf16[1,256,512]{2,1,0:T(8,128)(2,1)S(1)}, bf16[1,256,512]{2,1,0:T(8,128)(2,1)}, u32[]{:S(2)}) copy-start(bf16[1,256,512]{2,1,0:T(8,128)(2,1)} %param.7) | copy-start | bytes 786436
  38.0 19.0 %copy-start.2 = (bf16[1,2048,512]{2,1,0:T(8,128)(2,1)S(1)}, bf16[1,2048,512]{2,1,0:T(8,128)(2,1)}, u32[]{:S(2)}) copy-start(bf16[1,2048,512]{2,1,0:T(8,128)(2,1)} %param.11) | copy-start | bytes 6291460
  57.0 9.5 %copy-start.1 = (bf16[1,512,2304]{2,1,0:T(8,128)(2,1)S(1)}, bf16[1,512,2304]{2,1,0:T(8,128)(2,1)}, u32[]{:S(2)}) copy-start(bf16[1,512,2304]{2,1,0:T(8,128)(2,1)} %param.10) | copy-start | bytes 7077892
  57.0 9.5 %copy-start.8 = (bf16[2,256,512]{2,1,0:T(8,128)(2,1)S(1)}, bf16[2,256,512]{2,1,0:T(8,128)(2,1)}, u32[]{:S(2)}) copy-start(bf16[2,256,512]{2,1,0:T(8,128)(2,1)} %refs_3_.1) | copy-start | bytes 1572868
  57.1 9.5 %copy-start.16 = (bf16[1,512]{1,0:T(2,128)(2,1)S(1)}, bf16[1,512]{1,0:T(2,128)(2,1)}, u32[]{:S(2)}) copy-start(bf16[1,512]{1,0:T(2,128)(2,1)} %refs_4_.1) | copy-start | bytes 3076
  57.8 8.7 %collective-permute-start = (bf16[256,512]{1,0:T(8,128)(2,1)S(1)}, bf16[256,512]{1,0:T(8,128)(2,1)S(1)}, u32[]{:S(2)}, u32[]{:S(2)}) collective-permute-start(bf16[256,512]{1,0:T(8,128)(2,1)S(1)} %project_out.3), channel_id=1, source_target_pairs={{0,8},{8,16},{16,24},{24,32},{32,40},{40,48},{48,56},{56,64},{64,7... | collective-permute-start | bytes 786440 | tf_op jit(solution)/shard_map/ppermute | solution.py:192
  67.9 1.2 copy-start.10
  69.1 29.4 %all-to-all-start.2 = ((bf16[8,32,3456]{2,1,0:T(8,128)(2,1)}), bf16[8,32,3456]{2,1,0:T(8,128)(2,1)}, u32[]{:S(2)}, u32[]{:S(2)}) async-start(bf16[8,32,3456]{2,1,0:T(8,128)(2,1)} %copy-done.10), calls=%async_computation.2 | async-start | bytes 3538944 | tf_op jit(solution)/shard_map/all_to_all | solution.py:145
  100.9 19.0 %copy-start.3 = (bf16[1,2048,512]{2,1,0:T(8,128)(2,1)S(1)}, bf16[1,2048,512]{2,1,0:T(8,128)(2,1)}, u32[]{:S(2)}) copy-start(bf16[1,2048,512]{2,1,0:T(8,128)(2,1)} %param.11) | copy-start | bytes 6291460
  120.6 9.9 %collective-permute-start.1 = (bf16[256,512]{1,0:T(8,128)(2,1)S(1)}, bf16[256,512]{1,0:T(8,128)(2,1)S(1)}, u32[]{:S(2)}, u32[]{:S(2)}) collective-permute-start(bf16[256,512]{1,0:T(8,128)(2,1)S(1)} %project_out.4), channel_id=1, source_target_pairs={{0,8},{8,16},{16,24},{24,32},{32,40},{40,48},{48,56},{56,64},{64,7... | collective-permute-start | bytes 786440 | tf_op jit(solution)/shard_map/ppermute | solution.py:192
  131.8 1.2 copy-start.9
  133.1 0.7 copy-start.12
  133.8 0.7 copy-start.17
  134.4 0.7 copy-start.19
  135.1 6.3 %copy-start.20 = (bf16[128,512]{1,0:T(8,128)(2,1)S(1)}, bf16[128,512]{1,0:T(8,128)(2,1)}, u32[]{:S(2)}) copy-start(bf16[128,512]{1,0:T(8,128)(2,1)} %copy-done.19) | copy-start | bytes 393220
  135.1 7.6 %copy-start.18 = (bf16[128,512]{1,0:T(8,128)(2,1)S(1)}, bf16[128,512]{1,0:T(8,128)(2,1)}, u32[]{:S(2)}) copy-start(bf16[128,512]{1,0:T(8,128)(2,1)} %copy-done.17) | copy-start | bytes 393220
  135.1 29.8 %all-to-all-start.4 = ((bf16[8,32,3456]{2,1,0:T(8,128)(2,1)}), bf16[8,32,3456]{2,1,0:T(8,128)(2,1)S(1)}, u32[]{:S(2)}, u32[]{:S(2)}) async-start(bf16[8,32,3456]{2,1,0:T(8,128)(2,1)} %copy-done.9), calls=%async_computation.4 | async-start | bytes 3538944 | tf_op jit(solution)/shard_map/all_to_all | solution.py:145
  141.4 23.6 %collective-permute-start.2 = (bf16[128,512]{1,0:T(8,128)(2,1)S(1)}, bf16[128,512]{1,0:T(8,128)(2,1)S(1)}, u32[]{:S(2)}, u32[]{:S(2)}) collective-permute-start(bf16[128,512]{1,0:T(8,128)(2,1)S(1)} %copy-done.20), channel_id=1, source_target_pairs={{0,256},{8,264},{16,272},{24,280},{32,288},{40,296},{48,304},{56,3... | collective-permute-start | bytes 393224 | tf_op jit(solution)/shard_map/ppermute | solution.py:215
  142.7 22.3 %collective-permute-start.3 = (bf16[128,512]{1,0:T(8,128)(2,1)S(1)}, bf16[128,512]{1,0:T(8,128)(2,1)S(1)}, u32[]{:S(2)}, u32[]{:S(2)}) collective-permute-start(bf16[128,512]{1,0:T(8,128)(2,1)S(1)} %copy-done.18), channel_id=1, source_target_pairs={{0,248},{8,240},{16,232},{24,224},{32,216},{40,208},{48,200},{56,1... | collective-permute-start | bytes 393224 | tf_op jit(solution)/shard_map/ppermute | solution.py:215
  166.4 1.0 copy-start.5
  167.3 0.7 copy-start.14
  168.0 23.5 %copy-start.4 = (bf16[1,2048,512]{2,1,0:T(8,128)(2,1)S(1)}, bf16[1,2048,512]{2,1,0:T(8,128)(2,1)}, u32[]{:S(2)}) copy-start(bf16[1,2048,512]{2,1,0:T(8,128)(2,1)} %param.11) | copy-start | bytes 6291460
  168.0 23.5 %copy-start.13 = (bf16[256,512]{1,0:T(8,128)(2,1)S(1)}, bf16[256,512]{1,0:T(8,128)(2,1)}, u32[]{:S(2)}) copy-start(bf16[256,512]{1,0:T(8,128)(2,1)} %copy-done.12) | copy-start | bytes 786436
  168.0 23.5 %all-to-all-start.5 = ((bf16[8,32,2048]{2,1,0:T(8,128)(2,1)}), bf16[8,32,2048]{2,1,0:T(8,128)(2,1)S(1)}, u32[]{:S(2)}, u32[]{:S(2)}) async-start(bf16[8,32,2048]{2,1,0:T(8,128)(2,1)} %copy-done.5), calls=%async_computation.5 | async-start | bytes 2097152 | tf_op jit(solution)/shard_map/all_to_all | solution.py:145
  174.8 15.9 %collective-permute-start.4 = (bf16[128,512]{1,0:T(8,128)(2,1)S(1)}, bf16[128,512]{1,0:T(8,128)(2,1)S(1)}, u32[]{:S(2)}, u32[]{:S(2)}) collective-permute-start(bf16[128,512]{1,0:T(8,128)(2,1)S(1)} %collective-permute-done.2.refs_0_), channel_id=1, source_target_pairs={{256,504},{264,496},{272,488},{280,480},{288,472},{296,464},{304,4... | collective-permute-start | bytes 393224 | tf_op jit(solution)/shard_map/ppermute | solution.py:218
  183.7 7.0 %collective-permute-start.5 = (bf16[128,512]{1,0:T(8,128)(2,1)}, bf16[128,512]{1,0:T(8,128)(2,1)S(1)}, u32[]{:S(2)}, u32[]{:S(2)}) collective-permute-start(bf16[128,512]{1,0:T(8,128)(2,1)} %copy-done.14), channel_id=1, source_target_pairs={{0,256},{8,264},{16,272},{24,280},{32,288},{40,296},{48,304},{56,3... | collective-permute-start | bytes 393224 | tf_op jit(solution)/shard_map/ppermute | solution.py:219

commit v3 on v1

v3 whole, which is shorter than its diff:
```python
import functools

import jax
import jax.numpy as jnp
from jax import lax
from jax.experimental import pallas as pl
from jax.experimental.pallas import tpu as pltpu
from jax.sharding import PartitionSpec as P

HEAD_DIM = 128
Q_HEADS = 16
Q_COLS = Q_HEADS * HEAD_DIM
HALF_COLS = Q_COLS // 2
KV_COLS = 2 * HEAD_DIM
LONGEST_SEGMENT = 128
NORM_EPS = 1e-05
STEP = 256
GAIN_ROWS = 16
F32 = jnp.float32
BF16 = jnp.bfloat16

RANK, HALF, SECTION, LAST, EVICT = range(5)


def window_blocks(rows):
    return (LONGEST_SEGMENT + rows - 2) // rows + 1


def put_sums(high_low, rows):
    lane = lax.broadcasted_iota(jnp.int32, (rows, 128), 1)
    sums = jnp.zeros((rows, 128), F32)
    for b, squares in enumerate(high_low):
        high = squares.astype(BF16).astype(F32)
        sums = jnp.where(lane == 2 * b, high, sums)
        sums = jnp.where(lane == 2 * b + 1, squares - high, sums)
    return sums.astype(BF16)


def put_window(kv, squares, out_ref, start):
    parts, rows, _ = out_ref.shape
    blocks = window_blocks(rows)
    last = start + blocks * KV_COLS
    for j in range(parts):
        spots = [max(j - blocks + 1 + b, 0) * rows for b in range(blocks)]
        for b, at in enumerate(spots):
            out_ref[j, :, start + b * KV_COLS : start + (b + 1) * KV_COLS] = kv[at : at + rows]
        out_ref[j, :, last:] = put_sums([squares[at : at + rows] for at in spots], rows)


def scale_rows(x_ref, gain):
    wide = x_ref[...].astype(F32)
    squares = jnp.sum(wide * wide, axis=1, keepdims=True)
    return (wide * gain.astype(F32)).astype(BF16), squares


def dot(a, b):
    return jnp.dot(a, b, preferred_element_type=F32)


def project_first_kernel(x_ref, gain_ref, weight_ref, out_ref):
    parts, rows, _ = out_ref.shape
    scaled, squares = scale_rows(x_ref, gain_ref[...])
    for start in range(0, Q_COLS, STEP):
        tile = dot(scaled, weight_ref[:, start : start + STEP]).astype(BF16)
        out_ref[:, :, start : start + STEP] = tile.reshape(parts, rows, STEP)
    kv = dot(scaled, weight_ref[:, Q_COLS:]).astype(BF16)
    put_window(kv, squares, out_ref, Q_COLS)


def project_kernel(stash, place_ref, own_ref, other_ref, gain_ref, weight_ref, first_ref, second_ref, *refs):
    if stash:
        earlier, (out_ref, top_ref, low_ref) = refs[:-3], refs[-3:]
        chosen = own_ref[...]
        for at, earlier_ref in enumerate(earlier):
            chosen = jnp.where(place_ref[EVICT] == at, earlier_ref[...], chosen)
        middle = chosen.shape[0] // 2
        top_ref[...] = chosen[:middle]
        low_ref[...] = chosen[middle:]
    else:
        (out_ref,) = refs
    parts, rows, _ = out_ref.shape
    depth = second_ref.shape[0]
    width = own_ref.shape[1]
    own, own_squares = scale_rows(own_ref, gain_ref[...])
    other, other_squares = scale_rows(other_ref, first_ref[depth : depth + 1, :width])
    squares = own_squares + other_squares

    def tile(columns, at):
        total = dot(own, weight_ref[:, columns])
        total = total + dot(other[:, :depth], first_ref[:depth, at : at + STEP])
        return (total + dot(other[:, depth:], second_ref[:, at : at + STEP])).astype(BF16)

    half = place_ref[HALF] * HALF_COLS
    for start in range(0, HALF_COLS, STEP):
        queries = tile(pl.ds(pl.multiple_of(half + start, STEP), STEP), start)
        out_ref[:, :, start : start + STEP] = queries.reshape(parts, rows, STEP)
    kv = tile(slice(Q_COLS, Q_COLS + KV_COLS), HALF_COLS)
    put_window(kv, squares, out_ref, HALF_COLS)


def share_kernel(begin, gain_rows, place_ref, gain_ref, weight_ref, *refs):
    out_ref = refs[-1]
    depth = out_ref.shape[0] - gain_rows
    half = pl.multiple_of((1 - place_ref[HALF]) * HALF_COLS, HALF_COLS)
    out_ref[:depth, :HALF_COLS] = weight_ref[begin : begin + depth, pl.ds(half, HALF_COLS)]
    out_ref[:depth, HALF_COLS:] = weight_ref[begin : begin + depth, Q_COLS:]
    if gain_rows:
        width = gain_ref.shape[1]
        out_ref[depth:, :width] = jnp.broadcast_to(gain_ref[...], (gain_rows, width))
        out_ref[depth:, width:] = jnp.zeros((gain_rows, out_ref.shape[1] - width), BF16)


def fold_kernel(place_ref, got_ref, waited_ref, keep_ref, send_ref):
    parts, rows, _ = got_ref.shape
    blocks = window_blocks(rows)

    def total(columns):
        value = got_ref[0, :, columns].astype(F32)
        for j in range(1, parts):
            value = value + got_ref[j, :, columns].astype(F32)
        return value

    own = place_ref[HALF] * HALF_COLS
    other = HALF_COLS - own
    for start in range(0, HALF_COLS, STEP):
        columns = slice(start, start + STEP)
        keep_ref[0, :, columns] = total(pl.ds(pl.multiple_of(own + start, STEP), STEP)).astype(BF16)
        send_ref[0, :, columns] = total(pl.ds(pl.multiple_of(other + start, STEP), STEP)).astype(BF16)
    span = blocks * KV_COLS
    window = total(slice(Q_COLS, Q_COLS + span)).astype(BF16)
    sums = total(slice(Q_COLS + span, Q_COLS + span + 128))
    sums = put_sums([sums[:, 2 * b : 2 * b + 1] + sums[:, 2 * b + 1 : 2 * b + 2] for b in range(blocks)], rows)
    for ref in (keep_ref, send_ref):
        ref[0, :, HALF_COLS : HALF_COLS + span] = window
        ref[0, :, HALF_COLS + span :] = sums


def attend_kernel(tick, ticks, parts, width, partials, place_ref, segments_ref, *refs):
    out_ref = refs[-1]
    copies, rows, columns = out_ref.shape
    heads = columns // HEAD_DIM
    tokens = rows * parts
    blocks = window_blocks(rows)
    span = blocks * rows
    before = span - rows

    def total(start, size):
        value = None
        for ref in refs[:partials]:
            for j in range(ref.shape[0]):
                piece = ref[j, :, start : start + size].astype(F32)
                value = piece if value is None else value + piece
        return value

    sums = total(columns + blocks * KV_COLS, 128)
    scales = []
    for b in range(blocks):
        squares = sums[:, 2 * b : 2 * b + 1] + sums[:, 2 * b + 1 : 2 * b + 2]
        scales.append(lax.rsqrt(squares / width + NORM_EPS))
    keys, values = [], []
    for b in range(blocks):
        both = (total(columns + b * KV_COLS, KV_COLS) * scales[b]).astype(BF16)
        keys.append(both[:, :HEAD_DIM])
        values.append(both[:, HEAD_DIM:])
    keys = jnp.concatenate(keys, axis=0)
    values = jnp.concatenate(values, axis=0)
    queries = []
    for h in range(heads):
        queries.append((total(h * HEAD_DIM, HEAD_DIM) * scales[-1]).astype(BF16))
    queries = jnp.concatenate(queries, axis=0)

    first = place_ref[RANK] * rows - before
    item = place_ref[SECTION] + (ticks - 1 - tick)
    segment_row = segments_ref[pl.ds(item, 1), :]
    segment_row = pltpu.roll(segment_row, lax.rem(tokens - first, tokens), 1)
    segment_rows = jnp.broadcast_to(segment_row, (rows, tokens))
    column = lax.broadcasted_iota(jnp.int32, (rows, tokens), 1)
    own = lax.broadcasted_iota(jnp.int32, (rows, tokens), 0) + before
    own_segment = jnp.sum(jnp.where(column == own, segment_rows, 0), axis=1, keepdims=True)
    visible = (segment_rows == own_segment) & (column <= own) & (column + first >= 0)
    visible = visible[:, :span]

    scores = lax.dot_general(
        queries, keys, (((1,), (1,)), ((), ())), preferred_element_type=F32
    ) * HEAD_DIM ** (-0.5)
    scores = scores.reshape(heads, rows, span)
    scores = jnp.where(visible[None], scores, F32(-1e30))
    highest = jnp.max(scores, axis=-1, keepdims=True)
    exponentials = jnp.where(visible[None], jnp.exp(scores - highest), F32(0.0))
    totals = jnp.sum(exponentials, axis=-1, keepdims=True)
    attention = (exponentials / totals).astype(BF16).reshape(heads * rows, span)
    mixed = dot(attention, values).astype(BF16)
    for h in range(heads):
        piece = mixed[h * rows : (h + 1) * rows]
        for j in range(copies):
            out_ref[j, :, h * HEAD_DIM : (h + 1) * HEAD_DIM] = piece


def join_kernel(place_ref, own_ref, other_ref, out_ref):
    own = pl.multiple_of(place_ref[HALF] * HALF_COLS, HALF_COLS)
    other = pl.multiple_of((1 - place_ref[HALF]) * HALF_COLS, HALF_COLS)
    for j in range(out_ref.shape[0]):
        out_ref[j, :, pl.ds(own, HALF_COLS)] = own_ref[0]
        out_ref[j, :, pl.ds(other, HALF_COLS)] = other_ref[0]


def output_kernel(tick, place_ref, x_ref, mixed_ref, weight_ref, *refs):
    out_ref = refs[-1]
    tokens = x_ref.shape[0]
    parts, rows, columns = mixed_ref.shape
    group = tokens // rows
    product = None
    for at in range(parts // group):
        mixed = mixed_ref[at * group : (at + 1) * group].reshape(tokens, columns)
        piece = dot(mixed, weight_ref[at * columns : (at + 1) * columns])
        product = piece if product is None else product + piece
    result = (x_ref[...].astype(F32) + product).astype(BF16)
    if tick is not None:
        result = jnp.where(place_ref[LAST] == 1, refs[0][tick], result)
    out_ref[...] = result


VMEM = pl.BlockSpec(memory_space=pltpu.VMEM)
SMEM = pl.BlockSpec(memory_space=pltpu.SMEM)
ANY = pl.BlockSpec(memory_space=pl.ANY)
PARAMS = pltpu.CompilerParams(vmem_limit_bytes=24 * 1024 * 1024)


def call(kernel, name, shapes, operands, waited=()):
    specs = [SMEM if value.ndim == 1 else VMEM for value in operands] + [ANY] * len(waited)
    outs = [jax.ShapeDtypeStruct(shape, BF16) for shape in shapes]
    got = pl.pallas_call(
        kernel,
        out_shape=outs,
        in_specs=specs,
        out_specs=[VMEM] * len(outs),
        compiler_params=PARAMS,
        name=name,
    )(*operands, *waited)
    return got if len(outs) > 1 else got[0]


def shards(carried, fresh, gains, qkv_weight, out_weight, segments, evict_tick):
    section = lax.axis_index("pipe")
    rank = lax.axis_index("tp")
    sections = lax.axis_size("pipe")
    parts = lax.axis_size("tp")
    group = parts // 2
    ticks = fresh.shape[0] + 1
    tokens, width = carried.shape[1:]
    rows = tokens // group
    tail = window_blocks(rows) * KV_COLS + 128
    qkv_weight, out_weight = qkv_weight[0], out_weight[0]
    place = jnp.stack(
        [rank % group, rank // group, section, (section == sections - 1).astype(jnp.int32), evict_tick[0]]
    )
    groups = [list(range(group)), list(range(group, parts))]
    partner = [(i, (i + group) % parts) for i in range(parts)]
    following = [(i, (i + 1) % sections) for i in range(sections)]
    crossing = [(i * parts + a, j * parts + b) for i, j in following for a, b in partner]
    half = sections // 2
    across = [(i, i + half) for i in range(half)]
    turned = [(i, half - 1 - i) for i in range(half)]
    turned_across = [(half + i, sections - 1 - i) for i in range(half)]

    def exchange(value, groups=None):
        return lax.all_to_all(value, "tp", split_axis=0, concat_axis=0, tiled=True, axis_index_groups=groups)

    def attend(tick, copies, sums, waited=()):
        kernel = functools.partial(attend_kernel, tick, ticks, group, width * parts, len(sums))
        shape = (copies, rows, HALF_COLS)
        return call(kernel, "attend", [shape], [place, segments, *sums], waited)

    def share(begin, depth, gain_rows, waited=()):
        kernel = functools.partial(share_kernel, begin, gain_rows)
        shape = (depth + gain_rows, HALF_COLS + KV_COLS)
        piece = call(kernel, "share", [shape], [place, gains, qkv_weight], waited)
        return lax.ppermute(piece, "tp", partner)

    own = carried[0]
    partial_proj = call(
        project_first_kernel, "project_first", [(group, rows, Q_COLS + tail)], [own, gains, qkv_weight]
    )
    first = share(0, width // 2, GAIN_ROWS, [partial_proj])
    sums = exchange(partial_proj, groups)
    keep, send = call(fold_kernel, "fold", [(1, rows, HALF_COLS + tail)] * 2, [place, sums], [first])
    mixed = attend(0, 1, [keep, lax.ppermute(send, "tp", partner)])
    arrived = lax.ppermute(mixed, "tp", partner)
    second = share(width // 2, width // 2, 0, [arrived])
    joined = call(join_kernel, "join", [(group, rows, Q_COLS)], [place, mixed, arrived])
    mixed = exchange(joined, groups)
    waited = (second,)
    inputs = [own]
    for tick in range(ticks):
        if tick > 0:
            other = lax.ppermute(result, ("pipe", "tp"), crossing)
            own = lax.ppermute(result, "pipe", following)
            stash = tick == ticks - 1
            operands = [place, own, other, gains, qkv_weight, first, second]
            shapes = [(group, rows, HALF_COLS + tail)]
            if stash:
                operands += inputs
                shapes += [(tokens // 2, width)] * 2
            got = call(functools.partial(project_kernel, stash), "project", shapes, operands)
            inputs.append(own)
            waited = ()
            if stash:
                got, top, low = got
                waited = (lax.ppermute(top, "pipe", across), lax.ppermute(low, "pipe", turned))
            sums = exchange(got, groups)
            mixed = exchange(attend(tick, parts, [sums], waited))
            hops, waited = waited, ()
        operands = [place, own, mixed, out_weight]
        kernel = functools.partial(output_kernel, None)
        if tick < ticks - 1:
            kernel = functools.partial(output_kernel, tick)
            operands.append(fresh)
        result = call(kernel, "project_out", [(tokens, width)], operands, waited)
    top = lax.ppermute(hops[0], "pipe", turned_across)
    low = lax.ppermute(hops[1], "pipe", across)
    evicted = jnp.concatenate([top, low], axis=0)
    return (result[None], evicted[None])


def solution(mesh):
    placed = (
        P("pipe", None, "tp"),
        P(None, None, "tp"),
        P("pipe", "tp"),
        P("pipe", "tp", None),
        P("pipe", None, "tp"),
        P(),
        P("pipe"),
    )
    return jax.shard_map(
        shards,
        mesh=mesh,
        in_specs=placed,
        out_specs=(P("pipe", None, "tp"), P("pipe", None, "tp")),
        check_vma=False,
    )
```

time: 201 us -> 211 us (1.050)
  the two profiles are of different devices: /device:TPU:231 before, /device:TPU:6 now
where the time goes in v3:
time: 211 us; the launch traced here: 210 us
  waiting for transfers between devices  85.8 us (41%)
  starting transfers between devices  58.6 us (28%)
  blocking collectives  31.5 us (15%)
  Pallas kernels  17.5 us (8%)
  local copies, waits for them, and re-layouts  14 us (7%)
    all_to_all x2, blocking collectives, exchange(): lax.all_to_all(value, 'tp', split_axis=0, concat_axis=0, tiled=True, axis...  31.5 us
    ppermute x2, waiting for transfers between devices, share(): return lax.ppermute(piece, 'tp', partner)  30.8 us
    all_to_all x4, starting transfers between devices, exchange(): lax.all_to_all(value, 'tp', split_axis=0, concat_axis=0, tiled=True, axis...  18.2 us
    pallas_call x13, Pallas kernels, call(): pl.pallas_call(kernel, out_shape=outs, in_specs=specs, out_specs=[VMEM] *...  17.5 us
    ppermute x1, waiting for transfers between devices, shards(): low = lax.ppermute(hops[1], 'pipe', across)  16.8 us
    unnamed x46, local copies, waits for them, and re-layouts  13.9 us
    ppermute x2, starting transfers between devices, shards(): own = lax.ppermute(result, 'pipe', following)  13.4 us
    all_to_all x4, waiting for transfers between devices, exchange(): lax.all_to_all(value, 'tp', split_axis=0, concat_axis=0, tiled=True, axis...  7.29 us
  transfers between devices with their start and end apart: 16, of which 12 were waited for; matrix products, arithmetic and copies ran while one was open for 0% of the time, Pallas kernels for 1%

profile of v3, /device:TPU:6, one launch (start us, length us, event | category | flops | bytes accessed | tf_op | source)
XLA Modules:
  0.0 209.7 jit_solution(1373550871510845315)
XLA Ops:
  0.6 1.7 copy-done
  2.3 0.9 copy-done.11
  4.7 1.1 copy-done.5
  5.8 4.6 %all-to-all-start = ((bf16[4,64,2944]{2,1,0:T(8,128)(2,1)}), bf16[4,64,2944]{2,1,0:T(8,128)(2,1)}, u32[]{:S(2)}, u32[]{:S(2)}) async-start(bf16[4,64,2944]{2,1,0:T(8,128)(2,1)} %copy-done.5), calls=%async_computation | async-start | bytes 3014656 | tf_op jit(solution)/shard_map/all_to_all | solution.py:267
  11.2 1.4 copy-done.6
  13.2 3.4 %collective-permute-start = (bf16[272,1280]{1,0:T(8,128)(2,1)S(1)}, bf16[272,1280]{1,0:T(8,128)(2,1)S(1)}, u32[]{:S(2)}, u32[]{:S(2)}) collective-permute-start(bf16[272,1280]{1,0:T(8,128)(2,1)S(1)} %share.2), channel_id=1, source_target_pairs={{0,4},{1,5},{2,6},{3,7},{4,0},{5,1},{6,2},{7,3},{8,12},{9,13},{10,... | collective-permute-start | bytes 2088968 | tf_op jit(solution)/shard_map/ppermute | solution.py:278
  16.6 17.3 %collective-permute-done.waited_ref.first_ref = bf16[272,1280]{1,0:T(8,128)(2,1)S(1)} collective-permute-done((bf16[272,1280]{1,0:T(8,128)(2,1)S(1)}, bf16[272,1280]{1,0:T(8,128)(2,1)S(1)}, u32[]{:S(2)}, u32[]{:S(2)}) %collective-permute-start) | collective-permute-done | bytes 696352 | tf_op jit(solution)/shard_map/ppermute | solution.py:278
  33.9 1.7 fold.1
  35.6 3.3 %collective-permute-start.1 = (bf16[1,64,1920]{2,1,0:T(8,128)(2,1)S(1)}, bf16[1,64,1920]{2,1,0:T(8,128)(2,1)S(1)}, u32[]{:S(2)}, u32[]{:S(2)}) collective-permute-start(bf16[1,64,1920]{2,1,0:T(8,128)(2,1)S(1)} %get-tuple-element.8), channel_id=1, source_target_pairs={{0,4},{1,5},{2,6},{3,7},{4,0},{5,1},{6,2},{7,3},{8,12},{9,13},{10,... | collective-permute-start | bytes 737288 | tf_op jit(solution)/shard_map/ppermute | solution.py:287
  39.0 6.8 %collective-permute-done.1.refs_1_ = bf16[1,64,1920]{2,1,0:T(8,128)(2,1)S(1)} collective-permute-done((bf16[1,64,1920]{2,1,0:T(8,128)(2,1)S(1)}, bf16[1,64,1920]{2,1,0:T(8,128)(2,1)S(1)}, u32[]{:S(2)}, u32[]{:S(2)}) %collective-permute-start.1) | collective-permute-done | bytes 245792 | tf_op jit(solution)/shard_map/ppermute | solution.py:287
  45.7 1.4 attend.3.own_ref
  47.1 3.3 %collective-permute-start.2 = (bf16[1,64,1024]{2,1,0:T(8,128)(2,1)S(1)}, bf16[1,64,1024]{2,1,0:T(8,128)(2,1)S(1)}, u32[]{:S(2)}, u32[]{:S(2)}) collective-permute-start(bf16[1,64,1024]{2,1,0:T(8,128)(2,1)S(1)} %attend.3.own_ref), channel_id=1, source_target_pairs={{0,4},{1,5},{2,6},{3,7},{4,0},{5,1},{6,2},{7,3},{8,12},{9,13},{10,... | collective-permute-start | bytes 393224 | tf_op jit(solution)/shard_map/ppermute | solution.py:288
  50.4 5.0 %collective-permute-done.2.other_ref.refs_0_ = bf16[1,64,1024]{2,1,0:T(8,128)(2,1)S(1)} collective-permute-done((bf16[1,64,1024]{2,1,0:T(8,128)(2,1)S(1)}, bf16[1,64,1024]{2,1,0:T(8,128)(2,1)S(1)}, u32[]{:S(2)}, u32[]{:S(2)}) %collective-permute-start.2) | collective-permute-done | bytes 131104 | tf_op jit(solution)/shard_map/ppermute | solution.py:288
  56.1 1.0 copy-done.10
  57.1 4.2 %all-to-all-start.1 = ((bf16[4,64,2048]{2,1,0:T(8,128)(2,1)}), bf16[4,64,2048]{2,1,0:T(8,128)(2,1)}, u32[]{:S(2)}, u32[]{:S(2)}) async-start(bf16[4,64,2048]{2,1,0:T(8,128)(2,1)} %copy-done.10), calls=%async_computation.1 | async-start | bytes 2097152 | tf_op jit(solution)/shard_map/all_to_all | solution.py:267
  61.9 3.3 %collective-permute-start.3 = (bf16[256,1280]{1,0:T(8,128)(2,1)S(1)}, bf16[256,1280]{1,0:T(8,128)(2,1)S(1)}, u32[]{:S(2)}, u32[]{:S(2)}) collective-permute-start(bf16[256,1280]{1,0:T(8,128)(2,1)S(1)} %share.3), channel_id=1, source_target_pairs={{0,4},{1,5},{2,6},{3,7},{4,0},{5,1},{6,2},{7,3},{8,12},{9,13},{10,... | collective-permute-start | bytes 1966088 | tf_op jit(solution)/shard_map/ppermute | solution.py:278
  65.2 13.5 %collective-permute-done.3.refs_1_.second_ref = bf16[256,1280]{1,0:T(8,128)(2,1)S(1)} collective-permute-done((bf16[256,1280]{1,0:T(8,128)(2,1)S(1)}, bf16[256,1280]{1,0:T(8,128)(2,1)S(1)}, u32[]{:S(2)}, u32[]{:S(2)}) %collective-permute-start.3) | collective-permute-done | bytes 655392 | tf_op jit(solution)/shard_map/ppermute | solution.py:278
  79.5 1.6 copy-done.2
  81.1 1.1 copy-done.8
  82.2 1.0 copy-done.13
  83.3 1.9 project_out.3
  85.2 1.9 collective-permute-start.5
  87.1 4.8 %collective-permute-start.4 = (bf16[256,512]{1,0:T(8,128)(2,1)S(1)}, bf16[256,512]{1,0:T(8,128)(2,1)S(1)}, u32[]{:S(2)}, u32[]{:S(2)}) collective-permute-start(bf16[256,512]{1,0:T(8,128)(2,1)S(1)} %project_out.3), channel_id=1, source_target_pairs={{0,8},{8,16},{16,24},{24,32},{32,40},{40,48},{48,56},{56,64},{64,7... | collective-permute-start | bytes 786440 | tf_op jit(solution)/shard_map/ppermute | solution.py:297
  91.9 4.3 %collective-permute-done.5.other_ref = bf16[256,512]{1,0:T(8,128)(2,1)S(1)} collective-permute-done((bf16[256,512]{1,0:T(8,128)(2,1)S(1)}, bf16[256,512]{1,0:T(8,128)(2,1)S(1)}, u32[]{:S(2)}, u32[]{:S(2)}) %collective-permute-start.5) | collective-permute-done | bytes 262176 | tf_op jit(solution)/shard_map/ppermute | solution.py:296
  96.2 2.9 %collective-permute-done.4.own_ref.x_ref.refs_1_ = bf16[256,512]{1,0:T(8,128)(2,1)S(1)} collective-permute-done((bf16[256,512]{1,0:T(8,128)(2,1)S(1)}, bf16[256,512]{1,0:T(8,128)(2,1)S(1)}, u32[]{:S(2)}, u32[]{:S(2)}) %collective-permute-start.4) | collective-permute-done | bytes 262176 | tf_op jit(solution)/shard_map/ppermute | solution.py:297
  99.2 1.4 project.2
  100.6 15.8 %all_to_all.30.refs_0_ = bf16[4,64,1920]{2,1,0:T(8,128)(2,1)S(1)} all-to-all(bf16[4,64,1920]{2,1,0:T(8,128)(2,1)S(1)} %project.2), channel_id=1, replica_groups={{0,1,2,3},{4,5,6,7},{8,9,10,11},{12,13,14,15},{16,17,18,19},{20,21,22,2..., dimensions={0} | all-to-all | bytes 1966080 | tf_op jit(solution)/shard_map/all_to_all | solution.py:267
  116.4 1.4 attend.4
  117.8 15.7 %all_to_all.31.mixed_ref = bf16[8,64,1024]{2,1,0:T(8,128)(2,1)S(1)} all-to-all(bf16[8,64,1024]{2,1,0:T(8,128)(2,1)S(1)} %attend.4), channel_id=1, replica_groups=mesh['pipe'=64,'tp'=8] {'tp'}, dimensions={0} | all-to-all | bytes 2097152 | tf_op jit(solution)/shard_map/all_to_all | solution.py:267
  133.5 1.2 project_out.4
  134.8 1.9 collective-permute-start.7
  136.7 8.6 %collective-permute-start.6 = (bf16[256,512]{1,0:T(8,128)(2,1)S(1)}, bf16[256,512]{1,0:T(8,128)(2,1)S(1)}, u32[]{:S(2)}, u32[]{:S(2)}) collective-permute-start(bf16[256,512]{1,0:T(8,128)(2,1)S(1)} %project_out.4), channel_id=1, source_target_pairs={{0,8},{8,16},{16,24},{24,32},{32,40},{40,48},{48,56},{56,64},{64,7... | collective-permute-start | bytes 786440 | tf_op jit(solution)/shard_map/ppermute | solution.py:297
  145.3 3.0 %collective-permute-done.7.other_ref = bf16[256,512]{1,0:T(8,128)(2,1)S(1)} collective-permute-done((bf16[256,512]{1,0:T(8,128)(2,1)S(1)}, bf16[256,512]{1,0:T(8,128)(2,1)S(1)}, u32[]{:S(2)}, u32[]{:S(2)}) %collective-permute-start.7) | collective-permute-done | bytes 262176 | tf_op jit(solution)/shard_map/ppermute | solution.py:296
  148.3 0.9 collective-permute-done.6.own_ref.x_ref
  149.2 1.5 project.3
  150.7 0.9 copy-done.17
  152.3 4.0 %all-to-all-start.4 = ((bf16[4,64,1920]{2,1,0:T(8,128)(2,1)}), bf16[4,64,1920]{2,1,0:T(8,128)(2,1)S(1)}, u32[]{:S(2)}, u32[]{:S(2)}) async-start(bf16[4,64,1920]{2,1,0:T(8,128)(2,1)} %copy-done.17), calls=%async_computation.4 | async-start | bytes 1966080 | tf_op jit(solution)/shard_map/all_to_all | solution.py:267
  156.3 1.3 collective-permute-start.8
  158.4 5.2 %collective-permute-done.8.refs_1_ = bf16[128,512]{1,0:T(8,128)(2,1)S(1)} collective-permute-done((bf16[128,512]{1,0:T(8,128)(2,1)}, bf16[128,512]{1,0:T(8,128)(2,1)S(1)}, u32[]{:S(2)}, u32[]{:S(2)}) %collective-permute-start.8) | collective-permute-done | bytes 131104 | tf_op jit(solution)/shard_map/ppermute | solution.py:309
  163.6 7.3 %all-to-all-done.4.refs_0_ = bf16[4,64,1920]{2,1,0:T(8,128)(2,1)S(1)} async-done(((bf16[4,64,1920]{2,1,0:T(8,128)(2,1)}), bf16[4,64,1920]{2,1,0:T(8,128)(2,1)S(1)}, u32[]{:S(2)}, u32[]{:S(2)}) %all-to-all-start.4) | async-done | bytes 983072 | tf_op jit(solution)/shard_map/all_to_all | solution.py:267
  170.9 2.4 %attend.5 = bf16[8,64,1024]{2,1,0:T(8,128)(2,1)} custom-call(s32[5]{0:T(128)S(1)} %stack.23.place_ref, s32[66,256]{1,0:T(8,128)S(1)} %copy-done.18, bf16[4,64,1920]{2,1,0:T(8,128)(2,1)S(1)} %all-to-all-done.4.refs_0_, bf16[128,512]{1,0:T(8,128)(2,1)S(1)} %collective-permute-done.8.refs_1_, bf16[128,512]{1,0:T(8,128)(2,1)S(1)} %collective-permute-done.9.refs_2_), custom_call_target="tpu_custom_call" | custom-call | tf_op jit(solution)/shard_map/attend/pallas_call | solution.py:232
  173.3 5.4 %all-to-all-start.5 = ((bf16[8,64,1024]{2,1,0:T(8,128)(2,1)}), bf16[8,64,1024]{2,1,0:T(8,128)(2,1)S(1)}, u32[]{:S(2)}, u32[]{:S(2)}) async-start(bf16[8,64,1024]{2,1,0:T(8,128)(2,1)} %attend.5), calls=%async_computation.5 | async-start | bytes 2097152 | tf_op jit(solution)/shard_map/all_to_all | solution.py:267
  178.7 6.4 %collective-permute-start.10 = (bf16[128,512]{1,0:T(8,128)(2,1)S(1)}, bf16[128,512]{1,0:T(8,128)(2,1)S(1)}, u32[]{:S(2)}, u32[]{:S(2)}) collective-permute-start(bf16[128,512]{1,0:T(8,128)(2,1)S(1)} %collective-permute-done.8.refs_1_), channel_id=1, source_target_pairs={{256,504},{264,496},{272,488},{280,480},{288,472},{296,464},{304,4... | collective-permute-start | bytes 393224 | tf_op jit(solution)/shard_map/ppermute | solution.py:319
  185.2 1.3 collective-permute-start.11
  186.5 2.7 %collective-permute-done.10 = bf16[128,512]{1,0:T(8,128)(2,1)S(1)} collective-permute-done((bf16[128,512]{1,0:T(8,128)(2,1)S(1)}, bf16[128,512]{1,0:T(8,128)(2,1)S(1)}, u32[]{:S(2)}, u32[]{:S(2)}) %collective-permute-start.10) | collective-permute-done | bytes 131104 | tf_op jit(solution)/shard_map/ppermute | solution.py:319
  189.2 16.8 %collective-permute-done.11 = bf16[128,512]{1,0:T(8,128)(2,1)S(1)} collective-permute-done((bf16[128,512]{1,0:T(8,128)(2,1)S(1)}, bf16[128,512]{1,0:T(8,128)(2,1)S(1)}, u32[]{:S(2)}, u32[]{:S(2)}) %collective-permute-start.11) | collective-permute-done | bytes 131104 | tf_op jit(solution)/shard_map/ppermute | solution.py:320
  206.8 0.9 copy-done.16
  207.7 1.9 project_out.5
  (47 shorter events, 6.4 us)
Async XLA Ops:
  0.6 1.7 copy-start
  2.3 0.9 copy-start.11
  3.2 0.7 copy-start.19
  4.7 1.1 copy-start.5
  5.8 5.3 %copy-start.1 = (bf16[1,512,2304]{2,1,0:T(8,128)(2,1)S(1)}, bf16[1,512,2304]{2,1,0:T(8,128)(2,1)}, u32[]{:S(2)}) copy-start(bf16[1,512,2304]{2,1,0:T(8,128)(2,1)} %param.10) | copy-start | bytes 7077892
  5.8 5.3 %copy-start.20 = (bf16[1,512]{1,0:T(2,128)(2,1)S(1)}, bf16[1,512]{1,0:T(2,128)(2,1)}, u32[]{:S(2)}) copy-start(bf16[1,512]{1,0:T(2,128)(2,1)} %gain_ref.9) | copy-start | bytes 3076
  5.8 28.1 %all-to-all-start = ((bf16[4,64,2944]{2,1,0:T(8,128)(2,1)}), bf16[4,64,2944]{2,1,0:T(8,128)(2,1)}, u32[]{:S(2)}, u32[]{:S(2)}) async-start(bf16[4,64,2944]{2,1,0:T(8,128)(2,1)} %copy-done.5), calls=%async_computation | async-start | bytes 3014656 | tf_op jit(solution)/shard_map/all_to_all | solution.py:267
  11.2 1.4 copy-start.6
  13.2 32.6 %copy-start.18 = (s32[66,256]{1,0:T(8,128)S(1)}, s32[66,256]{1,0:T(8,128)}, u32[]{:S(2)}) copy-start(s32[66,256]{1,0:T(8,128)} %segments_ref.5) | copy-start | bytes 202756
  13.2 20.8 %collective-permute-start = (bf16[272,1280]{1,0:T(8,128)(2,1)S(1)}, bf16[272,1280]{1,0:T(8,128)(2,1)S(1)}, u32[]{:S(2)}, u32[]{:S(2)}) collective-permute-start(bf16[272,1280]{1,0:T(8,128)(2,1)S(1)} %share.2), channel_id=1, source_target_pairs={{0,4},{1,5},{2,6},{3,7},{4,0},{5,1},{6,2},{7,3},{8,12},{9,13},{10,... | collective-permute-start | bytes 2088968 | tf_op jit(solution)/shard_map/ppermute | solution.py:278
  35.6 10.1 %collective-permute-start.1 = (bf16[1,64,1920]{2,1,0:T(8,128)(2,1)S(1)}, bf16[1,64,1920]{2,1,0:T(8,128)(2,1)S(1)}, u32[]{:S(2)}, u32[]{:S(2)}) collective-permute-start(bf16[1,64,1920]{2,1,0:T(8,128)(2,1)S(1)} %get-tuple-element.8), channel_id=1, source_target_pairs={{0,4},{1,5},{2,6},{3,7},{4,0},{5,1},{6,2},{7,3},{8,12},{9,13},{10,... | collective-permute-start | bytes 737288 | tf_op jit(solution)/shard_map/ppermute | solution.py:287
  47.1 8.4 %collective-permute-start.2 = (bf16[1,64,1024]{2,1,0:T(8,128)(2,1)S(1)}, bf16[1,64,1024]{2,1,0:T(8,128)(2,1)S(1)}, u32[]{:S(2)}, u32[]{:S(2)}) collective-permute-start(bf16[1,64,1024]{2,1,0:T(8,128)(2,1)S(1)} %attend.3.own_ref), channel_id=1, source_target_pairs={{0,4},{1,5},{2,6},{3,7},{4,0},{5,1},{6,2},{7,3},{8,12},{9,13},{10,... | collective-permute-start | bytes 393224 | tf_op jit(solution)/shard_map/ppermute | solution.py:288
  56.1 1.0 copy-start.10
  57.1 22.5 %all-to-all-start.1 = ((bf16[4,64,2048]{2,1,0:T(8,128)(2,1)}), bf16[4,64,2048]{2,1,0:T(8,128)(2,1)}, u32[]{:S(2)}, u32[]{:S(2)}) async-start(bf16[4,64,2048]{2,1,0:T(8,128)(2,1)} %copy-done.10), calls=%async_computation.1 | async-start | bytes 2097152 | tf_op jit(solution)/shard_map/all_to_all | solution.py:267
  61.3 18.2 %copy-start.12 = (bf16[1,256,512]{2,1,0:T(8,128)(2,1)S(1)}, bf16[1,256,512]{2,1,0:T(8,128)(2,1)}, u32[]{:S(2)}) copy-start(bf16[1,256,512]{2,1,0:T(8,128)(2,1)} %param.7) | copy-start | bytes 786436
  61.9 16.8 %collective-permute-start.3 = (bf16[256,1280]{1,0:T(8,128)(2,1)S(1)}, bf16[256,1280]{1,0:T(8,128)(2,1)S(1)}, u32[]{:S(2)}, u32[]{:S(2)}) collective-permute-start(bf16[256,1280]{1,0:T(8,128)(2,1)S(1)} %share.3), channel_id=1, source_target_pairs={{0,4},{1,5},{2,6},{3,7},{4,0},{5,1},{6,2},{7,3},{8,12},{9,13},{10,... | collective-permute-start | bytes 1966088 | tf_op jit(solution)/shard_map/ppermute | solution.py:278
  78.7 0.8 copy-start.7
  79.5 1.6 copy-start.2
  81.1 1.1 copy-start.8
  82.2 1.0 copy-start.13
  85.2 11.0 %collective-permute-start.5 = (bf16[256,512]{1,0:T(8,128)(2,1)S(1)}, bf16[256,512]{1,0:T(8,128)(2,1)S(1)}, u32[]{:S(2)}, u32[]{:S(2)}) collective-permute-start(bf16[256,512]{1,0:T(8,128)(2,1)S(1)} %project_out.3), channel_id=1, source_target_pairs={{0,12},{1,13},{2,14},{3,15},{4,8},{5,9},{6,10},{7,11},{8,20},{9,21... | collective-permute-start | bytes 786440 | tf_op jit(solution)/shard_map/ppermute | solution.py:296
  87.1 12.0 %collective-permute-start.4 = (bf16[256,512]{1,0:T(8,128)(2,1)S(1)}, bf16[256,512]{1,0:T(8,128)(2,1)S(1)}, u32[]{:S(2)}, u32[]{:S(2)}) collective-permute-start(bf16[256,512]{1,0:T(8,128)(2,1)S(1)} %project_out.3), channel_id=1, source_target_pairs={{0,8},{8,16},{16,24},{24,32},{32,40},{40,48},{48,56},{56,64},{64,7... | collective-permute-start | bytes 786440 | tf_op jit(solution)/shard_map/ppermute | solution.py:297
  116.4 17.1 %copy-start.3 = (bf16[1,2048,512]{2,1,0:T(8,128)(2,1)S(1)}, bf16[1,2048,512]{2,1,0:T(8,128)(2,1)}, u32[]{:S(2)}) copy-start(bf16[1,2048,512]{2,1,0:T(8,128)(2,1)} %param.11) | copy-start | bytes 6291460
  116.4 17.1 %copy-start.14 = (bf16[2,256,512]{2,1,0:T(8,128)(2,1)S(1)}, bf16[2,256,512]{2,1,0:T(8,128)(2,1)}, u32[]{:S(2)}) copy-start(bf16[2,256,512]{2,1,0:T(8,128)(2,1)} %refs_0_.3) | copy-start | bytes 1572868
  133.5 15.7 %copy-start.9 = (bf16[256,1280]{1,0:T(8,128)(2,1)S(1)}, bf16[256,1280]{1,0:T(8,128)(2,1)}, u32[]{:S(2)}) copy-start(bf16[256,1280]{1,0:T(8,128)(2,1)} %copy-done.7) | copy-start | bytes 1966084
  134.8 13.5 %collective-permute-start.7 = (bf16[256,512]{1,0:T(8,128)(2,1)S(1)}, bf16[256,512]{1,0:T(8,128)(2,1)S(1)}, u32[]{:S(2)}, u32[]{:S(2)}) collective-permute-start(bf16[256,512]{1,0:T(8,128)(2,1)S(1)} %project_out.4), channel_id=1, source_target_pairs={{0,12},{1,13},{2,14},{3,15},{4,8},{5,9},{6,10},{7,11},{8,20},{9,21... | collective-permute-start | bytes 786440 | tf_op jit(solution)/shard_map/ppermute | solution.py:296
  136.7 12.5 %collective-permute-start.6 = (bf16[256,512]{1,0:T(8,128)(2,1)S(1)}, bf16[256,512]{1,0:T(8,128)(2,1)S(1)}, u32[]{:S(2)}, u32[]{:S(2)}) collective-permute-start(bf16[256,512]{1,0:T(8,128)(2,1)S(1)} %project_out.4), channel_id=1, source_target_pairs={{0,8},{8,16},{16,24},{24,32},{32,40},{40,48},{48,56},{56,64},{64,7... | collective-permute-start | bytes 786440 | tf_op jit(solution)/shard_map/ppermute | solution.py:297
  149.2 1.5 copy-start.15
  150.7 1.0 copy-start.17
  151.6 0.7 copy-start.22
  152.3 4.0 %copy-start.21 = (bf16[128,512]{1,0:T(8,128)(2,1)}, bf16[128,512]{1,0:T(8,128)(2,1)S(1)}, u32[]{:S(2)}) copy-start(bf16[128,512]{1,0:T(8,128)(2,1)S(1)} %get-tuple-element.11) | copy-start | bytes 393220
  152.3 18.6 %all-to-all-start.4 = ((bf16[4,64,1920]{2,1,0:T(8,128)(2,1)}), bf16[4,64,1920]{2,1,0:T(8,128)(2,1)S(1)}, u32[]{:S(2)}, u32[]{:S(2)}) async-start(bf16[4,64,1920]{2,1,0:T(8,128)(2,1)} %copy-done.17), calls=%async_computation.4 | async-start | bytes 1966080 | tf_op jit(solution)/shard_map/all_to_all | solution.py:267
  156.3 7.3 %collective-permute-start.8 = (bf16[128,512]{1,0:T(8,128)(2,1)}, bf16[128,512]{1,0:T(8,128)(2,1)S(1)}, u32[]{:S(2)}, u32[]{:S(2)}) collective-permute-start(bf16[128,512]{1,0:T(8,128)(2,1)} %copy-done.22), channel_id=1, source_target_pairs={{0,256},{8,264},{16,272},{24,280},{32,288},{40,296},{48,304},{56,3... | collective-permute-start | bytes 393224 | tf_op jit(solution)/shard_map/ppermute | solution.py:309
  157.6 49.2 %copy-start.4 = (bf16[1,2048,512]{2,1,0:T(8,128)(2,1)S(1)}, bf16[1,2048,512]{2,1,0:T(8,128)(2,1)}, u32[]{:S(2)}) copy-start(bf16[1,2048,512]{2,1,0:T(8,128)(2,1)} %param.11) | copy-start | bytes 6291460
  157.6 6.0 %collective-permute-start.9 = (bf16[128,512]{1,0:T(8,128)(2,1)}, bf16[128,512]{1,0:T(8,128)(2,1)S(1)}, u32[]{:S(2)}, u32[]{:S(2)}) collective-permute-start(bf16[128,512]{1,0:T(8,128)(2,1)} %copy-done.21), channel_id=1, source_target_pairs={{0,248},{8,240},{16,232},{24,224},{32,216},{40,208},{48,200},{56,1... | collective-permute-start | bytes 393224 | tf_op jit(solution)/shard_map/ppermute | solution.py:309
  173.3 33.4 %all-to-all-start.5 = ((bf16[8,64,1024]{2,1,0:T(8,128)(2,1)}), bf16[8,64,1024]{2,1,0:T(8,128)(2,1)S(1)}, u32[]{:S(2)}, u32[]{:S(2)}) async-start(bf16[8,64,1024]{2,1,0:T(8,128)(2,1)} %attend.5), calls=%async_computation.5 | async-start | bytes 2097152 | tf_op jit(solution)/shard_map/all_to_all | solution.py:267
  178.7 10.5 %collective-permute-start.10 = (bf16[128,512]{1,0:T(8,128)(2,1)S(1)}, bf16[128,512]{1,0:T(8,128)(2,1)S(1)}, u32[]{:S(2)}, u32[]{:S(2)}) collective-permute-start(bf16[128,512]{1,0:T(8,128)(2,1)S(1)} %collective-permute-done.8.refs_1_), channel_id=1, source_target_pairs={{256,504},{264,496},{272,488},{280,480},{288,472},{296,464},{304,4... | collective-permute-start | bytes 393224 | tf_op jit(solution)/shard_map/ppermute | solution.py:319
  185.2 20.9 %collective-permute-start.11 = (bf16[128,512]{1,0:T(8,128)(2,1)S(1)}, bf16[128,512]{1,0:T(8,128)(2,1)S(1)}, u32[]{:S(2)}, u32[]{:S(2)}) collective-permute-start(bf16[128,512]{1,0:T(8,128)(2,1)S(1)} %collective-permute-done.9.refs_2_), channel_id=1, source_target_pairs={{0,256},{8,264},{16,272},{24,280},{32,288},{40,296},{48,304},{56,3... | collective-permute-start | bytes 393224 | tf_op jit(solution)/shard_map/ppermute | solution.py:320
  206.8 1.0 copy-start.16

commit v4 on v1

v4 whole, which is shorter than its diff:
```python
import functools

import jax
import jax.numpy as jnp
from jax import lax
from jax.experimental import pallas as pl
from jax.experimental.pallas import tpu as pltpu
from jax.sharding import PartitionSpec as P

HEAD_DIM = 128
Q_HEADS = 16
Q_COLS = Q_HEADS * HEAD_DIM
KV_COLS = 2 * HEAD_DIM
LONGEST_SEGMENT = 128
NORM_EPS = 1e-05
STEP = 256
F32 = jnp.float32
BF16 = jnp.bfloat16

RANK, INDEX, EVICT = range(3)


def window_blocks(rows):
    return (LONGEST_SEGMENT + rows - 2) // rows + 1


def dot(a, b):
    return jnp.dot(a, b, preferred_element_type=F32)


def project_kernel(pieces, streamed, stashed, place_ref, x_ref, gain_ref, *refs):
    weights, earlier, refs = refs[:pieces], refs[pieces : pieces + stashed], refs[pieces + stashed :]
    out_ref, refs = refs[0], refs[1:]
    if stashed:
        stash_refs, refs = refs[:2], refs[2:]
    made_ref, out_sems, refs = refs[0], refs[1], refs[2:]
    parts, rows, columns = out_ref.shape
    blocks = window_blocks(rows)
    last = columns - 128
    spans = [(start, start + STEP) for start in range(0, Q_COLS + KV_COLS, STEP)]
    if streamed:
        x_held, weight_held, x_sem, weight_sems = refs
        x_copy = pltpu.make_async_copy(x_ref, x_held, x_sem)
        x_copy.start()
        weight_copies = []
        for at, (start, end) in enumerate(spans):
            source, target = weights[0].at[:, start:end], weight_held.at[:, start:end]
            weight_copies.append(pltpu.make_async_copy(source, target, weight_sems.at[at]))
            weight_copies[-1].start()
        x_copy.wait()
        x_ref, weights = x_held, [weight_held]
    elif stashed:
        held_ref, stash_sems = refs
        chosen = x_ref[...]
        for at, earlier_ref in enumerate(earlier):
            chosen = jnp.where(place_ref[EVICT] == at, earlier_ref[...], chosen)
        held_ref[...] = chosen
        middle = chosen.shape[0] // 2
        stash_copies = []
        for at, stash_ref in enumerate(stash_refs):
            source = held_ref.at[at * middle : (at + 1) * middle]
            stash_copies.append(pltpu.make_async_copy(source, stash_ref, stash_sems.at[at]))
            stash_copies[-1].start()
    wide = x_ref[...].astype(F32)
    scaled = (wide * gain_ref[:1].astype(F32)).astype(BF16)
    squares = jnp.sum(wide * wide, axis=1, keepdims=True)
    high = squares.astype(BF16).astype(F32)
    low = squares - high
    depth = scaled.shape[1] // len(weights)
    out_copies = []
    for at, (start, end) in enumerate(spans):
        if streamed:
            weight_copies[at].wait()
        tile = dot(scaled[:, :depth], weights[0][:, start:end])
        for piece in range(1, len(weights)):
            tile = tile + dot(scaled[:, piece * depth : (piece + 1) * depth], weights[piece][:, start:end])
        tile = tile.astype(BF16)
        if start < Q_COLS:
            made_ref[:, :, start:end] = tile.reshape(parts, rows, STEP)
        else:
            lane = lax.broadcasted_iota(jnp.int32, (rows, 128), 1)
            for j in range(parts):
                sums = jnp.zeros((rows, 128), F32)
                for b in range(blocks):
                    first = max(j - blocks + 1 + b, 0) * rows
                    made_ref[j, :, start + b * KV_COLS : start + (b + 1) * KV_COLS] = tile[first : first + rows]
                    sums = jnp.where(lane == 2 * b, high[first : first + rows], sums)
                    sums = jnp.where(lane == 2 * b + 1, low[first : first + rows], sums)
                made_ref[j, :, last:] = sums.astype(BF16)
            end = columns
        source, target = made_ref.at[:, :, start:end], out_ref.at[:, :, start:end]
        out_copies.append(pltpu.make_async_copy(source, target, out_sems.at[at]))
        out_copies[-1].start()
    for copy in out_copies:
        copy.wait()
    if stashed:
        for copy in stash_copies:
            copy.wait()


def piece_kernel(begin, value_ref, *refs):
    out_ref, sem = refs[-2:]
    copy = pltpu.make_async_copy(value_ref.at[begin : begin + out_ref.shape[0]], out_ref, sem)
    copy.start()
    copy.wait()


def spread_kernel(value_ref, waited_ref, out_ref):
    out_ref[...] = jnp.broadcast_to(value_ref[...], out_ref.shape)


def attend_kernel(row, width, place_ref, segments_ref, got_ref, *refs):
    out_ref = refs[-1]
    parts, rows, _ = got_ref.shape
    tokens = rows * parts
    blocks = window_blocks(rows)
    span = blocks * rows
    before = span - rows

    def total(start, size):
        value = got_ref[0, :, start : start + size].astype(F32)
        for j in range(1, parts):
            value = value + got_ref[j, :, start : start + size].astype(F32)
        return value

    sums = total(Q_COLS + blocks * KV_COLS, 128)
    scales = []
    for b in range(blocks):
        squares = sums[:, 2 * b : 2 * b + 1] + sums[:, 2 * b + 1 : 2 * b + 2]
        scales.append(lax.rsqrt(squares / width + NORM_EPS))
    keys, values = [], []
    for b in range(blocks):
        both = (total(Q_COLS + b * KV_COLS, KV_COLS) * scales[b]).astype(BF16)
        keys.append(both[:, :HEAD_DIM])
        values.append(both[:, HEAD_DIM:])
    keys = jnp.concatenate(keys, axis=0)
    values = jnp.concatenate(values, axis=0)
    queries = []
    for h in range(Q_HEADS):
        queries.append((total(h * HEAD_DIM, HEAD_DIM) * scales[-1]).astype(BF16))
    queries = jnp.concatenate(queries, axis=0)

    first = place_ref[RANK] * rows - before
    segment_row = segments_ref[pl.ds(row(place_ref[INDEX]), 1), :]
    segment_row = pltpu.roll(segment_row, lax.rem(tokens - first, tokens), 1)
    segment_rows = jnp.broadcast_to(segment_row, (rows, tokens))
    column = lax.broadcasted_iota(jnp.int32, (rows, tokens), 1)
    own = lax.broadcasted_iota(jnp.int32, (rows, tokens), 0) + before
    own_segment = jnp.sum(jnp.where(column == own, segment_rows, 0), axis=1, keepdims=True)
    visible = (segment_rows == own_segment) & (column <= own) & (column + first >= 0)
    visible = visible[:, :span]

    scores = lax.dot_general(
        queries, keys, (((1,), (1,)), ((), ())), preferred_element_type=F32
    ) * HEAD_DIM ** (-0.5)
    scores = scores.reshape(Q_HEADS, rows, span)
    scores = jnp.where(visible[None], scores, F32(-1e30))
    highest = jnp.max(scores, axis=-1, keepdims=True)
    exponentials = jnp.where(visible[None], jnp.exp(scores - highest), F32(0.0))
    totals = jnp.sum(exponentials, axis=-1, keepdims=True)
    attention = (exponentials / totals).astype(BF16).reshape(Q_HEADS * rows, span)
    mixed = dot(attention, values).astype(BF16)
    for h in range(Q_HEADS):
        piece = mixed[h * rows : (h + 1) * rows]
        for j in range(parts):
            out_ref[j, :, h * HEAD_DIM : (h + 1) * HEAD_DIM] = piece


def output_kernel(pieces, spare, place_ref, x_ref, mixed_ref, *refs):
    out_ref = refs[-1]
    depth = refs[0].shape[0]
    product = dot(mixed_ref[:, :depth], refs[0][...])
    for piece in range(1, pieces):
        product = product + dot(mixed_ref[:, piece * depth : (piece + 1) * depth], refs[piece][...])
    result = (x_ref[...].astype(F32) + product).astype(BF16)
    if spare is not None:
        index, tick = spare
        result = jnp.where(place_ref[INDEX] == index, refs[pieces][tick], result)
    out_ref[...] = result


VMEM = pl.BlockSpec(memory_space=pltpu.VMEM)
SMEM = pl.BlockSpec(memory_space=pltpu.SMEM)
ANY = pl.BlockSpec(memory_space=pl.ANY)
HBM = pl.BlockSpec(memory_space=pltpu.HBM)
PARAMS = pltpu.CompilerParams(vmem_limit_bytes=24 * 1024 * 1024)
ALONE = pltpu.CompilerParams(vmem_limit_bytes=60 * 1024 * 1024)


def shard(*shape):
    return jax.ShapeDtypeStruct(shape, BF16)


def project(place, current, gain, weights, parts, streamed=False, earlier=()):
    tokens, width = current.shape
    rows = tokens // parts
    columns = Q_COLS + window_blocks(rows) * KV_COLS + 128
    tiles = (Q_COLS + KV_COLS) // STEP
    outs = [shard(parts, rows, columns)]
    scratch = [pltpu.VMEM((parts, rows, columns), BF16), pltpu.SemaphoreType.DMA((tiles,))]
    if streamed:
        scratch += [pltpu.VMEM(current.shape, BF16), pltpu.VMEM(weights[0].shape, BF16)]
        scratch += [pltpu.SemaphoreType.DMA, pltpu.SemaphoreType.DMA((tiles,))]
    if earlier:
        outs += [shard(tokens // 2, width)] * 2
        scratch += [pltpu.VMEM(current.shape, BF16), pltpu.SemaphoreType.DMA((2,))]
    space = HBM if streamed else VMEM
    return pl.pallas_call(
        functools.partial(project_kernel, len(weights), streamed, len(earlier)),
        out_shape=outs,
        in_specs=[SMEM, space, VMEM] + [space] * len(weights) + [VMEM] * len(earlier),
        out_specs=[ANY] * len(outs),
        scratch_shapes=scratch,
        compiler_params=ALONE if streamed else PARAMS,
        name="project",
    )(place, current, gain, *weights, *earlier)


def halves(value, waited):
    depth = value.shape[0] // 2
    return [
        pl.pallas_call(
            functools.partial(piece_kernel, begin),
            out_shape=shard(depth, *value.shape[1:]),
            in_specs=[ANY] * (1 + len(waited)),
            out_specs=ANY,
            scratch_shapes=[pltpu.SemaphoreType.DMA],
            compiler_params=PARAMS,
            name="piece",
        )(value, *waited)
        for begin in (0, depth)
    ]


def attend(place, segments, got, row, width, waited):
    parts, rows, _ = got.shape
    return pl.pallas_call(
        functools.partial(attend_kernel, row, width),
        out_shape=shard(parts, rows, Q_COLS),
        in_specs=[SMEM, VMEM, VMEM] + [ANY] * len(waited),
        out_specs=VMEM,
        compiler_params=PARAMS,
        name="attend",
    )(place, segments, got, *waited)


def project_out(place, current, mixed, weights, fresh, spare, waited):
    operands = [current, mixed.reshape(current.shape[0], Q_COLS), *weights]
    if spare is not None:
        operands.append(fresh)
    return pl.pallas_call(
        functools.partial(output_kernel, len(weights), spare),
        out_shape=shard(*current.shape),
        in_specs=[SMEM] + [VMEM] * len(operands) + [ANY] * len(waited),
        out_specs=VMEM,
        compiler_params=PARAMS,
        name="project_out",
    )(place, *operands, *waited)


def shards(carried, fresh, gains, qkv_weight, out_weight, segments, evict_tick):
    index = lax.axis_index("pipe")
    sections = lax.axis_size("pipe")
    parts = lax.axis_size("tp")
    width = carried.shape[2] * parts
    qkv_weight, out_weight = qkv_weight[0], out_weight[0]
    place = jnp.stack([lax.axis_index("tp"), index, evict_tick[0]])
    half = sections // 2
    across = [(i, i + half) for i in range(half)]
    turned = [(i, half - 1 - i) for i in range(half)]
    turned_across = [(half + i, sections - 1 - i) for i in range(half)]

    def move(value, by):
        return lax.ppermute(value, "pipe", [(i, (i + by) % sections) for i in range(sections)])

    def exchange(value):
        return lax.all_to_all(value, "tp", split_axis=0, concat_axis=0, tiled=True)

    start = carried[0]
    partial_proj = project(place, start, gains, [qkv_weight], parts, streamed=True)[0]
    sums = exchange(partial_proj)
    next_gains = pl.pallas_call(
        spread_kernel,
        out_shape=shard(16, gains.shape[1]),
        in_specs=[VMEM, ANY],
        out_specs=VMEM,
        compiler_params=PARAMS,
        name="spread",
    )(gains, partial_proj)
    next_gains = move(next_gains, -1)
    next_qkv = [move(piece, -1) for piece in halves(qkv_weight, (partial_proj,))]
    mixed = attend(place, segments, sums, lambda at: at + 2, width, (next_gains, next_qkv[0]))
    next_out = [move(piece, -1) for piece in halves(out_weight, (mixed,))]
    mixed = exchange(mixed)
    spare = (sections - 1, 0)
    result = project_out(place, start, mixed, [out_weight], fresh, spare, (next_qkv[1],))

    current = result
    sums = exchange(project(place, current, next_gains, next_qkv, parts)[0])
    moved = move(current, 1)
    row = lambda at: lax.rem(at + 1, sections) + 1
    mixed = exchange(attend(place, segments, sums, row, width, (next_out[0],)))
    spare = (sections - 2, 1)
    result = project_out(place, current, mixed, next_out, fresh, spare, (moved,))

    current = move(result, 2)
    got, *stash = project(place, current, gains, [qkv_weight], parts, earlier=(start, moved))
    sums = exchange(got)
    top = lax.ppermute(stash[0], "pipe", across)
    low = lax.ppermute(stash[1], "pipe", turned)
    mixed = exchange(attend(place, segments, sums, lambda at: at, width, (top, low)))
    top = lax.ppermute(top, "pipe", turned_across)
    low = lax.ppermute(low, "pipe", across)
    result = project_out(place, current, mixed, [out_weight], None, None, ())
    evicted = jnp.concatenate([top, low], axis=0)
    return (result[None], evicted[None])


def solution(mesh):
    placed = (
        P("pipe", None, "tp"),
        P(None, None, "tp"),
        P("pipe", "tp"),
        P("pipe", "tp", None),
        P("pipe", None, "tp"),
        P(),
        P("pipe"),
    )
    return jax.shard_map(
        shards,
        mesh=mesh,
        in_specs=placed,
        out_specs=(P("pipe", None, "tp"), P("pipe", None, "tp")),
        check_vma=False,
    )
```

time: 201 us -> 252 us (1.25)
  the two profiles are of different devices: /device:TPU:231 before, /device:TPU:6 now
where the time goes in v4:
time: 252 us; the launch traced here: 251 us
  waiting for transfers between devices  114 us (45%)
  starting transfers between devices  89.3 us (35%)
  Pallas kernels  31.7 us (13%)
  local copies, waits for them, and re-layouts  12.4 us (5%)
    ppermute x7, waiting for transfers between devices, move(): lax.ppermute(value, 'pipe', [(i, (i + by) % sections) for i in range(sect...  73.6 us
    ppermute x7, starting transfers between devices, move(): lax.ppermute(value, 'pipe', [(i, (i + by) % sections) for i in range(sect...  42.3 us
    all_to_all x6, starting transfers between devices, exchange(): return lax.all_to_all(value, 'tp', split_axis=0, concat_axis=0, tiled=True)  41.9 us
    ppermute x1, waiting for transfers between devices, shards(): top = lax.ppermute(stash[0], 'pipe', across)  21 us
    pallas_call x3, Pallas kernels, project(): pl.pallas_call(functools.partial(project_kernel, len(weights), streamed,...  13.8 us
    unnamed x52, local copies, waits for them, and re-layouts  12.4 us
    all_to_all x6, waiting for transfers between devices, exchange(): return lax.all_to_all(value, 'tp', split_axis=0, concat_axis=0, tiled=True)  10.2 us
    ppermute x1, waiting for transfers between devices, shards(): low = lax.ppermute(low, 'pipe', across)  9.72 us
  transfers between devices with their start and end apart: 17, of which 7 were waited for; matrix products, arithmetic and copies ran while one was open for 0% of the time, Pallas kernels for 3%

profile of v4, /device:TPU:6, one launch (start us, length us, event | category | flops | bytes accessed | tf_op | source)
XLA Modules:
  0.0 250.8 jit_solution(4762700652120864806)
XLA Ops:
  1.9 6.1 %project.3.waited_ref.refs_0_ = bf16[8,32,3456]{2,1,0:T(8,128)(2,1)} custom-call(s32[3]{0:T(128)} %pad_add_fusion.place_ref, bf16[256,512]{1,0:T(8,128)(2,1)} %bitcast.21, bf16[1,512]{1,0:T(2,128)(2,1)} %gain_ref.3, bf16[512,2304]{1,0:T(8,128)(2,1)} %bitcast.11), custom_call_target="tpu_custom_call" | custom-call | tf_op jit(solution)/shard_map/project/pallas_call | solution.py:208
  8.0 7.6 %all-to-all-start = ((bf16[8,32,3456]{2,1,0:T(8,128)(2,1)}), bf16[8,32,3456]{2,1,0:T(8,128)(2,1)}, u32[]{:S(2)}, u32[]{:S(2)}) async-start(bf16[8,32,3456]{2,1,0:T(8,128)(2,1)} %project.3.waited_ref.refs_0_), calls=%async_computation | async-start | bytes 3538944 | tf_op jit(solution)/shard_map/all_to_all | solution.py:277
  15.6 1.7 copy-done.1
  17.5 10.5 %collective-permute-start.1 = (bf16[256,2304]{1,0:T(8,128)(2,1)S(1)}, bf16[256,2304]{1,0:T(8,128)(2,1)S(1)}, u32[]{:S(2)}, u32[]{:S(2)}) collective-permute-start(bf16[256,2304]{1,0:T(8,128)(2,1)S(1)} %piece.4), channel_id=1, source_target_pairs={{0,504},{8,0},{16,8},{24,16},{32,24},{40,32},{48,40},{56,48},{64,5... | collective-permute-start | bytes 3538952 | tf_op jit(solution)/shard_map/ppermute | solution.py:274
  28.0 1.1 piece.5
  29.1 3.3 %collective-permute-start.2 = (bf16[256,2304]{1,0:T(8,128)(2,1)}, bf16[256,2304]{1,0:T(8,128)(2,1)}, u32[]{:S(2)}, u32[]{:S(2)}) collective-permute-start(bf16[256,2304]{1,0:T(8,128)(2,1)} %piece.5), channel_id=1, source_target_pairs={{0,504},{8,0},{16,8},{24,16},{32,24},{40,32},{48,40},{56,48},{64,5... | collective-permute-start | bytes 3538952 | tf_op jit(solution)/shard_map/ppermute | solution.py:274
  32.4 1.9 collective-permute-start
  34.4 20.2 %collective-permute-done.refs_0_.gain_ref = bf16[16,512]{1,0:T(8,128)(2,1)S(1)} collective-permute-done((bf16[16,512]{1,0:T(8,128)(2,1)S(1)}, bf16[16,512]{1,0:T(8,128)(2,1)S(1)}, u32[]{:S(2)}, u32[]{:S(2)}) %collective-permute-start) | collective-permute-done | bytes 16416 | tf_op jit(solution)/shard_map/ppermute | solution.py:274
  54.6 3.4 %attend.3.refs_0_ = bf16[8,32,2048]{2,1,0:T(8,128)(2,1)} custom-call(s32[3]{0:T(128)S(1)} %copy-done.20, s32[66,256]{1,0:T(8,128)S(1)} %copy-done.16, bf16[8,32,3456]{2,1,0:T(8,128)(2,1)} %all-to-all-done.got_ref, bf16[16,512]{1,0:T(8,128)(2,1)S(1)} %collective-permute-done.refs_0_.gain_ref, bf16[256,2304]{1,0:T(8,128)(2,1)S(1)} %collective-permute-done.1.refs_1_.refs_0_), custom_call_target="tpu_custom_call" | custom-call | tf_op jit(solution)/shard_map/attend/pallas_call | solution.py:237
  58.0 7.3 %all-to-all-start.1 = ((bf16[8,32,2048]{2,1,0:T(8,128)(2,1)}), bf16[8,32,2048]{2,1,0:T(8,128)(2,1)}, u32[]{:S(2)}, u32[]{:S(2)}) async-start(bf16[8,32,2048]{2,1,0:T(8,128)(2,1)} %attend.3.refs_0_), calls=%async_computation.1 | async-start | bytes 2097152 | tf_op jit(solution)/shard_map/all_to_all | solution.py:277
  65.4 10.1 %all-to-all-done.1 = bf16[8,32,2048]{2,1,0:T(8,128)(2,1)} async-done(((bf16[8,32,2048]{2,1,0:T(8,128)(2,1)}), bf16[8,32,2048]{2,1,0:T(8,128)(2,1)}, u32[]{:S(2)}, u32[]{:S(2)}) %all-to-all-start.1) | async-done | bytes 1048608 | tf_op jit(solution)/shard_map/all_to_all | solution.py:277
  75.5 1.0 copy-done.11
  76.5 0.6 copy-done.21
  77.2 1.9 project_out.3.x_ref
  79.1 4.0 %project.4 = bf16[8,32,3456]{2,1,0:T(8,128)(2,1)S(1)} custom-call(s32[3]{0:T(128)S(1)} %copy-done.22, bf16[256,512]{1,0:T(8,128)(2,1)S(1)} %project_out.3.x_ref, bf16[16,512]{1,0:T(8,128)(2,1)S(1)} %collective-permute-done.refs_0_.gain_ref, bf16[256,2304]{1,0:T(8,128)(2,1)S(1)} %collective-permute-done.1.refs_1_.refs_0_, ...), custom_call_target="tpu_custom_call" | custom-call | tf_op jit(solution)/shard_map/project/pallas_call | solution.py:208
  83.2 1.2 copy-done.4
  84.4 0.7 copy-done.9
  85.1 6.5 %all-to-all-start.2 = ((bf16[8,32,3456]{2,1,0:T(8,128)(2,1)}), bf16[8,32,3456]{2,1,0:T(8,128)(2,1)}, u32[]{:S(2)}, u32[]{:S(2)}) async-start(bf16[8,32,3456]{2,1,0:T(8,128)(2,1)} %copy-done.4), calls=%async_computation.2 | async-start | bytes 3538944 | tf_op jit(solution)/shard_map/all_to_all | solution.py:277
  91.7 19.6 %collective-permute-start.3 = (bf16[1024,512]{1,0:T(8,128)(2,1)S(1)}, bf16[1024,512]{1,0:T(8,128)(2,1)S(1)}, u32[]{:S(2)}, u32[]{:S(2)}) collective-permute-start(bf16[1024,512]{1,0:T(8,128)(2,1)S(1)} %piece.6), channel_id=1, source_target_pairs={{0,504},{8,0},{16,8},{24,16},{32,24},{40,32},{48,40},{56,48},{64,5... | collective-permute-start | bytes 3145736 | tf_op jit(solution)/shard_map/ppermute | solution.py:274
  111.3 1.0 piece.7
  112.3 3.1 %collective-permute-start.4 = (bf16[1024,512]{1,0:T(8,128)(2,1)}, bf16[1024,512]{1,0:T(8,128)(2,1)}, u32[]{:S(2)}, u32[]{:S(2)}) collective-permute-start(bf16[1024,512]{1,0:T(8,128)(2,1)} %piece.7), channel_id=1, source_target_pairs={{0,504},{8,0},{16,8},{24,16},{32,24},{40,32},{48,40},{56,48},{64,5... | collective-permute-start | bytes 3145736 | tf_op jit(solution)/shard_map/ppermute | solution.py:274
  115.4 8.2 %collective-permute-done.3.refs_0_ = bf16[1024,512]{1,0:T(8,128)(2,1)S(1)} collective-permute-done((bf16[1024,512]{1,0:T(8,128)(2,1)S(1)}, bf16[1024,512]{1,0:T(8,128)(2,1)S(1)}, u32[]{:S(2)}, u32[]{:S(2)}) %collective-permute-start.3) | collective-permute-done | bytes 1048608 | tf_op jit(solution)/shard_map/ppermute | solution.py:274
  123.6 2.7 %attend.4 = bf16[8,32,2048]{2,1,0:T(8,128)(2,1)S(1)} custom-call(s32[3]{0:T(128)S(1)} %copy-done.23, s32[66,256]{1,0:T(8,128)S(1)} %copy-done.17, bf16[8,32,3456]{2,1,0:T(8,128)(2,1)} %all-to-all-done.2.got_ref, bf16[1024,512]{1,0:T(8,128)(2,1)S(1)} %collective-permute-done.3.refs_0_), custom_call_target="tpu_custom_call" | custom-call | tf_op jit(solution)/shard_map/attend/pallas_call | solution.py:237
  126.4 1.0 copy-done.7
  127.4 7.2 %all-to-all-start.3 = ((bf16[8,32,2048]{2,1,0:T(8,128)(2,1)}), bf16[8,32,2048]{2,1,0:T(8,128)(2,1)S(1)}, u32[]{:S(2)}, u32[]{:S(2)}) async-start(bf16[8,32,2048]{2,1,0:T(8,128)(2,1)} %copy-done.7), calls=%async_computation.3 | async-start | bytes 2097152 | tf_op jit(solution)/shard_map/all_to_all | solution.py:277
  134.6 1.9 collective-permute-start.5
  136.5 30.6 %collective-permute-done.5.refs_3_.refs_2_ = bf16[256,512]{1,0:T(8,128)(2,1)S(1)} collective-permute-done((bf16[256,512]{1,0:T(8,128)(2,1)}, bf16[256,512]{1,0:T(8,128)(2,1)S(1)}, u32[]{:S(2)}, u32[]{:S(2)}) %collective-permute-start.5) | collective-permute-done | bytes 262176 | tf_op jit(solution)/shard_map/ppermute | solution.py:274
  167.1 0.7 copy-done.14
  167.8 1.2 copy-done.6
  169.0 0.9 copy-done.10
  170.0 1.0 copy-done.12
  171.0 0.9 copy-done.15
  172.0 2.1 project_out.4
  174.1 1.9 collective-permute-start.6
  176.0 14.6 %collective-permute-done.6.x_ref = bf16[256,512]{1,0:T(8,128)(2,1)S(1)} collective-permute-done((bf16[256,512]{1,0:T(8,128)(2,1)S(1)}, bf16[256,512]{1,0:T(8,128)(2,1)S(1)}, u32[]{:S(2)}, u32[]{:S(2)}) %collective-permute-start.6) | collective-permute-done | bytes 262176 | tf_op jit(solution)/shard_map/ppermute | solution.py:274
  190.6 3.7 %project.5 = (bf16[8,32,3456]{2,1,0:T(8,128)(2,1)S(1)}, bf16[128,512]{1,0:T(8,128)(2,1)S(1)}, bf16[128,512]{1,0:T(8,128)(2,1)S(1)}) custom-call(s32[3]{0:T(128)S(1)} %copy-done.23, bf16[256,512]{1,0:T(8,128)(2,1)S(1)} %collective-permute-done.6.x_ref, bf16[1,512]{1,0:T(2,128)(2,1)S(1)} %copy-done.25, bf16[512,2304]{1,0:T(8,128)(2,1)S(1)} %bitcast.14, ...), custom_call_target="tpu_custom_call" | custom-call | tf_op jit(solution)/shard_map/project/pallas_call | solution.py:208
  194.2 1.2 copy-done.13
  195.5 6.1 %all-to-all-start.4 = ((bf16[8,32,3456]{2,1,0:T(8,128)(2,1)}), bf16[8,32,3456]{2,1,0:T(8,128)(2,1)}, u32[]{:S(2)}, u32[]{:S(2)}) async-start(bf16[8,32,3456]{2,1,0:T(8,128)(2,1)} %copy-done.13), calls=%async_computation.4 | async-start | bytes 3538944 | tf_op jit(solution)/shard_map/all_to_all | solution.py:277
  201.5 0.7 collective-permute-start.8
  202.2 1.3 collective-permute-start.7
  203.5 21.0 %collective-permute-done.7.refs_0_ = bf16[128,512]{1,0:T(8,128)(2,1)S(1)} collective-permute-done((bf16[128,512]{1,0:T(8,128)(2,1)S(1)}, bf16[128,512]{1,0:T(8,128)(2,1)S(1)}, u32[]{:S(2)}, u32[]{:S(2)}) %collective-permute-start.7) | collective-permute-done | bytes 131104 | tf_op jit(solution)/shard_map/ppermute | solution.py:309
  224.6 3.4 %attend.5 = bf16[8,32,2048]{2,1,0:T(8,128)(2,1)} custom-call(s32[3]{0:T(128)S(1)} %copy-done.23, s32[66,256]{1,0:T(8,128)S(1)} %copy-done.17, bf16[8,32,3456]{2,1,0:T(8,128)(2,1)} %all-to-all-done.4.got_ref, bf16[128,512]{1,0:T(8,128)(2,1)S(1)} %collective-permute-done.7.refs_0_, bf16[128,512]{1,0:T(8,128)(2,1)S(1)} %collective-permute-done.8.refs_1_), custom_call_target="tpu_custom_call" | custom-call | tf_op jit(solution)/shard_map/attend/pallas_call | solution.py:237
  228.0 7.2 %all-to-all-start.5 = ((bf16[8,32,2048]{2,1,0:T(8,128)(2,1)}), bf16[8,32,2048]{2,1,0:T(8,128)(2,1)S(1)}, u32[]{:S(2)}, u32[]{:S(2)}) async-start(bf16[8,32,2048]{2,1,0:T(8,128)(2,1)} %attend.5), calls=%async_computation.5 | async-start | bytes 2097152 | tf_op jit(solution)/shard_map/all_to_all | solution.py:277
  235.2 1.3 collective-permute-start.10
  236.5 1.9 collective-permute-start.9
  238.4 9.7 %collective-permute-done.10 = bf16[128,512]{1,0:T(8,128)(2,1)S(1)} collective-permute-done((bf16[128,512]{1,0:T(8,128)(2,1)}, bf16[128,512]{1,0:T(8,128)(2,1)S(1)}, u32[]{:S(2)}, u32[]{:S(2)}) %collective-permute-start.10) | collective-permute-done | bytes 131104 | tf_op jit(solution)/shard_map/ppermute | solution.py:313
  248.1 0.7 maximum_bitcast_fusion
  248.8 2.0 project_out.5
  (54 shorter events, 1.1 us)
Async XLA Ops:
  8.0 7.6 %copy-start = (bf16[8,32,3456]{2,1,0:T(8,128)(2,1)S(1)}, bf16[8,32,3456]{2,1,0:T(8,128)(2,1)}, u32[]{:S(2)}) copy-start(bf16[8,32,3456]{2,1,0:T(8,128)(2,1)} %project.3.waited_ref.refs_0_) | copy-start | bytes 5308420
  8.0 46.6 %all-to-all-start = ((bf16[8,32,3456]{2,1,0:T(8,128)(2,1)}), bf16[8,32,3456]{2,1,0:T(8,128)(2,1)}, u32[]{:S(2)}, u32[]{:S(2)}) async-start(bf16[8,32,3456]{2,1,0:T(8,128)(2,1)} %project.3.waited_ref.refs_0_), calls=%async_computation | async-start | bytes 3538944 | tf_op jit(solution)/shard_map/all_to_all | solution.py:277
  15.6 1.7 copy-start.1
  17.5 14.9 %copy-start.24 = (bf16[1,512]{1,0:T(2,128)(2,1)S(1)}, bf16[1,512]{1,0:T(2,128)(2,1)}, u32[]{:S(2)}) copy-start(bf16[1,512]{1,0:T(2,128)(2,1)} %gain_ref.3) | copy-start | bytes 3076
  17.5 37.1 %collective-permute-start.1 = (bf16[256,2304]{1,0:T(8,128)(2,1)S(1)}, bf16[256,2304]{1,0:T(8,128)(2,1)S(1)}, u32[]{:S(2)}, u32[]{:S(2)}) collective-permute-start(bf16[256,2304]{1,0:T(8,128)(2,1)S(1)} %piece.4), channel_id=1, source_target_pairs={{0,504},{8,0},{16,8},{24,16},{32,24},{40,32},{48,40},{56,48},{64,5... | collective-permute-start | bytes 3538952 | tf_op jit(solution)/shard_map/ppermute | solution.py:274
  29.1 25.5 %copy-start.16 = (s32[66,256]{1,0:T(8,128)S(1)}, s32[66,256]{1,0:T(8,128)}, u32[]{:S(2)}) copy-start(s32[66,256]{1,0:T(8,128)} %segments_ref.5) | copy-start | bytes 202756
  29.1 25.5 %copy-start.20 = (s32[3]{0:T(128)S(1)}, s32[3]{0:T(128)}, u32[]{:S(2)}) copy-start(s32[3]{0:T(128)} %pad_add_fusion.place_ref) | copy-start | bytes 40
  29.1 36.2 %collective-permute-start.2 = (bf16[256,2304]{1,0:T(8,128)(2,1)}, bf16[256,2304]{1,0:T(8,128)(2,1)}, u32[]{:S(2)}, u32[]{:S(2)}) collective-permute-start(bf16[256,2304]{1,0:T(8,128)(2,1)} %piece.5), channel_id=1, source_target_pairs={{0,504},{8,0},{16,8},{24,16},{32,24},{40,32},{48,40},{56,48},{64,5... | collective-permute-start | bytes 3538952 | tf_op jit(solution)/shard_map/ppermute | solution.py:274
  32.4 22.2 %collective-permute-start = (bf16[16,512]{1,0:T(8,128)(2,1)S(1)}, bf16[16,512]{1,0:T(8,128)(2,1)S(1)}, u32[]{:S(2)}, u32[]{:S(2)}) collective-permute-start(bf16[16,512]{1,0:T(8,128)(2,1)S(1)} %spread.1), channel_id=1, source_target_pairs={{0,504},{8,0},{16,8},{24,16},{32,24},{40,32},{48,40},{56,48},{64,5... | collective-permute-start | bytes 49160 | tf_op jit(solution)/shard_map/ppermute | solution.py:274
  54.6 20.9 %copy-start.8 = (bf16[1,256,512]{2,1,0:T(8,128)(2,1)S(1)}, bf16[1,256,512]{2,1,0:T(8,128)(2,1)}, u32[]{:S(2)}) copy-start(bf16[1,256,512]{2,1,0:T(8,128)(2,1)} %param.7) | copy-start | bytes 786436
  58.0 17.5 %copy-start.3 = (bf16[1,2048,512]{2,1,0:T(8,128)(2,1)S(1)}, bf16[1,2048,512]{2,1,0:T(8,128)(2,1)}, u32[]{:S(2)}) copy-start(bf16[1,2048,512]{2,1,0:T(8,128)(2,1)} %param.11) | copy-start | bytes 6291460
  58.0 17.5 %all-to-all-start.1 = ((bf16[8,32,2048]{2,1,0:T(8,128)(2,1)}), bf16[8,32,2048]{2,1,0:T(8,128)(2,1)}, u32[]{:S(2)}, u32[]{:S(2)}) async-start(bf16[8,32,2048]{2,1,0:T(8,128)(2,1)} %attend.3.refs_0_), calls=%async_computation.1 | async-start | bytes 2097152 | tf_op jit(solution)/shard_map/all_to_all | solution.py:277
  75.5 1.0 copy-start.11
  76.5 0.6 copy-start.21
  77.2 1.9 copy-start.22
  83.2 1.2 copy-start.4
  84.4 0.7 copy-start.9
  85.1 38.5 %all-to-all-start.2 = ((bf16[8,32,3456]{2,1,0:T(8,128)(2,1)}), bf16[8,32,3456]{2,1,0:T(8,128)(2,1)}, u32[]{:S(2)}, u32[]{:S(2)}) async-start(bf16[8,32,3456]{2,1,0:T(8,128)(2,1)} %copy-done.4), calls=%async_computation.2 | async-start | bytes 3538944 | tf_op jit(solution)/shard_map/all_to_all | solution.py:277
  91.6 32.0 %copy-start.17 = (s32[66,256]{1,0:T(8,128)S(1)}, s32[66,256]{1,0:T(8,128)}, u32[]{:S(2)}) copy-start(s32[66,256]{1,0:T(8,128)} %segments_ref.5) | copy-start | bytes 202756
  91.7 31.9 %copy-start.23 = (s32[3]{0:T(128)S(1)}, s32[3]{0:T(128)}, u32[]{:S(2)}) copy-start(s32[3]{0:T(128)} %pad_add_fusion.place_ref) | copy-start | bytes 40
  91.7 31.9 %collective-permute-start.3 = (bf16[1024,512]{1,0:T(8,128)(2,1)S(1)}, bf16[1024,512]{1,0:T(8,128)(2,1)S(1)}, u32[]{:S(2)}, u32[]{:S(2)}) collective-permute-start(bf16[1024,512]{1,0:T(8,128)(2,1)S(1)} %piece.6), channel_id=1, source_target_pairs={{0,504},{8,0},{16,8},{24,16},{32,24},{40,32},{48,40},{56,48},{64,5... | collective-permute-start | bytes 3145736 | tf_op jit(solution)/shard_map/ppermute | solution.py:274
  112.3 24.2 %collective-permute-start.4 = (bf16[1024,512]{1,0:T(8,128)(2,1)}, bf16[1024,512]{1,0:T(8,128)(2,1)}, u32[]{:S(2)}, u32[]{:S(2)}) collective-permute-start(bf16[1024,512]{1,0:T(8,128)(2,1)} %piece.7), channel_id=1, source_target_pairs={{0,504},{8,0},{16,8},{24,16},{32,24},{40,32},{48,40},{56,48},{64,5... | collective-permute-start | bytes 3145736 | tf_op jit(solution)/shard_map/ppermute | solution.py:274
  123.6 2.8 %copy-start.5 = (bf16[1024,512]{1,0:T(8,128)(2,1)}, bf16[1024,512]{1,0:T(8,128)(2,1)S(1)}, u32[]{:S(2)}) copy-start(bf16[1024,512]{1,0:T(8,128)(2,1)S(1)} %collective-permute-done.3.refs_0_) | copy-start | bytes 3145732
  126.4 1.0 copy-start.7
  127.4 40.4 %all-to-all-start.3 = ((bf16[8,32,2048]{2,1,0:T(8,128)(2,1)}), bf16[8,32,2048]{2,1,0:T(8,128)(2,1)S(1)}, u32[]{:S(2)}, u32[]{:S(2)}) async-start(bf16[8,32,2048]{2,1,0:T(8,128)(2,1)} %copy-done.7), calls=%async_computation.3 | async-start | bytes 2097152 | tf_op jit(solution)/shard_map/all_to_all | solution.py:277
  134.6 32.5 %collective-permute-start.5 = (bf16[256,512]{1,0:T(8,128)(2,1)}, bf16[256,512]{1,0:T(8,128)(2,1)S(1)}, u32[]{:S(2)}, u32[]{:S(2)}) collective-permute-start(bf16[256,512]{1,0:T(8,128)(2,1)} %copy-done.9), channel_id=1, source_target_pairs={{0,8},{8,16},{16,24},{24,32},{32,40},{40,48},{48,56},{56,64},{64,7... | collective-permute-start | bytes 786440 | tf_op jit(solution)/shard_map/ppermute | solution.py:274
  167.1 0.7 copy-start.14
  167.8 1.2 copy-start.6
  169.0 0.9 copy-start.10
  170.0 1.0 copy-start.12
  171.0 0.9 copy-start.15
  172.0 18.6 %copy-start.2 = (bf16[1,512,2304]{2,1,0:T(8,128)(2,1)S(1)}, bf16[1,512,2304]{2,1,0:T(8,128)(2,1)}, u32[]{:S(2)}) copy-start(bf16[1,512,2304]{2,1,0:T(8,128)(2,1)} %param.10) | copy-start | bytes 7077892
  172.0 18.6 %copy-start.25 = (bf16[1,512]{1,0:T(2,128)(2,1)S(1)}, bf16[1,512]{1,0:T(2,128)(2,1)}, u32[]{:S(2)}) copy-start(bf16[1,512]{1,0:T(2,128)(2,1)} %gain_ref.3) | copy-start | bytes 3076
  174.1 16.5 %collective-permute-start.6 = (bf16[256,512]{1,0:T(8,128)(2,1)S(1)}, bf16[256,512]{1,0:T(8,128)(2,1)S(1)}, u32[]{:S(2)}, u32[]{:S(2)}) collective-permute-start(bf16[256,512]{1,0:T(8,128)(2,1)S(1)} %project_out.4), channel_id=1, source_target_pairs={{0,16},{8,24},{16,32},{24,40},{32,48},{40,56},{48,64},{56,72},{64,... | collective-permute-start | bytes 786440 | tf_op jit(solution)/shard_map/ppermute | solution.py:274
  194.2 1.2 copy-start.13
  195.5 29.1 %all-to-all-start.4 = ((bf16[8,32,3456]{2,1,0:T(8,128)(2,1)}), bf16[8,32,3456]{2,1,0:T(8,128)(2,1)}, u32[]{:S(2)}, u32[]{:S(2)}) async-start(bf16[8,32,3456]{2,1,0:T(8,128)(2,1)} %copy-done.13), calls=%async_computation.4 | async-start | bytes 3538944 | tf_op jit(solution)/shard_map/all_to_all | solution.py:277
  201.5 2.0 collective-permute-start.8
  202.2 22.3 %collective-permute-start.7 = (bf16[128,512]{1,0:T(8,128)(2,1)S(1)}, bf16[128,512]{1,0:T(8,128)(2,1)S(1)}, u32[]{:S(2)}, u32[]{:S(2)}) collective-permute-start(bf16[128,512]{1,0:T(8,128)(2,1)S(1)} %get-tuple-element.6), channel_id=1, source_target_pairs={{0,256},{8,264},{16,272},{24,280},{32,288},{40,296},{48,304},{56,3... | collective-permute-start | bytes 393224 | tf_op jit(solution)/shard_map/ppermute | solution.py:309
  203.5 24.4 %copy-start.18 = (bf16[128,512]{1,0:T(8,128)(2,1)}, bf16[128,512]{1,0:T(8,128)(2,1)S(1)}, u32[]{:S(2)}) copy-start(bf16[128,512]{1,0:T(8,128)(2,1)S(1)} %collective-permute-done.8.refs_1_) | copy-start | bytes 393220
  224.6 3.4 %copy-start.19 = (bf16[128,512]{1,0:T(8,128)(2,1)}, bf16[128,512]{1,0:T(8,128)(2,1)S(1)}, u32[]{:S(2)}) copy-start(bf16[128,512]{1,0:T(8,128)(2,1)S(1)} %collective-permute-done.7.refs_0_) | copy-start | bytes 393220
  228.0 20.9 %all-to-all-start.5 = ((bf16[8,32,2048]{2,1,0:T(8,128)(2,1)}), bf16[8,32,2048]{2,1,0:T(8,128)(2,1)S(1)}, u32[]{:S(2)}, u32[]{:S(2)}) async-start(bf16[8,32,2048]{2,1,0:T(8,128)(2,1)} %attend.5), calls=%async_computation.5 | async-start | bytes 2097152 | tf_op jit(solution)/shard_map/all_to_all | solution.py:277
  235.2 12.9 %collective-permute-start.10 = (bf16[128,512]{1,0:T(8,128)(2,1)}, bf16[128,512]{1,0:T(8,128)(2,1)S(1)}, u32[]{:S(2)}, u32[]{:S(2)}) collective-permute-start(bf16[128,512]{1,0:T(8,128)(2,1)} %copy-done.18), channel_id=1, source_target_pairs={{0,256},{8,264},{16,272},{24,280},{32,288},{40,296},{48,304},{56,3... | collective-permute-start | bytes 393224 | tf_op jit(solution)/shard_map/ppermute | solution.py:313
  236.5 11.6 %collective-permute-start.9 = (bf16[128,512]{1,0:T(8,128)(2,1)}, bf16[128,512]{1,0:T(8,128)(2,1)S(1)}, u32[]{:S(2)}, u32[]{:S(2)}) collective-permute-start(bf16[128,512]{1,0:T(8,128)(2,1)} %copy-done.19), channel_id=1, source_target_pairs={{256,504},{264,496},{272,488},{280,480},{288,472},{296,464},{304,4... | collective-permute-start | bytes 393224 | tf_op jit(solution)/shard_map/ppermute | solution.py:312

commit v5 on v1

--- a/solution.py
+++ b/solution.py
@@ -21,11 +21,52 @@
     return (LONGEST_SEGMENT + rows - 2) // rows + 1
 
 
-def project_kernel(parts, x_ref, gain_ref, weight_ref, out_ref):
-    tokens = x_ref.shape[0]
-    rows = tokens // parts
+FIRST, EVICT = range(2)
+
+
+def copy_all(sources, targets, sems):
+    copies = [pltpu.make_async_copy(a, b, sems.at[at]) for at, (a, b) in enumerate(zip(sources, targets))]
+    for copy in copies:
+        copy.start()
+    return copies
+
+
+def tick_input(tick, flags_ref, arrived_ref, fresh_ref):
+    if tick == 0:
+        return arrived_ref[...]
+    return jnp.where(flags_ref[FIRST] == 1, fresh_ref[tick - 1], arrived_ref[...])
+
+
+def project_kernel(tick, stash, flags_ref, fresh_ref, gain_ref, weight_ref, *refs):
+    arrived, refs = (refs[: tick + 1], refs[tick + 1 :]) if stash else (refs[:1], refs[1:])
+    out_ref, refs = refs[0], refs[1:]
+    if stash:
+        stash_refs, refs = refs[:2], refs[2:]
+    made_ref, out_sems, refs = refs[0], refs[1], refs[2:]
+    parts, rows, columns = out_ref.shape
     blocks = window_blocks(rows)
-    wide = x_ref[...].astype(F32)
+    last = columns - 128
+    copies = []
+    if tick == 0:
+        x_held, weight_held, in_sems = refs
+        count = in_sems.shape[0] - 1
+        depth = weight_held.shape[0] // count
+        spans = [slice(at * depth, (at + 1) * depth) for at in range(count)]
+        sources = [arrived[0]] + [weight_ref.at[span] for span in spans]
+        targets = [x_held] + [weight_held.at[span] for span in spans]
+        for copy in copy_all(sources, targets, in_sems):
+            copy.wait()
+        arrived, weight_ref = [x_held], weight_held
+    current = tick_input(tick, flags_ref, arrived[-1], fresh_ref)
+    if stash:
+        held_ref, stash_sems = refs
+        chosen = current
+        for at in range(tick):
+            chosen = jnp.where(flags_ref[EVICT] == at, tick_input(at, flags_ref, arrived[at], fresh_ref), chosen)
+        held_ref[...] = chosen
+        middle = chosen.shape[0] // 2
+        copies += copy_all([held_ref.at[:middle], held_ref.at[middle:]], stash_refs, stash_sems)
+    wide = current.astype(F32)
     scaled = (wide * gain_ref[...].astype(F32)).astype(BF16)
     squares = jnp.sum(wide * wide, axis=1, keepdims=True)
     high = squares.astype(BF16).astype(F32)
@@ -34,21 +75,25 @@
     step = 256
     for start in range(0, Q_COLS, step):
         tile = jnp.dot(scaled, weight_ref[:, start : start + step], preferred_element_type=F32)
-        out_ref[:, :, start : start + step] = tile.astype(BF16).reshape(parts, rows, step)
+        made_ref[:, :, start : start + step] = tile.astype(BF16).reshape(parts, rows, step)
     tile = jnp.dot(scaled, weight_ref[:, Q_COLS:], preferred_element_type=F32).astype(BF16)
-    last = Q_COLS + blocks * KV_COLS
     for j in range(parts):
         sums = jnp.zeros((rows, 128), F32)
         for b in range(blocks):
             at = max(j - blocks + 1 + b, 0) * rows
             start = Q_COLS + b * KV_COLS
-            out_ref[j, :, start : start + KV_COLS] = tile[at : at + rows]
+            made_ref[j, :, start : start + KV_COLS] = tile[at : at + rows]
             sums = jnp.where(lane == 2 * b, high[at : at + rows], sums)
             sums = jnp.where(lane == 2 * b + 1, low[at : at + rows], sums)
-        out_ref[j, :, last:] = sums.astype(BF16)
-
-
-def attend_kernel(parts, width, place_ref, segments_ref, got_ref, out_ref):
+        made_ref[j, :, last:] = sums.astype(BF16)
+        copies.append(pltpu.make_async_copy(made_ref.at[j], out_ref.at[j], out_sems.at[j]))
+        copies[-1].start()
+    for copy in copies:
+        copy.wait()
+
+
+def attend_kernel(parts, width, place_ref, segments_ref, got_ref, *refs):
+    out_ref, held_ref, out_sems = refs[-3:]
     rows = got_ref.shape[1]
     tokens = rows * parts
     blocks = window_blocks(rows)
@@ -102,73 +147,128 @@
     attention = (exponentials / totals).astype(BF16).reshape(Q_HEADS * rows, span)
     mixed = jnp.dot(attention, values, preferred_element_type=F32).astype(BF16)
     for h in range(Q_HEADS):
-        piece = mixed[h * rows : (h + 1) * rows]
-        for j in range(parts):
-            out_ref[j, :, h * HEAD_DIM : (h + 1) * HEAD_DIM] = piece
-
-
-def output_kernel(x_ref, mixed_ref, weight_ref, out_ref):
+        held_ref[:, h * HEAD_DIM : (h + 1) * HEAD_DIM] = mixed[h * rows : (h + 1) * rows]
+    for copy in copy_all([held_ref] * parts, [out_ref.at[j] for j in range(parts)], out_sems):
+        copy.wait()
+
+
+def output_kernel(tick, flags_ref, fresh_ref, arrived_ref, mixed_ref, weight_ref, *refs):
+    copies = []
+    out_ref = refs[0]
+    if len(refs) > 1:
+        top_ref, low_ref, out_ref, evicted_ref, sems = refs
+        middle = top_ref.shape[0]
+        copies = copy_all([top_ref, low_ref], [evicted_ref.at[:middle], evicted_ref.at[middle:]], sems)
+    current = tick_input(tick, flags_ref, arrived_ref, fresh_ref)
     product = jnp.dot(mixed_ref[...], weight_ref[...], preferred_element_type=F32)
-    out_ref[...] = (x_ref[...].astype(F32) + product).astype(BF16)
+    out_ref[...] = (current.astype(F32) + product).astype(BF16)
+    for copy in copies:
+        copy.wait()
 
 
 VMEM = pl.BlockSpec(memory_space=pltpu.VMEM)
 SMEM = pl.BlockSpec(memory_space=pltpu.SMEM)
+ANY = pl.BlockSpec(memory_space=pl.ANY)
+HBM = pl.BlockSpec(memory_space=pltpu.HBM)
 PARAMS = pltpu.CompilerParams(vmem_limit_bytes=24 * 1024 * 1024)
-
-
-def section_layer(current, gain, qkv_weight, out_weight, segments, place):
-    parts = lax.axis_size("tp")
-    tokens, width = current.shape
+ALONE = pltpu.CompilerParams(vmem_limit_bytes=60 * 1024 * 1024)
+WEIGHT_COPIES = 4
+
+
+def shard(shape):
+    return jax.ShapeDtypeStruct(shape, BF16)
+
+
+def exchange(value):
+    return lax.all_to_all(value, "tp", split_axis=0, concat_axis=0, tiled=True)
+
+
+def attend(place, segments, got, width, waited=()):
+    parts, rows, _ = got.shape
+    return pl.pallas_call(
+        functools.partial(attend_kernel, parts, width),
+        out_shape=shard((parts, rows, Q_COLS)),
+        in_specs=[SMEM, VMEM, VMEM] + [ANY] * len(waited),
+        out_specs=ANY,
+        scratch_shapes=[pltpu.VMEM((rows, Q_COLS), BF16), pltpu.SemaphoreType.DMA((parts,))],
+        compiler_params=PARAMS,
+        name="attend",
+    )(place, segments, got, *waited)
+
+
+def project(tick, stash, flags, fresh, gains, weight, arrived, parts):
+    tokens, width = arrived[0].shape
     rows = tokens // parts
     columns = Q_COLS + window_blocks(rows) * KV_COLS + 128
-    partial_proj = pl.pallas_call(
-        functools.partial(project_kernel, parts),
-        out_shape=jax.ShapeDtypeStruct((parts, rows, columns), BF16),
-        in_specs=[VMEM] * 3,
-        out_specs=VMEM,
-        compiler_params=PARAMS,
+    outs = [shard((parts, rows, columns))]
+    scratch = [pltpu.VMEM((parts, rows, columns), BF16), pltpu.SemaphoreType.DMA((parts,))]
+    if tick == 0:
+        scratch += [pltpu.VMEM((tokens, width), BF16), pltpu.VMEM(weight.shape, BF16)]
+        scratch += [pltpu.SemaphoreType.DMA((1 + WEIGHT_COPIES,))]
+    if stash:
+        outs += [shard((tokens // 2, width))] * 2
+        scratch += [pltpu.VMEM((tokens, width), BF16), pltpu.SemaphoreType.DMA((2,))]
+    space = HBM if tick == 0 else VMEM
+    return pl.pallas_call(
+        functools.partial(project_kernel, tick, stash),
+        out_shape=outs,
+        in_specs=[SMEM, ANY if tick == 0 else VMEM, VMEM, space] + [space] * len(arrived),
+        out_specs=[ANY] * len(outs),
+        scratch_shapes=scratch,
+        compiler_params=ALONE if tick == 0 else PARAMS,
         name="project",
-    )(current, gain, qkv_weight)
-    got = lax.all_to_all(partial_proj, "tp", split_axis=0, concat_axis=0, tiled=True)
-    mixed = pl.pallas_call(
-        functools.partial(attend_kernel, parts, width * parts),
-        out_shape=jax.ShapeDtypeStruct((parts, rows, Q_COLS), BF16),
-        in_specs=[SMEM, VMEM, VMEM],
-        out_specs=VMEM,
-        compiler_params=PARAMS,
-        name="attend",
-    )(place, segments, got)
-    mixed = lax.all_to_all(mixed, "tp", split_axis=0, concat_axis=0, tiled=True)
+    )(flags, fresh, gains, weight, *arrived)
+
+
+def project_out(tick, flags, fresh, arrived, mixed, weight, stash=()):
+    outs, out_specs, scratch = [shard(arrived.shape)], [VMEM], []
+    if stash:
+        outs.append(shard(arrived.shape))
+        out_specs.append(ANY)
+        scratch.append(pltpu.SemaphoreType.DMA((2,)))
     return pl.pallas_call(
-        output_kernel,
-        out_shape=jax.ShapeDtypeStruct((tokens, width), BF16),
-        in_specs=[VMEM] * 3,
-        out_specs=VMEM,
+        functools.partial(output_kernel, tick),
+        out_shape=outs,
+        in_specs=[SMEM, ANY if tick == 0 else VMEM] + [VMEM] * 3 + [ANY] * len(stash),
+        out_specs=out_specs,
+        scratch_shapes=scratch,
         compiler_params=PARAMS,
         name="project_out",
-    )(current, mixed.reshape(tokens, Q_COLS), out_weight)
+    )(flags, fresh, arrived, mixed.reshape(arrived.shape[0], Q_COLS), weight, *stash)
 
 
 def shards(carried, fresh, gains, qkv_weight, out_weight, segments, evict_tick):
     section = lax.axis_index("pipe")
     rank = lax.axis_index("tp")
     sections = lax.axis_size("pipe")
+    parts = lax.axis_size("tp")
     ticks = fresh.shape[0] + 1
-    current = carried[0]
-    chosen = current
-    result = current
+    width = carried.shape[2] * parts
+    qkv_weight, out_weight = qkv_weight[0], out_weight[0]
+    flags = jnp.stack([(section == 0).astype(jnp.int32), evict_tick[0]])
+    following = [(i, i + 1) for i in range(sections - 1)]
+    half = sections // 2
+    across = [(i, i + half) for i in range(half)]
+    turned = [(i, half - 1 - i) for i in range(half)]
+    turned_across = [(half + i, sections - 1 - i) for i in range(half)]
+    arrived = [carried[0]]
     for tick in range(ticks):
+        stash = tick == ticks - 1
         if tick > 0:
-            pairs = [(i, i + 1) for i in range(sections - 1)]
-            arrived = lax.ppermute(result, "pipe", pairs)
-            current = jnp.where(section == 0, fresh[tick - 1], arrived)
-            chosen = jnp.where(evict_tick[0] == tick, current, chosen)
+            arrived.append(lax.ppermute(result[0], "pipe", following))
+        sources = arrived if stash else arrived[-1:]
+        got = project(tick, stash, flags, fresh, gains, qkv_weight, sources, parts)
+        sums = exchange(got[0])
         place = jnp.stack([rank, section - tick + ticks - 1]).astype(jnp.int32)
-        result = section_layer(current, gains, qkv_weight[0], out_weight[0], segments, place)
-    pairs = [(i, sections - 1 - i) for i in range(sections // 2)]
-    evicted = lax.ppermute(chosen, "pipe", pairs)
-    return (result[None], evicted[None])
+        waited = ()
+        if stash:
+            waited = (lax.ppermute(got[1], "pipe", across), lax.ppermute(got[2], "pipe", turned))
+        mixed = exchange(attend(place, segments, sums, width, waited))
+        landed = ()
+        if stash:
+            landed = (lax.ppermute(waited[0], "pipe", turned_across), lax.ppermute(waited[1], "pipe", across))
+        result = project_out(tick, flags, fresh, arrived[-1], mixed, out_weight, landed)
+    return (result[0][None], result[1][None])
 
 
 def solution(mesh):

time: 201 us -> 202 us (level)
  the two profiles are of different devices: /device:TPU:231 before, /device:TPU:71 now
where the time goes in v5:
time: 202 us
  waiting for transfers between devices  78.5 us (39%)
  starting transfers between devices  51.1 us (25%)
  blocking collectives  38 us (19%)
  Pallas kernels  26.8 us (13%)
  local copies, waits for them, and re-layouts  4.74 us (2%)
    all_to_all x4, waiting for transfers between devices, exchange(): return lax.all_to_all(value, 'tp', split_axis=0, concat_axis=0, tiled=True)  44.7 us
    all_to_all x2, blocking collectives, exchange(): return lax.all_to_all(value, 'tp', split_axis=0, concat_axis=0, tiled=True)  38 us
    all_to_all x4, starting transfers between devices, exchange(): return lax.all_to_all(value, 'tp', split_axis=0, concat_axis=0, tiled=True)  27.1 us
    ppermute x1, waiting for transfers between devices, shards(): lax.ppermute(got[1], 'pipe', across)  21.5 us
    pallas_call x3, Pallas kernels, project(): pl.pallas_call(functools.partial(project_kernel, tick, stash), out_shape=...  12.4 us
    ppermute x2, starting transfers between devices, shards(): arrived.append(lax.ppermute(result[0], 'pipe', following))  11.9 us
    pallas_call x3, Pallas kernels, attend(): pl.pallas_call(functools.partial(attend_kernel, parts, width), out_shape=...  9.29 us
    ppermute x1, starting transfers between devices, shards(): lax.ppermute(waited[0], 'pipe', turned_across)  8.89 us
  transfers between devices with their start and end apart: 10, of which 6 were waited for; matrix products, arithmetic and copies ran while one was open for 0% of the time, Pallas kernels for 0%

profile of v5, /device:TPU:71, one launch (start us, length us, event | category | flops | bytes accessed | tf_op | source)
XLA Modules:
  0.0 201.6 jit_solution(8825294590725130815)
XLA Ops:
  1.3 0.6 pad_add_fusion.flags_ref
  1.9 4.5 %project.3 = bf16[8,32,3456]{2,1,0:T(8,128)(2,1)} custom-call(s32[2]{0:T(128)} %pad_add_fusion.flags_ref, bf16[2,256,512]{2,1,0:T(8,128)(2,1)} %fresh_ref.11, bf16[1,512]{1,0:T(2,128)(2,1)} %gain_ref.5, bf16[512,2304]{1,0:T(8,128)(2,1)} %bitcast.13, bf16[256,512]{1,0:T(8,128)(2,1)} %bitcast.21), custom_call_target="tpu_custom_call" | custom-call | tf_op jit(solution)/shard_map/project/pallas_call | solution.py:212
  6.4 0.0 copy-start.11
  6.4 7.0 %all-to-all-start = ((bf16[8,32,3456]{2,1,0:T(8,128)(2,1)}), bf16[8,32,3456]{2,1,0:T(8,128)(2,1)S(1)}, u32[]{:S(2)}, u32[]{:S(2)}) async-start(bf16[8,32,3456]{2,1,0:T(8,128)(2,1)} %project.3), calls=%async_computation | async-start | bytes 3538944 | tf_op jit(solution)/shard_map/all_to_all | solution.py:183
  13.4 0.1 pad_add_fusion.1.place_ref
  13.5 22.3 %all-to-all-done.got_ref = bf16[8,32,3456]{2,1,0:T(8,128)(2,1)S(1)} async-done(((bf16[8,32,3456]{2,1,0:T(8,128)(2,1)}), bf16[8,32,3456]{2,1,0:T(8,128)(2,1)S(1)}, u32[]{:S(2)}, u32[]{:S(2)}) %all-to-all-start) | async-done | bytes 1769504 | tf_op jit(solution)/shard_map/all_to_all | solution.py:183
  35.8 2.8 %attend.3 = bf16[8,32,2048]{2,1,0:T(8,128)(2,1)S(1)} custom-call(s32[2]{0:T(128)S(1)} %pad_add_fusion.1.place_ref, s32[66,256]{1,0:T(8,128)S(1)} %copy-done.11, bf16[8,32,3456]{2,1,0:T(8,128)(2,1)S(1)} %all-to-all-done.got_ref), custom_call_target="tpu_custom_call" | custom-call | tf_op jit(solution)/shard_map/attend/pallas_call | solution.py:188
  38.6 0.0 copy-start.1
  38.6 0.0 copy-start.7
  38.6 0.0 copy-start.13
  38.6 19.0 %all_to_all.30 = bf16[8,32,2048]{2,1,0:T(8,128)(2,1)S(1)} all-to-all(bf16[8,32,2048]{2,1,0:T(8,128)(2,1)S(1)} %attend.3), channel_id=1, replica_groups=mesh['pipe'=64,'tp'=8] {'tp'}, dimensions={0} | all-to-all | bytes 2097152 | tf_op jit(solution)/shard_map/all_to_all | solution.py:183
  57.6 0.0 copy-done.7
  57.6 0.0 copy-start
  57.6 0.0 copy-start.12
  57.7 1.2 project_out.3
  58.9 5.3 %collective-permute-start = (bf16[256,512]{1,0:T(8,128)(2,1)S(1)}, bf16[256,512]{1,0:T(8,128)(2,1)S(1)}, u32[]{:S(2)}, u32[]{:S(2)}) collective-permute-start(bf16[256,512]{1,0:T(8,128)(2,1)S(1)} %project_out.3), channel_id=1, source_target_pairs={{0,8},{8,16},{16,24},{24,32},{32,40},{40,48},{48,56},{56,64},{64,7... | collective-permute-start | bytes 786440 | tf_op jit(solution)/shard_map/ppermute | solution.py:258
  64.2 3.3 %collective-permute-done.refs_0_.arrived_ref.refs_1_ = bf16[256,512]{1,0:T(8,128)(2,1)S(1)} collective-permute-done((bf16[256,512]{1,0:T(8,128)(2,1)S(1)}, bf16[256,512]{1,0:T(8,128)(2,1)S(1)}, u32[]{:S(2)}, u32[]{:S(2)}) %collective-permute-start) | collective-permute-done | bytes 262176 | tf_op jit(solution)/shard_map/ppermute | solution.py:258
  67.5 3.7 %project.4 = bf16[8,32,3456]{2,1,0:T(8,128)(2,1)S(1)} custom-call(s32[2]{0:T(128)S(1)} %copy-done.13, bf16[2,256,512]{2,1,0:T(8,128)(2,1)S(1)} %copy-done.1, bf16[1,512]{1,0:T(2,128)(2,1)S(1)} %copy-done.12, bf16[512,2304]{1,0:T(8,128)(2,1)S(1)} %bitcast.14, bf16[256,512]{1,0:T(8,128)(2,1)S(1)} %collective-permute-done.refs_0_.arrived_ref.refs_1_), custom_call_target="tpu_custom_call" | custom-call | tf_op jit(solution)/shard_map/project/pallas_call | solution.py:212
  71.3 1.2 copy-done.5
  72.5 6.9 %all-to-all-start.2 = ((bf16[8,32,3456]{2,1,0:T(8,128)(2,1)}), bf16[8,32,3456]{2,1,0:T(8,128)(2,1)}, u32[]{:S(2)}, u32[]{:S(2)}) async-start(bf16[8,32,3456]{2,1,0:T(8,128)(2,1)} %copy-done.5), calls=%async_computation.2 | async-start | bytes 3538944 | tf_op jit(solution)/shard_map/all_to_all | solution.py:183
  79.4 0.1 pad_add_fusion.2.place_ref
  79.5 22.4 %all-to-all-done.2.got_ref = bf16[8,32,3456]{2,1,0:T(8,128)(2,1)} async-done(((bf16[8,32,3456]{2,1,0:T(8,128)(2,1)}), bf16[8,32,3456]{2,1,0:T(8,128)(2,1)}, u32[]{:S(2)}, u32[]{:S(2)}) %all-to-all-start.2) | async-done | bytes 1769504 | tf_op jit(solution)/shard_map/all_to_all | solution.py:183
  101.9 3.7 %attend.4 = bf16[8,32,2048]{2,1,0:T(8,128)(2,1)S(1)} custom-call(s32[2]{0:T(128)S(1)} %pad_add_fusion.2.place_ref, s32[66,256]{1,0:T(8,128)S(1)} %copy-done.11, bf16[8,32,3456]{2,1,0:T(8,128)(2,1)} %all-to-all-done.2.got_ref), custom_call_target="tpu_custom_call" | custom-call | tf_op jit(solution)/shard_map/attend/pallas_call | solution.py:188
  105.6 0.0 copy-start.3
  105.6 19.0 %all_to_all.31 = bf16[8,32,2048]{2,1,0:T(8,128)(2,1)S(1)} all-to-all(bf16[8,32,2048]{2,1,0:T(8,128)(2,1)S(1)} %attend.4), channel_id=1, replica_groups=mesh['pipe'=64,'tp'=8] {'tp'}, dimensions={0} | all-to-all | bytes 2097152 | tf_op jit(solution)/shard_map/all_to_all | solution.py:183
  124.6 1.2 project_out.4
  125.8 6.6 %collective-permute-start.1 = (bf16[256,512]{1,0:T(8,128)(2,1)S(1)}, bf16[256,512]{1,0:T(8,128)(2,1)S(1)}, u32[]{:S(2)}, u32[]{:S(2)}) collective-permute-start(bf16[256,512]{1,0:T(8,128)(2,1)S(1)} %project_out.4), channel_id=1, source_target_pairs={{0,8},{8,16},{16,24},{24,32},{32,40},{40,48},{48,56},{56,64},{64,7... | collective-permute-start | bytes 786440 | tf_op jit(solution)/shard_map/ppermute | solution.py:258
  132.5 3.3 %collective-permute-done.1.refs_2_.arrived_ref = bf16[256,512]{1,0:T(8,128)(2,1)S(1)} collective-permute-done((bf16[256,512]{1,0:T(8,128)(2,1)S(1)}, bf16[256,512]{1,0:T(8,128)(2,1)S(1)}, u32[]{:S(2)}, u32[]{:S(2)}) %collective-permute-start.1) | collective-permute-done | bytes 262176 | tf_op jit(solution)/shard_map/ppermute | solution.py:258
  135.8 4.2 %project.5 = (bf16[8,32,3456]{2,1,0:T(8,128)(2,1)S(1)}, bf16[128,512]{1,0:T(8,128)(2,1)S(1)}, bf16[128,512]{1,0:T(8,128)(2,1)S(1)}) custom-call(s32[2]{0:T(128)S(1)} %copy-done.13, bf16[2,256,512]{2,1,0:T(8,128)(2,1)S(1)} %copy-done.1, bf16[1,512]{1,0:T(2,128)(2,1)S(1)} %copy-done.12, bf16[512,2304]{1,0:T(8,128)(2,1)S(1)} %bitcast.15, ...), custom_call_target="tpu_custom_call" | custom-call | tf_op jit(solution)/shard_map/project/pallas_call | solution.py:212
  139.9 1.2 copy-done.8
  141.2 0.6 copy-done.14
  141.8 0.7 copy-done.16
  142.5 6.3 %all-to-all-start.4 = ((bf16[8,32,3456]{2,1,0:T(8,128)(2,1)}), bf16[8,32,3456]{2,1,0:T(8,128)(2,1)S(1)}, u32[]{:S(2)}, u32[]{:S(2)}) async-start(bf16[8,32,3456]{2,1,0:T(8,128)(2,1)} %copy-done.8), calls=%async_computation.4 | async-start | bytes 3538944 | tf_op jit(solution)/shard_map/all_to_all | solution.py:183
  148.8 1.3 collective-permute-start.2
  150.1 0.7 collective-permute-start.3
  150.7 0.1 pad_add_fusion.3.place_ref
  150.8 21.5 %collective-permute-done.2.refs_0_ = bf16[128,512]{1,0:T(8,128)(2,1)S(1)} collective-permute-done((bf16[128,512]{1,0:T(8,128)(2,1)S(1)}, bf16[128,512]{1,0:T(8,128)(2,1)S(1)}, u32[]{:S(2)}, u32[]{:S(2)}) %collective-permute-start.2) | collective-permute-done | bytes 131104 | tf_op jit(solution)/shard_map/ppermute | solution.py:265
  172.3 0.0 collective-permute-done.3.refs_1_
  172.3 0.0 all-to-all-done.4.got_ref
  172.3 2.8 %attend.5 = bf16[8,32,2048]{2,1,0:T(8,128)(2,1)S(1)} custom-call(s32[2]{0:T(128)S(1)} %pad_add_fusion.3.place_ref, s32[66,256]{1,0:T(8,128)S(1)} %copy-done.11, bf16[8,32,3456]{2,1,0:T(8,128)(2,1)S(1)} %all-to-all-done.4.got_ref, bf16[128,512]{1,0:T(8,128)(2,1)S(1)} %collective-permute-done.2.refs_0_, bf16[128,512]{1,0:T(8,128)(2,1)S(1)} %collective-permute-done.3.refs_1_), custom_call_target="tpu_custom_call" | custom-call | tf_op jit(solution)/shard_map/attend/pallas_call | solution.py:188
  175.1 1.0 copy-done.6
  176.1 6.8 %all-to-all-start.5 = ((bf16[8,32,2048]{2,1,0:T(8,128)(2,1)}), bf16[8,32,2048]{2,1,0:T(8,128)(2,1)}, u32[]{:S(2)}, u32[]{:S(2)}) async-start(bf16[8,32,2048]{2,1,0:T(8,128)(2,1)} %copy-done.6), calls=%async_computation.5 | async-start | bytes 2097152 | tf_op jit(solution)/shard_map/all_to_all | solution.py:183
  182.9 8.9 %collective-permute-start.4 = (bf16[128,512]{1,0:T(8,128)(2,1)S(1)}, bf16[128,512]{1,0:T(8,128)(2,1)S(1)}, u32[]{:S(2)}, u32[]{:S(2)}) collective-permute-start(bf16[128,512]{1,0:T(8,128)(2,1)S(1)} %collective-permute-done.2.refs_0_), channel_id=1, source_target_pairs={{256,504},{264,496},{272,488},{280,480},{288,472},{296,464},{304,4... | collective-permute-start | bytes 393224 | tf_op jit(solution)/shard_map/ppermute | solution.py:269
  191.8 1.3 collective-permute-start.5
  193.1 5.7 %collective-permute-done.4.refs_0_ = bf16[128,512]{1,0:T(8,128)(2,1)S(1)} collective-permute-done((bf16[128,512]{1,0:T(8,128)(2,1)S(1)}, bf16[128,512]{1,0:T(8,128)(2,1)S(1)}, u32[]{:S(2)}, u32[]{:S(2)}) %collective-permute-start.4) | collective-permute-done | bytes 131104 | tf_op jit(solution)/shard_map/ppermute | solution.py:269
  198.9 0.0 collective-permute-done.5.refs_1_
  198.9 0.0 all-to-all-done.5
  198.9 2.7 %project_out.5 = (bf16[256,512]{1,0:T(8,128)(2,1)}, bf16[256,512]{1,0:T(8,128)(2,1)}) custom-call(s32[2]{0:T(128)S(1)} %copy-done.13, bf16[2,256,512]{2,1,0:T(8,128)(2,1)S(1)} %copy-done.1, bf16[256,512]{1,0:T(8,128)(2,1)S(1)} %copy-done.10, bf16[256,2048]{1,0:T(8,128)(2,1)} %bitcast.10.mixed_ref, bf16[2048,512]{1,0:T(8,128)(2,1)S(1)} %bitcast.18, ...), custom_call_target="tpu_custom_call" | custom-call | tf_op jit(solution)/shard_map/project_out/pallas_call | solution.py:229
  (23 shorter events, 0.0 us)
Async XLA Ops:
  6.4 29.4 %copy-start.11 = (s32[66,256]{1,0:T(8,128)S(1)}, s32[66,256]{1,0:T(8,128)}, u32[]{:S(2)}) copy-start(s32[66,256]{1,0:T(8,128)} %segments_ref.5) | copy-start | bytes 202756
  6.4 29.4 %all-to-all-start = ((bf16[8,32,3456]{2,1,0:T(8,128)(2,1)}), bf16[8,32,3456]{2,1,0:T(8,128)(2,1)S(1)}, u32[]{:S(2)}, u32[]{:S(2)}) async-start(bf16[8,32,3456]{2,1,0:T(8,128)(2,1)} %project.3), calls=%async_computation | async-start | bytes 3538944 | tf_op jit(solution)/shard_map/all_to_all | solution.py:183
  35.8 21.8 %copy-start.2 = (bf16[1,2048,512]{2,1,0:T(8,128)(2,1)S(1)}, bf16[1,2048,512]{2,1,0:T(8,128)(2,1)}, u32[]{:S(2)}) copy-start(bf16[1,2048,512]{2,1,0:T(8,128)(2,1)} %param.11) | copy-start | bytes 6291460
  38.6 19.1 %copy-start.1 = (bf16[2,256,512]{2,1,0:T(8,128)(2,1)S(1)}, bf16[2,256,512]{2,1,0:T(8,128)(2,1)}, u32[]{:S(2)}) copy-start(bf16[2,256,512]{2,1,0:T(8,128)(2,1)} %fresh_ref.11) | copy-start | bytes 1572868
  38.6 19.1 %copy-start.7 = (bf16[1,256,512]{2,1,0:T(8,128)(2,1)S(1)}, bf16[1,256,512]{2,1,0:T(8,128)(2,1)}, u32[]{:S(2)}) copy-start(bf16[1,256,512]{2,1,0:T(8,128)(2,1)} %param.7) | copy-start | bytes 786436
  38.6 19.0 %copy-start.13 = (s32[2]{0:T(128)S(1)}, s32[2]{0:T(128)}, u32[]{:S(2)}) copy-start(s32[2]{0:T(128)} %pad_add_fusion.flags_ref) | copy-start | bytes 28
  57.6 9.9 %copy-start = (bf16[1,512,2304]{2,1,0:T(8,128)(2,1)S(1)}, bf16[1,512,2304]{2,1,0:T(8,128)(2,1)}, u32[]{:S(2)}) copy-start(bf16[1,512,2304]{2,1,0:T(8,128)(2,1)} %param.10) | copy-start | bytes 7077892
  57.6 9.9 %copy-start.12 = (bf16[1,512]{1,0:T(2,128)(2,1)S(1)}, bf16[1,512]{1,0:T(2,128)(2,1)}, u32[]{:S(2)}) copy-start(bf16[1,512]{1,0:T(2,128)(2,1)} %gain_ref.5) | copy-start | bytes 3076
  58.9 8.6 %collective-permute-start = (bf16[256,512]{1,0:T(8,128)(2,1)S(1)}, bf16[256,512]{1,0:T(8,128)(2,1)S(1)}, u32[]{:S(2)}, u32[]{:S(2)}) collective-permute-start(bf16[256,512]{1,0:T(8,128)(2,1)S(1)} %project_out.3), channel_id=1, source_target_pairs={{0,8},{8,16},{16,24},{24,32},{32,40},{40,48},{48,56},{56,64},{64,7... | collective-permute-start | bytes 786440 | tf_op jit(solution)/shard_map/ppermute | solution.py:258
  71.3 1.2 copy-start.5
  72.5 29.4 %all-to-all-start.2 = ((bf16[8,32,3456]{2,1,0:T(8,128)(2,1)}), bf16[8,32,3456]{2,1,0:T(8,128)(2,1)}, u32[]{:S(2)}, u32[]{:S(2)}) async-start(bf16[8,32,3456]{2,1,0:T(8,128)(2,1)} %copy-done.5), calls=%async_computation.2 | async-start | bytes 3538944 | tf_op jit(solution)/shard_map/all_to_all | solution.py:183
  105.6 19.0 %copy-start.3 = (bf16[1,2048,512]{2,1,0:T(8,128)(2,1)S(1)}, bf16[1,2048,512]{2,1,0:T(8,128)(2,1)}, u32[]{:S(2)}) copy-start(bf16[1,2048,512]{2,1,0:T(8,128)(2,1)} %param.11) | copy-start | bytes 6291460
  125.8 9.9 %collective-permute-start.1 = (bf16[256,512]{1,0:T(8,128)(2,1)S(1)}, bf16[256,512]{1,0:T(8,128)(2,1)S(1)}, u32[]{:S(2)}, u32[]{:S(2)}) collective-permute-start(bf16[256,512]{1,0:T(8,128)(2,1)S(1)} %project_out.4), channel_id=1, source_target_pairs={{0,8},{8,16},{16,24},{24,32},{32,40},{40,48},{48,56},{56,64},{64,7... | collective-permute-start | bytes 786440 | tf_op jit(solution)/shard_map/ppermute | solution.py:258
  135.8 4.2 %copy-start.9 = (bf16[256,512]{1,0:T(8,128)(2,1)}, bf16[256,512]{1,0:T(8,128)(2,1)S(1)}, u32[]{:S(2)}) copy-start(bf16[256,512]{1,0:T(8,128)(2,1)S(1)} %collective-permute-done.1.refs_2_.arrived_ref) | copy-start | bytes 786436
  139.9 1.2 copy-start.8
  141.2 0.6 copy-start.14
  141.8 0.7 copy-start.16
  142.5 6.3 %copy-start.17 = (bf16[128,512]{1,0:T(8,128)(2,1)S(1)}, bf16[128,512]{1,0:T(8,128)(2,1)}, u32[]{:S(2)}) copy-start(bf16[128,512]{1,0:T(8,128)(2,1)} %copy-done.16) | copy-start | bytes 393220
  142.5 7.6 %copy-start.15 = (bf16[128,512]{1,0:T(8,128)(2,1)S(1)}, bf16[128,512]{1,0:T(8,128)(2,1)}, u32[]{:S(2)}) copy-start(bf16[128,512]{1,0:T(8,128)(2,1)} %copy-done.14) | copy-start | bytes 393220
  142.5 29.9 %all-to-all-start.4 = ((bf16[8,32,3456]{2,1,0:T(8,128)(2,1)}), bf16[8,32,3456]{2,1,0:T(8,128)(2,1)S(1)}, u32[]{:S(2)}, u32[]{:S(2)}) async-start(bf16[8,32,3456]{2,1,0:T(8,128)(2,1)} %copy-done.8), calls=%async_computation.4 | async-start | bytes 3538944 | tf_op jit(solution)/shard_map/all_to_all | solution.py:183
  148.8 23.6 %collective-permute-start.2 = (bf16[128,512]{1,0:T(8,128)(2,1)S(1)}, bf16[128,512]{1,0:T(8,128)(2,1)S(1)}, u32[]{:S(2)}, u32[]{:S(2)}) collective-permute-start(bf16[128,512]{1,0:T(8,128)(2,1)S(1)} %copy-done.17), channel_id=1, source_target_pairs={{0,256},{8,264},{16,272},{24,280},{32,288},{40,296},{48,304},{56,3... | collective-permute-start | bytes 393224 | tf_op jit(solution)/shard_map/ppermute | solution.py:265
  150.1 22.3 %collective-permute-start.3 = (bf16[128,512]{1,0:T(8,128)(2,1)S(1)}, bf16[128,512]{1,0:T(8,128)(2,1)S(1)}, u32[]{:S(2)}, u32[]{:S(2)}) collective-permute-start(bf16[128,512]{1,0:T(8,128)(2,1)S(1)} %copy-done.15), channel_id=1, source_target_pairs={{0,248},{8,240},{16,232},{24,224},{32,216},{40,208},{48,200},{56,1... | collective-permute-start | bytes 393224 | tf_op jit(solution)/shard_map/ppermute | solution.py:265
  172.3 26.6 %copy-start.10 = (bf16[256,512]{1,0:T(8,128)(2,1)S(1)}, bf16[256,512]{1,0:T(8,128)(2,1)}, u32[]{:S(2)}) copy-start(bf16[256,512]{1,0:T(8,128)(2,1)} %copy-done.9) | copy-start | bytes 786436
  175.1 1.0 copy-start.6
  176.1 22.8 %copy-start.4 = (bf16[1,2048,512]{2,1,0:T(8,128)(2,1)S(1)}, bf16[1,2048,512]{2,1,0:T(8,128)(2,1)}, u32[]{:S(2)}) copy-start(bf16[1,2048,512]{2,1,0:T(8,128)(2,1)} %param.11) | copy-start | bytes 6291460
  176.1 22.8 %all-to-all-start.5 = ((bf16[8,32,2048]{2,1,0:T(8,128)(2,1)}), bf16[8,32,2048]{2,1,0:T(8,128)(2,1)}, u32[]{:S(2)}, u32[]{:S(2)}) async-start(bf16[8,32,2048]{2,1,0:T(8,128)(2,1)} %copy-done.6), calls=%async_computation.5 | async-start | bytes 2097152 | tf_op jit(solution)/shard_map/all_to_all | solution.py:183
  182.9 15.9 %collective-permute-start.4 = (bf16[128,512]{1,0:T(8,128)(2,1)S(1)}, bf16[128,512]{1,0:T(8,128)(2,1)S(1)}, u32[]{:S(2)}, u32[]{:S(2)}) collective-permute-start(bf16[128,512]{1,0:T(8,128)(2,1)S(1)} %collective-permute-done.2.refs_0_), channel_id=1, source_target_pairs={{256,504},{264,496},{272,488},{280,480},{288,472},{296,464},{304,4... | collective-permute-start | bytes 393224 | tf_op jit(solution)/shard_map/ppermute | solution.py:269
  191.8 7.0 %collective-permute-start.5 = (bf16[128,512]{1,0:T(8,128)(2,1)S(1)}, bf16[128,512]{1,0:T(8,128)(2,1)S(1)}, u32[]{:S(2)}, u32[]{:S(2)}) collective-permute-start(bf16[128,512]{1,0:T(8,128)(2,1)S(1)} %collective-permute-done.3.refs_1_), channel_id=1, source_target_pairs={{0,256},{8,264},{16,272},{24,280},{32,288},{40,296},{48,304},{56,3... | collective-permute-start | bytes 393224 | tf_op jit(solution)/shard_map/ppermute | solution.py:269

commit v6 on v2

--- a/solution.py
+++ b/solution.py
@@ -45,11 +45,14 @@
         out_ref[j, :, last:] = sums.astype(BF16)
 
 
+FIRST, EVICT, RANK, SECTION = range(4)
+
+
 def project_kernel(parts, tick, stash, flags_ref, *refs):
     earlier, refs = (refs[:tick], refs[tick:]) if stash else ((), refs)
     if tick > 0:
         arrived_ref, fresh_ref, gain_ref, weight_ref, out_ref, current_ref = refs[:6]
-        current = jnp.where(flags_ref[0] == 1, fresh_ref[tick - 1], arrived_ref[...])
+        current = jnp.where(flags_ref[FIRST] == 1, fresh_ref[tick - 1], arrived_ref[...])
         current_ref[...] = current
     else:
         arrived_ref, gain_ref, weight_ref, out_ref = refs
@@ -57,7 +60,7 @@
     if earlier:
         chosen = current
         for at, earlier_ref in enumerate(earlier):
-            chosen = jnp.where(flags_ref[1] == at, earlier_ref[...], chosen)
+            chosen = jnp.where(flags_ref[EVICT] == at, earlier_ref[...], chosen)
         half = chosen.shape[0] // 2
         refs[6][...] = chosen[:half]
         refs[7][...] = chosen[half:]
@@ -66,15 +69,15 @@
     project_rows(parts, wide, scaled, weight_ref, out_ref)
 
 
-def attend_kernel(parts, width, place_ref, segments_ref, got_ref, *refs):
+def attend_kernel(parts, width, back, flags_ref, segments_ref, got_ref, *refs):
     out_ref = refs[-1]
     rows = got_ref.shape[1]
     tokens = rows * parts
     blocks = window_blocks(rows)
     span = blocks * rows
     before = span - rows
-    rank = place_ref[0]
-    item = place_ref[1]
+    rank = flags_ref[RANK]
+    item = flags_ref[SECTION] + back
 
     def total(start, size):
         value = got_ref[0, :, start : start + size].astype(F32)
@@ -145,16 +148,16 @@
     return lax.all_to_all(value, "tp", split_axis=0, concat_axis=0, tiled=True)
 
 
-def attend(place, segments, got, width, waited=()):
+def attend(flags, segments, got, width, back, waited=()):
     parts, rows, _ = got.shape
     return pl.pallas_call(
-        functools.partial(attend_kernel, parts, width),
+        functools.partial(attend_kernel, parts, width, back),
         out_shape=shard((parts, rows, Q_COLS)),
         in_specs=[SMEM, VMEM, VMEM] + [ANY] * len(waited),
         out_specs=VMEM,
         compiler_params=PARAMS,
         name="attend",
-    )(place, segments, got, *waited)
+    )(flags, segments, got, *waited)
 
 
 def project_out(current, mixed, out_weight):
@@ -177,7 +180,7 @@
     tokens, width = carried.shape[1:]
     rows = tokens // parts
     columns = Q_COLS + window_blocks(rows) * KV_COLS + 128
-    flags = jnp.stack([(section == 0).astype(jnp.int32), evict_tick[0]])
+    flags = jnp.stack([(section == 0).astype(jnp.int32), evict_tick[0], rank, section])
     following = [(i, i + 1) for i in range(sections - 1)]
     half = sections // 2
     across = [(i, i + half) for i in range(half)]
@@ -209,11 +212,10 @@
         if tick > 0:
             inputs.append(got[1])
         sums = exchange(partial_proj)
-        place = jnp.stack([rank, section - tick + ticks - 1]).astype(jnp.int32)
         waited = ()
         if tick == ticks - 1:
             waited = (lax.ppermute(got[2], "pipe", across), lax.ppermute(got[3], "pipe", turned))
-        mixed = exchange(attend(place, segments, sums, width * parts, waited))
+        mixed = exchange(attend(flags, segments, sums, width * parts, ticks - 1 - tick, waited))
         result = project_out(inputs[tick], mixed, out_weight[0])
     top = lax.ppermute(waited[0], "pipe", turned_across)
     low = lax.ppermute(waited[1], "pipe", across)

time: 194 us -> 183 us (0.943)
  the two profiles are of different devices: /device:TPU:71 before, /device:TPU:199 now
where the time goes in v6:
time: 183 us
  blocking collectives  89.2 us (49%)
  waiting for transfers between devices  37.1 us (20%)
  starting transfers between devices  36.4 us (20%)
  Pallas kernels  12 us (7%)
  local copies, waits for them, and re-layouts  5.54 us (3%)
    all_to_all x4, blocking collectives, exchange(): return lax.all_to_all(value, 'tp', split_axis=0, concat_axis=0, tiled=True)  89.2 us
    ppermute x1, waiting for transfers between devices, shards(): lax.ppermute(got[2], 'pipe', across)  20.3 us
    ppermute x2, starting transfers between devices, shards(): arrived = lax.ppermute(result, 'pipe', following)  16.1 us
    all_to_all x2, starting transfers between devices, exchange(): return lax.all_to_all(value, 'tp', split_axis=0, concat_axis=0, tiled=True)  13.6 us
    ppermute x1, waiting for transfers between devices, shards(): top = lax.ppermute(waited[0], 'pipe', turned_across)  9.35 us
    ppermute x2, waiting for transfers between devices, shards(): arrived = lax.ppermute(result, 'pipe', following)  6.59 us
    unnamed x24, local copies, waits for them, and re-layouts  5.54 us
    pallas_call x3, Pallas kernels, attend(): pl.pallas_call(functools.partial(attend_kernel, parts, width, back), out_...  5.24 us
  transfers between devices with their start and end apart: 8, of which 5 were waited for; matrix products, arithmetic and copies ran while one was open for 0% of the time, Pallas kernels for 0%

profile of v6, /device:TPU:199, one launch (start us, length us, event | category | flops | bytes accessed | tf_op | source)
XLA Modules:
  0.0 182.6 jit_solution(13447852263076566349)
XLA Ops:
  1.3 0.1 pad_add_fusion.flags_ref
  1.4 1.7 copy-done
  3.0 0.9 copy-done.4
  4.0 0.7 copy-done.10
  4.7 1.3 project.3
  6.0 0.0 copy-start.8
  6.0 28.4 %all_to_all.30.got_ref = bf16[8,32,3456]{2,1,0:T(8,128)(2,1)S(1)} all-to-all(bf16[8,32,3456]{2,1,0:T(8,128)(2,1)S(1)} %project.3), channel_id=1, replica_groups=mesh['pipe'=64,'tp'=8] {'tp'}, dimensions={0} | all-to-all | bytes 3538944 | tf_op jit(solution)/shard_map/all_to_all | solution.py:148
  34.4 0.0 copy-done.8
  34.4 1.4 attend.3
  35.8 0.0 copy-start.2
  35.8 17.2 %all_to_all.31 = bf16[8,32,2048]{2,1,0:T(8,128)(2,1)S(1)} all-to-all(bf16[8,32,2048]{2,1,0:T(8,128)(2,1)S(1)} %attend.3), channel_id=1, replica_groups=mesh['pipe'=64,'tp'=8] {'tp'}, dimensions={0} | all-to-all | bytes 2097152 | tf_op jit(solution)/shard_map/all_to_all | solution.py:148
  53.0 0.0 copy-done.5
  53.0 0.0 copy-done.2
  53.1 0.0 copy-start.11
  53.1 0.7 project_out.3
  53.8 6.8 %collective-permute-start = (bf16[256,512]{1,0:T(8,128)(2,1)S(1)}, bf16[256,512]{1,0:T(8,128)(2,1)S(1)}, u32[]{:S(2)}, u32[]{:S(2)}) collective-permute-start(bf16[256,512]{1,0:T(8,128)(2,1)S(1)} %project_out.3), channel_id=1, source_target_pairs={{0,8},{8,16},{16,24},{24,32},{32,40},{40,48},{48,56},{56,64},{64,7... | collective-permute-start | bytes 786440 | tf_op jit(solution)/shard_map/ppermute | solution.py:195
  60.6 3.3 %collective-permute-done.refs_0_ = bf16[256,512]{1,0:T(8,128)(2,1)S(1)} collective-permute-done((bf16[256,512]{1,0:T(8,128)(2,1)S(1)}, bf16[256,512]{1,0:T(8,128)(2,1)S(1)}, u32[]{:S(2)}, u32[]{:S(2)}) %collective-permute-start) | collective-permute-done | bytes 262176 | tf_op jit(solution)/shard_map/ppermute | solution.py:195
  63.9 0.0 copy-done.1
  63.9 0.0 copy-done.6
  63.9 0.0 copy-done.11
  63.9 1.3 project.4
  65.2 25.7 %all_to_all.32.got_ref = bf16[8,32,3456]{2,1,0:T(8,128)(2,1)S(1)} all-to-all(bf16[8,32,3456]{2,1,0:T(8,128)(2,1)S(1)} %get-tuple-element.9), channel_id=1, replica_groups=mesh['pipe'=64,'tp'=8] {'tp'}, dimensions={0} | all-to-all | bytes 3538944 | tf_op jit(solution)/shard_map/all_to_all | solution.py:148
  91.0 1.4 attend.4
  92.4 17.9 %all_to_all.33 = bf16[8,32,2048]{2,1,0:T(8,128)(2,1)S(1)} all-to-all(bf16[8,32,2048]{2,1,0:T(8,128)(2,1)S(1)} %attend.4), channel_id=1, replica_groups=mesh['pipe'=64,'tp'=8] {'tp'}, dimensions={0} | all-to-all | bytes 2097152 | tf_op jit(solution)/shard_map/all_to_all | solution.py:148
  110.3 0.7 project_out.4
  111.0 9.3 %collective-permute-start.1 = (bf16[256,512]{1,0:T(8,128)(2,1)S(1)}, bf16[256,512]{1,0:T(8,128)(2,1)S(1)}, u32[]{:S(2)}, u32[]{:S(2)}) collective-permute-start(bf16[256,512]{1,0:T(8,128)(2,1)S(1)} %project_out.4), channel_id=1, source_target_pairs={{0,8},{8,16},{16,24},{24,32},{32,40},{40,48},{48,56},{56,64},{64,7... | collective-permute-start | bytes 786440 | tf_op jit(solution)/shard_map/ppermute | solution.py:195
  120.3 3.3 %collective-permute-done.1.refs_2_ = bf16[256,512]{1,0:T(8,128)(2,1)S(1)} collective-permute-done((bf16[256,512]{1,0:T(8,128)(2,1)S(1)}, bf16[256,512]{1,0:T(8,128)(2,1)S(1)}, u32[]{:S(2)}, u32[]{:S(2)}) %collective-permute-start.1) | collective-permute-done | bytes 262176 | tf_op jit(solution)/shard_map/ppermute | solution.py:195
  123.6 1.3 project.5
  124.9 0.0 copy-start.7
  124.9 1.2 copy-done.7
  126.1 6.9 %all-to-all-start.4 = ((bf16[8,32,3456]{2,1,0:T(8,128)(2,1)}), bf16[8,32,3456]{2,1,0:T(8,128)(2,1)}, u32[]{:S(2)}, u32[]{:S(2)}) async-start(bf16[8,32,3456]{2,1,0:T(8,128)(2,1)} %copy-done.7), calls=%async_computation.4 | async-start | bytes 3538944 | tf_op jit(solution)/shard_map/all_to_all | solution.py:148
  133.1 1.3 collective-permute-start.2
  134.4 0.7 collective-permute-start.3
  135.0 20.3 %collective-permute-done.2.refs_0_ = bf16[128,512]{1,0:T(8,128)(2,1)S(1)} collective-permute-done((bf16[128,512]{1,0:T(8,128)(2,1)S(1)}, bf16[128,512]{1,0:T(8,128)(2,1)S(1)}, u32[]{:S(2)}, u32[]{:S(2)}) %collective-permute-start.2) | collective-permute-done | bytes 131104 | tf_op jit(solution)/shard_map/ppermute | solution.py:217
  155.3 0.0 collective-permute-done.3.refs_1_
  155.3 0.0 all-to-all-done.4.got_ref
  155.3 2.4 %attend.5 = bf16[8,32,2048]{2,1,0:T(8,128)(2,1)S(1)} custom-call(s32[4]{0:T(128)S(1)} %pad_add_fusion.flags_ref, s32[66,256]{1,0:T(8,128)S(1)} %copy-done.8, bf16[8,32,3456]{2,1,0:T(8,128)(2,1)} %all-to-all-done.4.got_ref, bf16[128,512]{1,0:T(8,128)(2,1)S(1)} %collective-permute-done.2.refs_0_, bf16[128,512]{1,0:T(8,128)(2,1)S(1)} %collective-permute-done.3.refs_1_), custom_call_target="tpu_custom_call" | custom-call | tf_op jit(solution)/shard_map/attend/pallas_call | solution.py:153
  157.7 0.0 copy-start.3
  157.7 1.0 copy-done.3
  158.7 0.0 copy-done.9
  158.7 6.7 %all-to-all-start.5 = ((bf16[8,32,2048]{2,1,0:T(8,128)(2,1)}), bf16[8,32,2048]{2,1,0:T(8,128)(2,1)S(1)}, u32[]{:S(2)}, u32[]{:S(2)}) async-start(bf16[8,32,2048]{2,1,0:T(8,128)(2,1)} %copy-done.3), calls=%async_computation.5 | async-start | bytes 2097152 | tf_op jit(solution)/shard_map/all_to_all | solution.py:148
  165.4 3.5 %collective-permute-start.4 = (bf16[128,512]{1,0:T(8,128)(2,1)S(1)}, bf16[128,512]{1,0:T(8,128)(2,1)S(1)}, u32[]{:S(2)}, u32[]{:S(2)}) collective-permute-start(bf16[128,512]{1,0:T(8,128)(2,1)S(1)} %collective-permute-done.2.refs_0_), channel_id=1, source_target_pairs={{256,504},{264,496},{272,488},{280,480},{288,472},{296,464},{304,4... | collective-permute-start | bytes 393224 | tf_op jit(solution)/shard_map/ppermute | solution.py:220
  168.9 1.3 collective-permute-start.5
  170.2 9.4 %collective-permute-done.4 = bf16[128,512]{1,0:T(8,128)(2,1)S(1)} collective-permute-done((bf16[128,512]{1,0:T(8,128)(2,1)S(1)}, bf16[128,512]{1,0:T(8,128)(2,1)S(1)}, u32[]{:S(2)}, u32[]{:S(2)}) %collective-permute-start.4) | collective-permute-done | bytes 131104 | tf_op jit(solution)/shard_map/ppermute | solution.py:220
  179.5 0.9 collective-permute-done.5
  180.4 0.7 maximum_bitcast_fusion
  181.1 0.0 all-to-all-done.5
  181.1 1.4 project_out.5
  (7 shorter events, 0.0 us)
Async XLA Ops:
  1.4 1.7 copy-start
  3.0 0.9 copy-start.4
  4.0 0.7 copy-start.10
  6.0 28.4 %copy-start.8 = (s32[66,256]{1,0:T(8,128)S(1)}, s32[66,256]{1,0:T(8,128)}, u32[]{:S(2)}) copy-start(s32[66,256]{1,0:T(8,128)} %segments_ref.5) | copy-start | bytes 202756
  34.4 18.7 %copy-start.5 = (bf16[1,256,512]{2,1,0:T(8,128)(2,1)S(1)}, bf16[1,256,512]{2,1,0:T(8,128)(2,1)}, u32[]{:S(2)}) copy-start(bf16[1,256,512]{2,1,0:T(8,128)(2,1)} %param.7) | copy-start | bytes 786436
  35.8 17.3 %copy-start.2 = (bf16[1,2048,512]{2,1,0:T(8,128)(2,1)S(1)}, bf16[1,2048,512]{2,1,0:T(8,128)(2,1)}, u32[]{:S(2)}) copy-start(bf16[1,2048,512]{2,1,0:T(8,128)(2,1)} %param.11) | copy-start | bytes 6291460
  53.0 10.9 %copy-start.1 = (bf16[1,512,2304]{2,1,0:T(8,128)(2,1)S(1)}, bf16[1,512,2304]{2,1,0:T(8,128)(2,1)}, u32[]{:S(2)}) copy-start(bf16[1,512,2304]{2,1,0:T(8,128)(2,1)} %param.10) | copy-start | bytes 7077892
  53.0 10.9 %copy-start.6 = (bf16[2,256,512]{2,1,0:T(8,128)(2,1)S(1)}, bf16[2,256,512]{2,1,0:T(8,128)(2,1)}, u32[]{:S(2)}) copy-start(bf16[2,256,512]{2,1,0:T(8,128)(2,1)} %refs_3_.1) | copy-start | bytes 1572868
  53.1 10.9 %copy-start.11 = (bf16[1,512]{1,0:T(2,128)(2,1)S(1)}, bf16[1,512]{1,0:T(2,128)(2,1)}, u32[]{:S(2)}) copy-start(bf16[1,512]{1,0:T(2,128)(2,1)} %refs_4_.1) | copy-start | bytes 3076
  53.8 10.1 %collective-permute-start = (bf16[256,512]{1,0:T(8,128)(2,1)S(1)}, bf16[256,512]{1,0:T(8,128)(2,1)S(1)}, u32[]{:S(2)}, u32[]{:S(2)}) collective-permute-start(bf16[256,512]{1,0:T(8,128)(2,1)S(1)} %project_out.3), channel_id=1, source_target_pairs={{0,8},{8,16},{16,24},{24,32},{32,40},{40,48},{48,56},{56,64},{64,7... | collective-permute-start | bytes 786440 | tf_op jit(solution)/shard_map/ppermute | solution.py:195
  111.0 12.6 %collective-permute-start.1 = (bf16[256,512]{1,0:T(8,128)(2,1)S(1)}, bf16[256,512]{1,0:T(8,128)(2,1)S(1)}, u32[]{:S(2)}, u32[]{:S(2)}) collective-permute-start(bf16[256,512]{1,0:T(8,128)(2,1)S(1)} %project_out.4), channel_id=1, source_target_pairs={{0,8},{8,16},{16,24},{24,32},{32,40},{40,48},{48,56},{56,64},{64,7... | collective-permute-start | bytes 786440 | tf_op jit(solution)/shard_map/ppermute | solution.py:195
  124.9 1.2 copy-start.7
  126.1 29.2 %all-to-all-start.4 = ((bf16[8,32,3456]{2,1,0:T(8,128)(2,1)}), bf16[8,32,3456]{2,1,0:T(8,128)(2,1)}, u32[]{:S(2)}, u32[]{:S(2)}) async-start(bf16[8,32,3456]{2,1,0:T(8,128)(2,1)} %copy-done.7), calls=%async_computation.4 | async-start | bytes 3538944 | tf_op jit(solution)/shard_map/all_to_all | solution.py:148
  133.1 22.2 %collective-permute-start.2 = (bf16[128,512]{1,0:T(8,128)(2,1)S(1)}, bf16[128,512]{1,0:T(8,128)(2,1)S(1)}, u32[]{:S(2)}, u32[]{:S(2)}) collective-permute-start(bf16[128,512]{1,0:T(8,128)(2,1)S(1)} %get-tuple-element.12), channel_id=1, source_target_pairs={{0,256},{8,264},{16,272},{24,280},{32,288},{40,296},{48,304},{56,3... | collective-permute-start | bytes 393224 | tf_op jit(solution)/shard_map/ppermute | solution.py:217
  134.4 20.9 %collective-permute-start.3 = (bf16[128,512]{1,0:T(8,128)(2,1)S(1)}, bf16[128,512]{1,0:T(8,128)(2,1)S(1)}, u32[]{:S(2)}, u32[]{:S(2)}) collective-permute-start(bf16[128,512]{1,0:T(8,128)(2,1)S(1)} %get-tuple-element.13), channel_id=1, source_target_pairs={{0,248},{8,240},{16,232},{24,224},{32,216},{40,208},{48,200},{56,1... | collective-permute-start | bytes 393224 | tf_op jit(solution)/shard_map/ppermute | solution.py:217
  155.3 3.4 %copy-start.9 = (bf16[128,512]{1,0:T(8,128)(2,1)}, bf16[128,512]{1,0:T(8,128)(2,1)S(1)}, u32[]{:S(2)}) copy-start(bf16[128,512]{1,0:T(8,128)(2,1)S(1)} %collective-permute-done.3.refs_1_) | copy-start | bytes 393220
  157.7 1.0 copy-start.3
  158.7 22.4 %all-to-all-start.5 = ((bf16[8,32,2048]{2,1,0:T(8,128)(2,1)}), bf16[8,32,2048]{2,1,0:T(8,128)(2,1)S(1)}, u32[]{:S(2)}, u32[]{:S(2)}) async-start(bf16[8,32,2048]{2,1,0:T(8,128)(2,1)} %copy-done.3), calls=%async_computation.5 | async-start | bytes 2097152 | tf_op jit(solution)/shard_map/all_to_all | solution.py:148
  165.4 14.1 %collective-permute-start.4 = (bf16[128,512]{1,0:T(8,128)(2,1)S(1)}, bf16[128,512]{1,0:T(8,128)(2,1)S(1)}, u32[]{:S(2)}, u32[]{:S(2)}) collective-permute-start(bf16[128,512]{1,0:T(8,128)(2,1)S(1)} %collective-permute-done.2.refs_0_), channel_id=1, source_target_pairs={{256,504},{264,496},{272,488},{280,480},{288,472},{296,464},{304,4... | collective-permute-start | bytes 393224 | tf_op jit(solution)/shard_map/ppermute | solution.py:220
  168.9 11.5 %collective-permute-start.5 = (bf16[128,512]{1,0:T(8,128)(2,1)}, bf16[128,512]{1,0:T(8,128)(2,1)S(1)}, u32[]{:S(2)}, u32[]{:S(2)}) collective-permute-start(bf16[128,512]{1,0:T(8,128)(2,1)} %copy-done.9), channel_id=1, source_target_pairs={{0,256},{8,264},{16,272},{24,280},{32,288},{40,296},{48,304},{56,3... | collective-permute-start | bytes 393224 | tf_op jit(solution)/shard_map/ppermute | solution.py:221

commit v7 on v6

--- a/solution.py
+++ b/solution.py
@@ -22,27 +22,29 @@
 
 
 def project_rows(parts, wide, scaled, weight_ref, out_ref):
-    rows = wide.shape[0] // parts
+    tokens = wide.shape[0]
+    rows = tokens // parts
     blocks = window_blocks(rows)
-    squares = jnp.sum(wide * wide, axis=1, keepdims=True)
-    high = squares.astype(BF16).astype(F32)
-    low = squares - high
-    lane = lax.broadcasted_iota(jnp.int32, (rows, 128), 1)
+    ones = jnp.ones((8, wide.shape[1]), BF16)
+    squares = lax.dot_general(
+        ones, (wide * wide).astype(BF16), (((1,), (1,)), ((), ())), preferred_element_type=F32
+    )[:1]
+    top = lax.broadcasted_iota(jnp.int32, (rows, KV_COLS), 0) == 0
     step = 256
     for start in range(0, Q_COLS, step):
         tile = jnp.dot(scaled, weight_ref[:, start : start + step], preferred_element_type=F32)
         out_ref[:, :, start : start + step] = tile.astype(BF16).reshape(parts, rows, step)
-    tile = jnp.dot(scaled, weight_ref[:, Q_COLS:], preferred_element_type=F32).astype(BF16)
-    last = Q_COLS + blocks * KV_COLS
+    tile = jnp.dot(scaled, weight_ref[:, Q_COLS:], preferred_element_type=F32)
     for j in range(parts):
-        sums = jnp.zeros((rows, 128), F32)
+        first = (j + 1 - blocks) * rows
+        sums = pltpu.roll(squares, -first % tokens, 1) if first % tokens else squares
         for b in range(blocks):
-            at = max(j - blocks + 1 + b, 0) * rows
+            at = max(first + b * rows, 0)
             start = Q_COLS + b * KV_COLS
-            out_ref[j, :, start : start + KV_COLS] = tile[at : at + rows]
-            sums = jnp.where(lane == 2 * b, high[at : at + rows], sums)
-            sums = jnp.where(lane == 2 * b + 1, low[at : at + rows], sums)
-        out_ref[j, :, last:] = sums.astype(BF16)
+            piece = tile[at : at + rows]
+            if b == 0:
+                piece = jnp.where(top, jnp.broadcast_to(sums[:, :KV_COLS], piece.shape), piece)
+            out_ref[j, :, start : start + KV_COLS] = piece.astype(BF16)
 
 
 FIRST, EVICT, RANK, SECTION = range(4)
@@ -85,15 +87,15 @@
             value = value + got_ref[j, :, start : start + size].astype(F32)
         return value
 
-    last = Q_COLS + blocks * KV_COLS
-    sums = total(last, 128)
-    scales = []
+    column = lax.broadcasted_iota(jnp.int32, (rows, tokens), 1)
+    row = lax.broadcasted_iota(jnp.int32, (rows, tokens), 0)
+    windows = [total(Q_COLS + b * KV_COLS, KV_COLS) for b in range(blocks)]
+    sums = jnp.broadcast_to(windows[0][:1], (rows, KV_COLS))
+    scales, keys, values = [], [], []
     for b in range(blocks):
-        squares = sums[:, 2 * b : 2 * b + 1] + sums[:, 2 * b + 1 : 2 * b + 2]
+        squares = jnp.sum(jnp.where(column == row + b * rows, sums, F32(0.0)), axis=1, keepdims=True)
         scales.append(lax.rsqrt(squares / width + NORM_EPS))
-    keys, values = [], []
-    for b in range(blocks):
-        both = (total(Q_COLS + b * KV_COLS, KV_COLS) * scales[b]).astype(BF16)
+        both = (windows[b] * scales[b]).astype(BF16)
         keys.append(both[:, :HEAD_DIM])
         values.append(both[:, HEAD_DIM:])
     keys = jnp.concatenate(keys, axis=0)
@@ -107,10 +109,9 @@
     segment_row = segments_ref[pl.ds(item, 1), :]
     segment_row = pltpu.roll(segment_row, lax.rem(tokens - first, tokens), 1)
     segment_rows = jnp.broadcast_to(segment_row, (rows, tokens))
-    column = lax.broadcasted_iota(jnp.int32, (rows, tokens), 1)
-    own = lax.broadcasted_iota(jnp.int32, (rows, tokens), 0) + before
+    own = row + before
     own_segment = jnp.sum(jnp.where(column == own, segment_rows, 0), axis=1, keepdims=True)
-    visible = (segment_rows == own_segment) & (column <= own) & (column + first >= 0)
+    visible = (segment_rows == own_segment) & (column <= own) & (column + first >= 0) & (column >= 1)
     visible = visible[:, :span]
 
     scores = lax.dot_general(
@@ -179,7 +180,7 @@
     ticks = fresh.shape[0] + 1
     tokens, width = carried.shape[1:]
     rows = tokens // parts
-    columns = Q_COLS + window_blocks(rows) * KV_COLS + 128
+    columns = Q_COLS + window_blocks(rows) * KV_COLS
     flags = jnp.stack([(section == 0).astype(jnp.int32), evict_tick[0], rank, section])
     following = [(i, i + 1) for i in range(sections - 1)]
     half = sections // 2

time: 183 us -> 181 us (0.989)
  the two profiles are of different devices: /device:TPU:199 before, /device:TPU:71 now
where the time goes in v7:
time: 181 us
  blocking collectives  88.1 us (49%)
  starting transfers between devices  40.7 us (22%)
  waiting for transfers between devices  32.1 us (18%)
  Pallas kernels  12 us (7%)
  local copies, waits for them, and re-layouts  5.5 us (3%)
    all_to_all x4, blocking collectives, exchange(): return lax.all_to_all(value, 'tp', split_axis=0, concat_axis=0, tiled=True)  88.1 us
    ppermute x1, waiting for transfers between devices, shards(): lax.ppermute(got[2], 'pipe', across)  19.6 us
    ppermute x2, starting transfers between devices, shards(): arrived = lax.ppermute(result, 'pipe', following)  15.9 us
    all_to_all x2, starting transfers between devices, exchange(): return lax.all_to_all(value, 'tp', split_axis=0, concat_axis=0, tiled=True)  13.6 us
    ppermute x1, starting transfers between devices, shards(): top = lax.ppermute(waited[0], 'pipe', turned_across)  7.92 us
    ppermute x2, waiting for transfers between devices, shards(): arrived = lax.ppermute(result, 'pipe', following)  6.59 us
    ppermute x1, waiting for transfers between devices, shards(): top = lax.ppermute(waited[0], 'pipe', turned_across)  5.65 us
    unnamed x24, local copies, waits for them, and re-layouts  5.5 us
  transfers between devices with their start and end apart: 8, of which 5 were waited for; matrix products, arithmetic and copies ran while one was open for 0% of the time, Pallas kernels for 0%

profile of v7, /device:TPU:71, one launch (start us, length us, event | category | flops | bytes accessed | tf_op | source)
XLA Modules:
  0.0 180.7 jit_solution(3465286686228204460)
XLA Ops:
  1.3 0.1 pad_add_fusion.flags_ref
  1.4 1.7 copy-done
  3.0 0.9 copy-done.4
  4.0 0.7 copy-done.10
  4.7 1.4 project.3
  6.0 0.0 copy-start.8
  6.0 26.9 %all_to_all.30.got_ref = bf16[8,32,3328]{2,1,0:T(8,128)(2,1)S(1)} all-to-all(bf16[8,32,3328]{2,1,0:T(8,128)(2,1)S(1)} %project.3), channel_id=1, replica_groups=mesh['pipe'=64,'tp'=8] {'tp'}, dimensions={0} | all-to-all | bytes 3407872 | tf_op jit(solution)/shard_map/all_to_all | solution.py:149
  32.9 0.0 copy-done.8
  32.9 1.4 attend.3
  34.3 0.0 copy-start.2
  34.3 18.2 %all_to_all.31 = bf16[8,32,2048]{2,1,0:T(8,128)(2,1)S(1)} all-to-all(bf16[8,32,2048]{2,1,0:T(8,128)(2,1)S(1)} %attend.3), channel_id=1, replica_groups=mesh['pipe'=64,'tp'=8] {'tp'}, dimensions={0} | all-to-all | bytes 2097152 | tf_op jit(solution)/shard_map/all_to_all | solution.py:149
  52.5 0.0 copy-done.5
  52.5 0.0 copy-done.2
  52.5 0.0 copy-start.11
  52.5 0.7 project_out.3
  53.2 6.8 %collective-permute-start = (bf16[256,512]{1,0:T(8,128)(2,1)S(1)}, bf16[256,512]{1,0:T(8,128)(2,1)S(1)}, u32[]{:S(2)}, u32[]{:S(2)}) collective-permute-start(bf16[256,512]{1,0:T(8,128)(2,1)S(1)} %project_out.3), channel_id=1, source_target_pairs={{0,8},{8,16},{16,24},{24,32},{32,40},{40,48},{48,56},{56,64},{64,7... | collective-permute-start | bytes 786440 | tf_op jit(solution)/shard_map/ppermute | solution.py:196
  60.1 3.3 %collective-permute-done.refs_0_ = bf16[256,512]{1,0:T(8,128)(2,1)S(1)} collective-permute-done((bf16[256,512]{1,0:T(8,128)(2,1)S(1)}, bf16[256,512]{1,0:T(8,128)(2,1)S(1)}, u32[]{:S(2)}, u32[]{:S(2)}) %collective-permute-start) | collective-permute-done | bytes 262176 | tf_op jit(solution)/shard_map/ppermute | solution.py:196
  63.4 0.0 copy-done.1
  63.4 0.0 copy-done.6
  63.4 0.0 copy-done.11
  63.4 1.4 project.4
  64.8 24.8 %all_to_all.32.got_ref = bf16[8,32,3328]{2,1,0:T(8,128)(2,1)S(1)} all-to-all(bf16[8,32,3328]{2,1,0:T(8,128)(2,1)S(1)} %get-tuple-element.9), channel_id=1, replica_groups=mesh['pipe'=64,'tp'=8] {'tp'}, dimensions={0} | all-to-all | bytes 3407872 | tf_op jit(solution)/shard_map/all_to_all | solution.py:149
  89.6 1.4 attend.4
  91.0 18.2 %all_to_all.33 = bf16[8,32,2048]{2,1,0:T(8,128)(2,1)S(1)} all-to-all(bf16[8,32,2048]{2,1,0:T(8,128)(2,1)S(1)} %attend.4), channel_id=1, replica_groups=mesh['pipe'=64,'tp'=8] {'tp'}, dimensions={0} | all-to-all | bytes 2097152 | tf_op jit(solution)/shard_map/all_to_all | solution.py:149
  109.2 0.7 project_out.4
  109.9 9.1 %collective-permute-start.1 = (bf16[256,512]{1,0:T(8,128)(2,1)S(1)}, bf16[256,512]{1,0:T(8,128)(2,1)S(1)}, u32[]{:S(2)}, u32[]{:S(2)}) collective-permute-start(bf16[256,512]{1,0:T(8,128)(2,1)S(1)} %project_out.4), channel_id=1, source_target_pairs={{0,8},{8,16},{16,24},{24,32},{32,40},{40,48},{48,56},{56,64},{64,7... | collective-permute-start | bytes 786440 | tf_op jit(solution)/shard_map/ppermute | solution.py:196
  119.0 3.3 %collective-permute-done.1.refs_2_ = bf16[256,512]{1,0:T(8,128)(2,1)S(1)} collective-permute-done((bf16[256,512]{1,0:T(8,128)(2,1)S(1)}, bf16[256,512]{1,0:T(8,128)(2,1)S(1)}, u32[]{:S(2)}, u32[]{:S(2)}) %collective-permute-start.1) | collective-permute-done | bytes 262176 | tf_op jit(solution)/shard_map/ppermute | solution.py:196
  122.3 1.4 project.5
  123.7 0.0 copy-start.7
  123.7 1.2 copy-done.7
  124.9 6.9 %all-to-all-start.4 = ((bf16[8,32,3328]{2,1,0:T(8,128)(2,1)}), bf16[8,32,3328]{2,1,0:T(8,128)(2,1)}, u32[]{:S(2)}, u32[]{:S(2)}) async-start(bf16[8,32,3328]{2,1,0:T(8,128)(2,1)} %copy-done.7), calls=%async_computation.4 | async-start | bytes 3407872 | tf_op jit(solution)/shard_map/all_to_all | solution.py:149
  131.8 1.3 collective-permute-start.2
  133.1 0.7 collective-permute-start.3
  133.8 19.6 %collective-permute-done.2.refs_0_ = bf16[128,512]{1,0:T(8,128)(2,1)S(1)} collective-permute-done((bf16[128,512]{1,0:T(8,128)(2,1)S(1)}, bf16[128,512]{1,0:T(8,128)(2,1)S(1)}, u32[]{:S(2)}, u32[]{:S(2)}) %collective-permute-start.2) | collective-permute-done | bytes 131104 | tf_op jit(solution)/shard_map/ppermute | solution.py:218
  153.4 0.0 collective-permute-done.3.refs_1_
  153.4 0.0 all-to-all-done.4.got_ref
  153.4 2.3 %attend.5 = bf16[8,32,2048]{2,1,0:T(8,128)(2,1)S(1)} custom-call(s32[4]{0:T(128)S(1)} %pad_add_fusion.flags_ref, s32[66,256]{1,0:T(8,128)S(1)} %copy-done.8, bf16[8,32,3328]{2,1,0:T(8,128)(2,1)} %all-to-all-done.4.got_ref, bf16[128,512]{1,0:T(8,128)(2,1)S(1)} %collective-permute-done.2.refs_0_, bf16[128,512]{1,0:T(8,128)(2,1)S(1)} %collective-permute-done.3.refs_1_), custom_call_target="tpu_custom_call" | custom-call | tf_op jit(solution)/shard_map/attend/pallas_call | solution.py:154
  155.8 0.0 copy-start.3
  155.8 1.0 copy-done.3
  156.8 0.0 copy-done.9
  156.8 6.7 %all-to-all-start.5 = ((bf16[8,32,2048]{2,1,0:T(8,128)(2,1)}), bf16[8,32,2048]{2,1,0:T(8,128)(2,1)S(1)}, u32[]{:S(2)}, u32[]{:S(2)}) async-start(bf16[8,32,2048]{2,1,0:T(8,128)(2,1)} %copy-done.3), calls=%async_computation.5 | async-start | bytes 2097152 | tf_op jit(solution)/shard_map/all_to_all | solution.py:149
  163.5 7.9 %collective-permute-start.4 = (bf16[128,512]{1,0:T(8,128)(2,1)S(1)}, bf16[128,512]{1,0:T(8,128)(2,1)S(1)}, u32[]{:S(2)}, u32[]{:S(2)}) collective-permute-start(bf16[128,512]{1,0:T(8,128)(2,1)S(1)} %collective-permute-done.2.refs_0_), channel_id=1, source_target_pairs={{256,504},{264,496},{272,488},{280,480},{288,472},{296,464},{304,4... | collective-permute-start | bytes 393224 | tf_op jit(solution)/shard_map/ppermute | solution.py:221
  171.4 1.3 collective-permute-start.5
  172.7 5.6 %collective-permute-done.4 = bf16[128,512]{1,0:T(8,128)(2,1)S(1)} collective-permute-done((bf16[128,512]{1,0:T(8,128)(2,1)S(1)}, bf16[128,512]{1,0:T(8,128)(2,1)S(1)}, u32[]{:S(2)}, u32[]{:S(2)}) %collective-permute-start.4) | collective-permute-done | bytes 131104 | tf_op jit(solution)/shard_map/ppermute | solution.py:221
  178.4 0.2 collective-permute-done.5
  178.5 0.7 maximum_bitcast_fusion
  179.2 0.0 all-to-all-done.5
  179.3 1.4 project_out.5
  (7 shorter events, 0.0 us)
Async XLA Ops:
  1.4 1.7 copy-start
  3.0 0.9 copy-start.4
  4.0 0.7 copy-start.10
  6.0 26.9 %copy-start.8 = (s32[66,256]{1,0:T(8,128)S(1)}, s32[66,256]{1,0:T(8,128)}, u32[]{:S(2)}) copy-start(s32[66,256]{1,0:T(8,128)} %segments_ref.5) | copy-start | bytes 202756
  32.9 19.6 %copy-start.5 = (bf16[1,256,512]{2,1,0:T(8,128)(2,1)S(1)}, bf16[1,256,512]{2,1,0:T(8,128)(2,1)}, u32[]{:S(2)}) copy-start(bf16[1,256,512]{2,1,0:T(8,128)(2,1)} %param.7) | copy-start | bytes 786436
  34.3 18.2 %copy-start.2 = (bf16[1,2048,512]{2,1,0:T(8,128)(2,1)S(1)}, bf16[1,2048,512]{2,1,0:T(8,128)(2,1)}, u32[]{:S(2)}) copy-start(bf16[1,2048,512]{2,1,0:T(8,128)(2,1)} %param.11) | copy-start | bytes 6291460
  52.5 10.9 %copy-start.1 = (bf16[1,512,2304]{2,1,0:T(8,128)(2,1)S(1)}, bf16[1,512,2304]{2,1,0:T(8,128)(2,1)}, u32[]{:S(2)}) copy-start(bf16[1,512,2304]{2,1,0:T(8,128)(2,1)} %param.10) | copy-start | bytes 7077892
  52.5 10.9 %copy-start.6 = (bf16[2,256,512]{2,1,0:T(8,128)(2,1)S(1)}, bf16[2,256,512]{2,1,0:T(8,128)(2,1)}, u32[]{:S(2)}) copy-start(bf16[2,256,512]{2,1,0:T(8,128)(2,1)} %refs_3_.1) | copy-start | bytes 1572868
  52.5 10.9 %copy-start.11 = (bf16[1,512]{1,0:T(2,128)(2,1)S(1)}, bf16[1,512]{1,0:T(2,128)(2,1)}, u32[]{:S(2)}) copy-start(bf16[1,512]{1,0:T(2,128)(2,1)} %refs_4_.1) | copy-start | bytes 3076
  53.2 10.1 %collective-permute-start = (bf16[256,512]{1,0:T(8,128)(2,1)S(1)}, bf16[256,512]{1,0:T(8,128)(2,1)S(1)}, u32[]{:S(2)}, u32[]{:S(2)}) collective-permute-start(bf16[256,512]{1,0:T(8,128)(2,1)S(1)} %project_out.3), channel_id=1, source_target_pairs={{0,8},{8,16},{16,24},{24,32},{32,40},{40,48},{48,56},{56,64},{64,7... | collective-permute-start | bytes 786440 | tf_op jit(solution)/shard_map/ppermute | solution.py:196
  109.9 12.4 %collective-permute-start.1 = (bf16[256,512]{1,0:T(8,128)(2,1)S(1)}, bf16[256,512]{1,0:T(8,128)(2,1)S(1)}, u32[]{:S(2)}, u32[]{:S(2)}) collective-permute-start(bf16[256,512]{1,0:T(8,128)(2,1)S(1)} %project_out.4), channel_id=1, source_target_pairs={{0,8},{8,16},{16,24},{24,32},{32,40},{40,48},{48,56},{56,64},{64,7... | collective-permute-start | bytes 786440 | tf_op jit(solution)/shard_map/ppermute | solution.py:196
  123.7 1.2 copy-start.7
  124.9 28.5 %all-to-all-start.4 = ((bf16[8,32,3328]{2,1,0:T(8,128)(2,1)}), bf16[8,32,3328]{2,1,0:T(8,128)(2,1)}, u32[]{:S(2)}, u32[]{:S(2)}) async-start(bf16[8,32,3328]{2,1,0:T(8,128)(2,1)} %copy-done.7), calls=%async_computation.4 | async-start | bytes 3407872 | tf_op jit(solution)/shard_map/all_to_all | solution.py:149
  131.8 21.6 %collective-permute-start.2 = (bf16[128,512]{1,0:T(8,128)(2,1)S(1)}, bf16[128,512]{1,0:T(8,128)(2,1)S(1)}, u32[]{:S(2)}, u32[]{:S(2)}) collective-permute-start(bf16[128,512]{1,0:T(8,128)(2,1)S(1)} %get-tuple-element.12), channel_id=1, source_target_pairs={{0,256},{8,264},{16,272},{24,280},{32,288},{40,296},{48,304},{56,3... | collective-permute-start | bytes 393224 | tf_op jit(solution)/shard_map/ppermute | solution.py:218
  133.1 20.3 %collective-permute-start.3 = (bf16[128,512]{1,0:T(8,128)(2,1)S(1)}, bf16[128,512]{1,0:T(8,128)(2,1)S(1)}, u32[]{:S(2)}, u32[]{:S(2)}) collective-permute-start(bf16[128,512]{1,0:T(8,128)(2,1)S(1)} %get-tuple-element.13), channel_id=1, source_target_pairs={{0,248},{8,240},{16,232},{24,224},{32,216},{40,208},{48,200},{56,1... | collective-permute-start | bytes 393224 | tf_op jit(solution)/shard_map/ppermute | solution.py:218
  153.4 3.3 %copy-start.9 = (bf16[128,512]{1,0:T(8,128)(2,1)}, bf16[128,512]{1,0:T(8,128)(2,1)S(1)}, u32[]{:S(2)}) copy-start(bf16[128,512]{1,0:T(8,128)(2,1)S(1)} %collective-permute-done.3.refs_1_) | copy-start | bytes 393220
  155.8 1.0 copy-start.3
  156.8 22.5 %all-to-all-start.5 = ((bf16[8,32,2048]{2,1,0:T(8,128)(2,1)}), bf16[8,32,2048]{2,1,0:T(8,128)(2,1)S(1)}, u32[]{:S(2)}, u32[]{:S(2)}) async-start(bf16[8,32,2048]{2,1,0:T(8,128)(2,1)} %copy-done.3), calls=%async_computation.5 | async-start | bytes 2097152 | tf_op jit(solution)/shard_map/all_to_all | solution.py:149
  163.5 14.9 %collective-permute-start.4 = (bf16[128,512]{1,0:T(8,128)(2,1)S(1)}, bf16[128,512]{1,0:T(8,128)(2,1)S(1)}, u32[]{:S(2)}, u32[]{:S(2)}) collective-permute-start(bf16[128,512]{1,0:T(8,128)(2,1)S(1)} %collective-permute-done.2.refs_0_), channel_id=1, source_target_pairs={{256,504},{264,496},{272,488},{280,480},{288,472},{296,464},{304,4... | collective-permute-start | bytes 393224 | tf_op jit(solution)/shard_map/ppermute | solution.py:221
  171.4 7.1 %collective-permute-start.5 = (bf16[128,512]{1,0:T(8,128)(2,1)}, bf16[128,512]{1,0:T(8,128)(2,1)S(1)}, u32[]{:S(2)}, u32[]{:S(2)}) collective-permute-start(bf16[128,512]{1,0:T(8,128)(2,1)} %copy-done.9), channel_id=1, source_target_pairs={{0,256},{8,264},{16,272},{24,280},{32,288},{40,296},{48,304},{56,3... | collective-permute-start | bytes 393224 | tf_op jit(solution)/shard_map/ppermute | solution.py:222

commit v8 on v7

--- a/solution.py
+++ b/solution.py
@@ -47,14 +47,13 @@
             out_ref[j, :, start : start + KV_COLS] = piece.astype(BF16)
 
 
-FIRST, EVICT, RANK, SECTION = range(4)
-
-
-def project_kernel(parts, tick, stash, flags_ref, *refs):
-    earlier, refs = (refs[:tick], refs[tick:]) if stash else ((), refs)
+def project_kernel(parts, tick, stash, *refs):
+    earlier = ()
+    if stash:
+        evict_ref, earlier, refs = refs[0], refs[1 : tick + 1], refs[tick + 1 :]
     if tick > 0:
         arrived_ref, fresh_ref, gain_ref, weight_ref, out_ref, current_ref = refs[:6]
-        current = jnp.where(flags_ref[FIRST] == 1, fresh_ref[tick - 1], arrived_ref[...])
+        current = jnp.where(lax.axis_index("pipe") == 0, fresh_ref[tick - 1], arrived_ref[...])
         current_ref[...] = current
     else:
         arrived_ref, gain_ref, weight_ref, out_ref = refs
@@ -62,7 +61,7 @@
     if earlier:
         chosen = current
         for at, earlier_ref in enumerate(earlier):
-            chosen = jnp.where(flags_ref[EVICT] == at, earlier_ref[...], chosen)
+            chosen = jnp.where(evict_ref[0] == at, earlier_ref[...], chosen)
         half = chosen.shape[0] // 2
         refs[6][...] = chosen[:half]
         refs[7][...] = chosen[half:]
@@ -71,15 +70,15 @@
     project_rows(parts, wide, scaled, weight_ref, out_ref)
 
 
-def attend_kernel(parts, width, back, flags_ref, segments_ref, got_ref, *refs):
+def attend_kernel(parts, width, back, segments_ref, got_ref, *refs):
     out_ref = refs[-1]
     rows = got_ref.shape[1]
     tokens = rows * parts
     blocks = window_blocks(rows)
     span = blocks * rows
     before = span - rows
-    rank = flags_ref[RANK]
-    item = flags_ref[SECTION] + back
+    rank = lax.axis_index("tp")
+    item = lax.axis_index("pipe") + back
 
     def total(start, size):
         value = got_ref[0, :, start : start + size].astype(F32)
@@ -149,16 +148,16 @@
     return lax.all_to_all(value, "tp", split_axis=0, concat_axis=0, tiled=True)
 
 
-def attend(flags, segments, got, width, back, waited=()):
+def attend(segments, got, width, back, waited=()):
     parts, rows, _ = got.shape
     return pl.pallas_call(
         functools.partial(attend_kernel, parts, width, back),
         out_shape=shard((parts, rows, Q_COLS)),
-        in_specs=[SMEM, VMEM, VMEM] + [ANY] * len(waited),
+        in_specs=[VMEM, VMEM] + [ANY] * len(waited),
         out_specs=VMEM,
         compiler_params=PARAMS,
         name="attend",
-    )(flags, segments, got, *waited)
+    )(segments, got, *waited)
 
 
 def project_out(current, mixed, out_weight):
@@ -173,15 +172,12 @@
 
 
 def shards(carried, fresh, gains, qkv_weight, out_weight, segments, evict_tick):
-    section = lax.axis_index("pipe")
-    rank = lax.axis_index("tp")
     sections = lax.axis_size("pipe")
     parts = lax.axis_size("tp")
     ticks = fresh.shape[0] + 1
     tokens, width = carried.shape[1:]
     rows = tokens // parts
     columns = Q_COLS + window_blocks(rows) * KV_COLS
-    flags = jnp.stack([(section == 0).astype(jnp.int32), evict_tick[0], rank, section])
     following = [(i, i + 1) for i in range(sections - 1)]
     half = sections // 2
     across = [(i, i + half) for i in range(half)]
@@ -190,16 +186,16 @@
     inputs = [carried[0]]
     for tick in range(ticks):
         outs = [shard((parts, rows, columns))]
-        operands = [flags, inputs[0], gains, qkv_weight[0]]
-        specs = [SMEM, VMEM, VMEM, VMEM]
+        operands = [inputs[0], gains, qkv_weight[0]]
+        specs = [VMEM] * 3
         if tick > 0:
             arrived = lax.ppermute(result, "pipe", following)
-            operands = [flags, arrived, fresh, gains, qkv_weight[0]]
-            specs = [SMEM, VMEM, VMEM, VMEM, VMEM]
+            operands = [arrived, fresh, gains, qkv_weight[0]]
+            specs = [VMEM] * 4
             outs.append(shard((tokens, width)))
         if tick == ticks - 1:
-            operands[1:1] = inputs
-            specs[1:1] = [VMEM] * tick
+            operands[:0] = [evict_tick, *inputs]
+            specs[:0] = [SMEM] + [VMEM] * tick
             outs += [shard((tokens // 2, width))] * 2
         got = pl.pallas_call(
             functools.partial(project_kernel, parts, tick, tick == ticks - 1),
@@ -216,7 +212,7 @@
         waited = ()
         if tick == ticks - 1:
             waited = (lax.ppermute(got[2], "pipe", across), lax.ppermute(got[3], "pipe", turned))
-        mixed = exchange(attend(flags, segments, sums, width * parts, ticks - 1 - tick, waited))
+        mixed = exchange(attend(segments, sums, width * parts, ticks - 1 - tick, waited))
         result = project_out(inputs[tick], mixed, out_weight[0])
     top = lax.ppermute(waited[0], "pipe", turned_across)
     low = lax.ppermute(waited[1], "pipe", across)

time: 181 us -> 178 us (0.983)
  Pallas kernels: 12 us -> 9.3 us
where the time goes in v8:
time: 178 us; the launch traced here: 177 us
  blocking collectives  88.1 us (49%)
  starting transfers between devices  40.7 us (23%)
  waiting for transfers between devices  31.4 us (18%)
  Pallas kernels  9.3 us (5%)
  local copies, waits for them, and re-layouts  5.49 us (3%)
    all_to_all x4, blocking collectives, exchange(): return lax.all_to_all(value, 'tp', split_axis=0, concat_axis=0, tiled=True)  88.1 us
    ppermute x1, waiting for transfers between devices, shards(): lax.ppermute(got[2], 'pipe', across)  19.6 us
    ppermute x2, starting transfers between devices, shards(): arrived = lax.ppermute(result, 'pipe', following)  15.9 us
    all_to_all x2, starting transfers between devices, exchange(): return lax.all_to_all(value, 'tp', split_axis=0, concat_axis=0, tiled=True)  13.6 us
    ppermute x1, starting transfers between devices, shards(): top = lax.ppermute(waited[0], 'pipe', turned_across)  7.92 us
    ppermute x2, waiting for transfers between devices, shards(): arrived = lax.ppermute(result, 'pipe', following)  5.94 us
    ppermute x1, waiting for transfers between devices, shards(): top = lax.ppermute(waited[0], 'pipe', turned_across)  5.65 us
    unnamed x24, local copies, waits for them, and re-layouts  5.49 us
  transfers between devices with their start and end apart: 8, of which 5 were waited for; matrix products, arithmetic and copies ran while one was open for 0% of the time, Pallas kernels for 0%

profile of v8, /device:TPU:71, one launch (start us, length us, event | category | flops | bytes accessed | tf_op | source)
XLA Modules:
  0.0 177.2 jit_solution(13630837682484327067)
XLA Ops:
  0.6 0.0 copy-start
  0.6 1.7 copy-done
  2.3 0.9 copy-done.4
  3.2 0.7 copy-done.10
  3.9 0.8 project.3
  4.8 0.0 copy-start.8
  4.8 26.9 %all_to_all.30.got_ref = bf16[8,32,3328]{2,1,0:T(8,128)(2,1)S(1)} all-to-all(bf16[8,32,3328]{2,1,0:T(8,128)(2,1)S(1)} %project.3), channel_id=1, replica_groups=mesh['pipe'=64,'tp'=8] {'tp'}, dimensions={0} | all-to-all | bytes 3407872 | tf_op jit(solution)/shard_map/all_to_all | solution.py:148
  31.6 0.0 copy-done.8
  31.7 0.8 attend.3
  32.5 0.0 copy-start.2
  32.5 18.2 %all_to_all.31 = bf16[8,32,2048]{2,1,0:T(8,128)(2,1)S(1)} all-to-all(bf16[8,32,2048]{2,1,0:T(8,128)(2,1)S(1)} %attend.3), channel_id=1, replica_groups=mesh['pipe'=64,'tp'=8] {'tp'}, dimensions={0} | all-to-all | bytes 2097152 | tf_op jit(solution)/shard_map/all_to_all | solution.py:148
  50.7 0.0 copy-done.5
  50.7 0.0 copy-done.2
  50.7 0.0 copy-start.11
  50.7 0.7 project_out.3
  51.4 6.8 %collective-permute-start = (bf16[256,512]{1,0:T(8,128)(2,1)S(1)}, bf16[256,512]{1,0:T(8,128)(2,1)S(1)}, u32[]{:S(2)}, u32[]{:S(2)}) collective-permute-start(bf16[256,512]{1,0:T(8,128)(2,1)S(1)} %project_out.3), channel_id=1, source_target_pairs={{0,8},{8,16},{16,24},{24,32},{32,40},{40,48},{48,56},{56,64},{64,7... | collective-permute-start | bytes 786440 | tf_op jit(solution)/shard_map/ppermute | solution.py:192
  58.3 3.3 %collective-permute-done.refs_0_ = bf16[256,512]{1,0:T(8,128)(2,1)S(1)} collective-permute-done((bf16[256,512]{1,0:T(8,128)(2,1)S(1)}, bf16[256,512]{1,0:T(8,128)(2,1)S(1)}, u32[]{:S(2)}, u32[]{:S(2)}) %collective-permute-start) | collective-permute-done | bytes 262176 | tf_op jit(solution)/shard_map/ppermute | solution.py:192
  61.6 0.0 copy-done.1
  61.6 0.0 copy-done.6
  61.6 0.0 copy-done.11
  61.6 0.8 project.4
  62.4 24.8 %all_to_all.32.got_ref = bf16[8,32,3328]{2,1,0:T(8,128)(2,1)S(1)} all-to-all(bf16[8,32,3328]{2,1,0:T(8,128)(2,1)S(1)} %get-tuple-element.9), channel_id=1, replica_groups=mesh['pipe'=64,'tp'=8] {'tp'}, dimensions={0} | all-to-all | bytes 3407872 | tf_op jit(solution)/shard_map/all_to_all | solution.py:148
  87.3 0.8 attend.4
  88.1 18.2 %all_to_all.33 = bf16[8,32,2048]{2,1,0:T(8,128)(2,1)S(1)} all-to-all(bf16[8,32,2048]{2,1,0:T(8,128)(2,1)S(1)} %attend.4), channel_id=1, replica_groups=mesh['pipe'=64,'tp'=8] {'tp'}, dimensions={0} | all-to-all | bytes 2097152 | tf_op jit(solution)/shard_map/all_to_all | solution.py:148
  106.3 0.7 project_out.4
  107.0 9.1 %collective-permute-start.1 = (bf16[256,512]{1,0:T(8,128)(2,1)S(1)}, bf16[256,512]{1,0:T(8,128)(2,1)S(1)}, u32[]{:S(2)}, u32[]{:S(2)}) collective-permute-start(bf16[256,512]{1,0:T(8,128)(2,1)S(1)} %project_out.4), channel_id=1, source_target_pairs={{0,8},{8,16},{16,24},{24,32},{32,40},{40,48},{48,56},{56,64},{64,7... | collective-permute-start | bytes 786440 | tf_op jit(solution)/shard_map/ppermute | solution.py:192
  116.8 2.6 %collective-permute-done.1.refs_3_ = bf16[256,512]{1,0:T(8,128)(2,1)S(1)} collective-permute-done((bf16[256,512]{1,0:T(8,128)(2,1)S(1)}, bf16[256,512]{1,0:T(8,128)(2,1)S(1)}, u32[]{:S(2)}, u32[]{:S(2)}) %collective-permute-start.1) | collective-permute-done | bytes 262176 | tf_op jit(solution)/shard_map/ppermute | solution.py:192
  119.4 0.8 project.5
  120.3 0.0 copy-start.7
  120.3 1.2 copy-done.7
  121.5 6.9 %all-to-all-start.4 = ((bf16[8,32,3328]{2,1,0:T(8,128)(2,1)}), bf16[8,32,3328]{2,1,0:T(8,128)(2,1)}, u32[]{:S(2)}, u32[]{:S(2)}) async-start(bf16[8,32,3328]{2,1,0:T(8,128)(2,1)} %copy-done.7), calls=%async_computation.4 | async-start | bytes 3407872 | tf_op jit(solution)/shard_map/all_to_all | solution.py:148
  128.4 1.3 collective-permute-start.2
  129.7 0.7 collective-permute-start.3
  130.3 19.6 %collective-permute-done.2.refs_0_ = bf16[128,512]{1,0:T(8,128)(2,1)S(1)} collective-permute-done((bf16[128,512]{1,0:T(8,128)(2,1)S(1)}, bf16[128,512]{1,0:T(8,128)(2,1)S(1)}, u32[]{:S(2)}, u32[]{:S(2)}) %collective-permute-start.2) | collective-permute-done | bytes 131104 | tf_op jit(solution)/shard_map/ppermute | solution.py:214
  150.0 0.0 collective-permute-done.3.refs_1_
  150.0 0.0 all-to-all-done.4.got_ref
  150.0 2.3 %attend.5 = bf16[8,32,2048]{2,1,0:T(8,128)(2,1)S(1)} custom-call(s32[66,256]{1,0:T(8,128)S(1)} %copy-done.8, bf16[8,32,3328]{2,1,0:T(8,128)(2,1)} %all-to-all-done.4.got_ref, bf16[128,512]{1,0:T(8,128)(2,1)S(1)} %collective-permute-done.2.refs_0_, bf16[128,512]{1,0:T(8,128)(2,1)S(1)} %collective-permute-done.3.refs_1_), custom_call_target="tpu_custom_call" | custom-call | tf_op jit(solution)/shard_map/attend/pallas_call | solution.py:153
  152.3 0.0 copy-start.3
  152.3 1.0 copy-done.3
  153.3 0.0 copy-done.9
  153.3 6.7 %all-to-all-start.5 = ((bf16[8,32,2048]{2,1,0:T(8,128)(2,1)}), bf16[8,32,2048]{2,1,0:T(8,128)(2,1)S(1)}, u32[]{:S(2)}, u32[]{:S(2)}) async-start(bf16[8,32,2048]{2,1,0:T(8,128)(2,1)} %copy-done.3), calls=%async_computation.5 | async-start | bytes 2097152 | tf_op jit(solution)/shard_map/all_to_all | solution.py:148
  160.0 7.9 %collective-permute-start.4 = (bf16[128,512]{1,0:T(8,128)(2,1)S(1)}, bf16[128,512]{1,0:T(8,128)(2,1)S(1)}, u32[]{:S(2)}, u32[]{:S(2)}) collective-permute-start(bf16[128,512]{1,0:T(8,128)(2,1)S(1)} %collective-permute-done.2.refs_0_), channel_id=1, source_target_pairs={{256,504},{264,496},{272,488},{280,480},{288,472},{296,464},{304,4... | collective-permute-start | bytes 393224 | tf_op jit(solution)/shard_map/ppermute | solution.py:217
  168.0 1.3 collective-permute-start.5
  169.3 5.6 %collective-permute-done.4 = bf16[128,512]{1,0:T(8,128)(2,1)S(1)} collective-permute-done((bf16[128,512]{1,0:T(8,128)(2,1)S(1)}, bf16[128,512]{1,0:T(8,128)(2,1)S(1)}, u32[]{:S(2)}, u32[]{:S(2)}) %collective-permute-start.4) | collective-permute-done | bytes 131104 | tf_op jit(solution)/shard_map/ppermute | solution.py:217
  174.9 0.2 collective-permute-done.5
  175.1 0.7 maximum_bitcast_fusion
  175.8 0.0 all-to-all-done.5
  175.8 1.4 project_out.5
  (6 shorter events, 0.0 us)
Async XLA Ops:
  0.6 1.7 copy-start
  2.3 0.9 copy-start.4
  3.2 0.7 copy-start.10
  4.8 26.9 %copy-start.8 = (s32[66,256]{1,0:T(8,128)S(1)}, s32[66,256]{1,0:T(8,128)}, u32[]{:S(2)}) copy-start(s32[66,256]{1,0:T(8,128)} %segments_ref.5) | copy-start | bytes 202756
  31.6 19.0 %copy-start.5 = (bf16[1,256,512]{2,1,0:T(8,128)(2,1)S(1)}, bf16[1,256,512]{2,1,0:T(8,128)(2,1)}, u32[]{:S(2)}) copy-start(bf16[1,256,512]{2,1,0:T(8,128)(2,1)} %param.7) | copy-start | bytes 786436
  32.5 18.2 %copy-start.2 = (bf16[1,2048,512]{2,1,0:T(8,128)(2,1)S(1)}, bf16[1,2048,512]{2,1,0:T(8,128)(2,1)}, u32[]{:S(2)}) copy-start(bf16[1,2048,512]{2,1,0:T(8,128)(2,1)} %param.11) | copy-start | bytes 6291460
  50.7 10.9 %copy-start.1 = (bf16[1,512,2304]{2,1,0:T(8,128)(2,1)S(1)}, bf16[1,512,2304]{2,1,0:T(8,128)(2,1)}, u32[]{:S(2)}) copy-start(bf16[1,512,2304]{2,1,0:T(8,128)(2,1)} %param.10) | copy-start | bytes 7077892
  50.7 10.9 %copy-start.6 = (bf16[2,256,512]{2,1,0:T(8,128)(2,1)S(1)}, bf16[2,256,512]{2,1,0:T(8,128)(2,1)}, u32[]{:S(2)}) copy-start(bf16[2,256,512]{2,1,0:T(8,128)(2,1)} %refs_4_.1) | copy-start | bytes 1572868
  50.7 10.9 %copy-start.11 = (bf16[1,512]{1,0:T(2,128)(2,1)S(1)}, bf16[1,512]{1,0:T(2,128)(2,1)}, u32[]{:S(2)}) copy-start(bf16[1,512]{1,0:T(2,128)(2,1)} %refs_5_.1) | copy-start | bytes 3076
  51.4 10.1 %collective-permute-start = (bf16[256,512]{1,0:T(8,128)(2,1)S(1)}, bf16[256,512]{1,0:T(8,128)(2,1)S(1)}, u32[]{:S(2)}, u32[]{:S(2)}) collective-permute-start(bf16[256,512]{1,0:T(8,128)(2,1)S(1)} %project_out.3), channel_id=1, source_target_pairs={{0,8},{8,16},{16,24},{24,32},{32,40},{40,48},{48,56},{56,64},{64,7... | collective-permute-start | bytes 786440 | tf_op jit(solution)/shard_map/ppermute | solution.py:192
  107.0 12.4 %collective-permute-start.1 = (bf16[256,512]{1,0:T(8,128)(2,1)S(1)}, bf16[256,512]{1,0:T(8,128)(2,1)S(1)}, u32[]{:S(2)}, u32[]{:S(2)}) collective-permute-start(bf16[256,512]{1,0:T(8,128)(2,1)S(1)} %project_out.4), channel_id=1, source_target_pairs={{0,8},{8,16},{16,24},{24,32},{32,40},{40,48},{48,56},{56,64},{64,7... | collective-permute-start | bytes 786440 | tf_op jit(solution)/shard_map/ppermute | solution.py:192
  120.3 1.2 copy-start.7
  121.5 28.5 %all-to-all-start.4 = ((bf16[8,32,3328]{2,1,0:T(8,128)(2,1)}), bf16[8,32,3328]{2,1,0:T(8,128)(2,1)}, u32[]{:S(2)}, u32[]{:S(2)}) async-start(bf16[8,32,3328]{2,1,0:T(8,128)(2,1)} %copy-done.7), calls=%async_computation.4 | async-start | bytes 3407872 | tf_op jit(solution)/shard_map/all_to_all | solution.py:148
  128.4 21.6 %collective-permute-start.2 = (bf16[128,512]{1,0:T(8,128)(2,1)S(1)}, bf16[128,512]{1,0:T(8,128)(2,1)S(1)}, u32[]{:S(2)}, u32[]{:S(2)}) collective-permute-start(bf16[128,512]{1,0:T(8,128)(2,1)S(1)} %get-tuple-element.12), channel_id=1, source_target_pairs={{0,256},{8,264},{16,272},{24,280},{32,288},{40,296},{48,304},{56,3... | collective-permute-start | bytes 393224 | tf_op jit(solution)/shard_map/ppermute | solution.py:214
  129.7 20.3 %collective-permute-start.3 = (bf16[128,512]{1,0:T(8,128)(2,1)S(1)}, bf16[128,512]{1,0:T(8,128)(2,1)S(1)}, u32[]{:S(2)}, u32[]{:S(2)}) collective-permute-start(bf16[128,512]{1,0:T(8,128)(2,1)S(1)} %get-tuple-element.13), channel_id=1, source_target_pairs={{0,248},{8,240},{16,232},{24,224},{32,216},{40,208},{48,200},{56,1... | collective-permute-start | bytes 393224 | tf_op jit(solution)/shard_map/ppermute | solution.py:214
  150.0 3.3 %copy-start.9 = (bf16[128,512]{1,0:T(8,128)(2,1)}, bf16[128,512]{1,0:T(8,128)(2,1)S(1)}, u32[]{:S(2)}) copy-start(bf16[128,512]{1,0:T(8,128)(2,1)S(1)} %collective-permute-done.3.refs_1_) | copy-start | bytes 393220
  152.3 1.0 copy-start.3
  153.3 22.5 %all-to-all-start.5 = ((bf16[8,32,2048]{2,1,0:T(8,128)(2,1)}), bf16[8,32,2048]{2,1,0:T(8,128)(2,1)S(1)}, u32[]{:S(2)}, u32[]{:S(2)}) async-start(bf16[8,32,2048]{2,1,0:T(8,128)(2,1)} %copy-done.3), calls=%async_computation.5 | async-start | bytes 2097152 | tf_op jit(solution)/shard_map/all_to_all | solution.py:148
  160.0 14.9 %collective-permute-start.4 = (bf16[128,512]{1,0:T(8,128)(2,1)S(1)}, bf16[128,512]{1,0:T(8,128)(2,1)S(1)}, u32[]{:S(2)}, u32[]{:S(2)}) collective-permute-start(bf16[128,512]{1,0:T(8,128)(2,1)S(1)} %collective-permute-done.2.refs_0_), channel_id=1, source_target_pairs={{256,504},{264,496},{272,488},{280,480},{288,472},{296,464},{304,4... | collective-permute-start | bytes 393224 | tf_op jit(solution)/shard_map/ppermute | solution.py:217
  168.0 7.1 %collective-permute-start.5 = (bf16[128,512]{1,0:T(8,128)(2,1)}, bf16[128,512]{1,0:T(8,128)(2,1)S(1)}, u32[]{:S(2)}, u32[]{:S(2)}) collective-permute-start(bf16[128,512]{1,0:T(8,128)(2,1)} %copy-done.9), channel_id=1, source_target_pairs={{0,256},{8,264},{16,272},{24,280},{32,288},{40,296},{48,304},{56,3... | collective-permute-start | bytes 393224 | tf_op jit(solution)/shard_map/ppermute | solution.py:218

commit v9 on v8

--- a/solution.py
+++ b/solution.py
@@ -60,8 +60,9 @@
         current = arrived_ref[...]
     if earlier:
         chosen = current
+        evict = jnp.max(evict_ref[...])
         for at, earlier_ref in enumerate(earlier):
-            chosen = jnp.where(evict_ref[0] == at, earlier_ref[...], chosen)
+            chosen = jnp.where(evict == at, earlier_ref[...], chosen)
         half = chosen.shape[0] // 2
         refs[6][...] = chosen[:half]
         refs[7][...] = chosen[half:]
@@ -135,7 +136,6 @@
 
 
 VMEM = pl.BlockSpec(memory_space=pltpu.VMEM)
-SMEM = pl.BlockSpec(memory_space=pltpu.SMEM)
 ANY = pl.BlockSpec(memory_space=pl.ANY)
 PARAMS = pltpu.CompilerParams(vmem_limit_bytes=24 * 1024 * 1024)
 
@@ -194,8 +194,8 @@
             specs = [VMEM] * 4
             outs.append(shard((tokens, width)))
         if tick == ticks - 1:
-            operands[:0] = [evict_tick, *inputs]
-            specs[:0] = [SMEM] + [VMEM] * tick
+            operands[:0] = [jnp.broadcast_to(evict_tick, (8, 128)), *inputs]
+            specs[:0] = [VMEM] * (tick + 1)
             outs += [shard((tokens // 2, width))] * 2
         got = pl.pallas_call(
             functools.partial(project_kernel, parts, tick, tick == ticks - 1),

time: 178 us -> 178 us (level)
  no operation moved by 1% of the time
where the time goes in v9:
time: 178 us; the launch traced here: 177 us
  blocking collectives  88.1 us (49%)
  starting transfers between devices  40.7 us (23%)
  waiting for transfers between devices  31.4 us (18%)
  Pallas kernels  9.38 us (5%)
  local copies, waits for them, and re-layouts  5.5 us (3%)
    all_to_all x4, blocking collectives, exchange(): return lax.all_to_all(value, 'tp', split_axis=0, concat_axis=0, tiled=True)  88.1 us
    ppermute x1, waiting for transfers between devices, shards(): lax.ppermute(got[2], 'pipe', across)  19.6 us
    ppermute x2, starting transfers between devices, shards(): arrived = lax.ppermute(result, 'pipe', following)  15.9 us
    all_to_all x2, starting transfers between devices, exchange(): return lax.all_to_all(value, 'tp', split_axis=0, concat_axis=0, tiled=True)  13.6 us
    ppermute x1, starting transfers between devices, shards(): top = lax.ppermute(waited[0], 'pipe', turned_across)  7.92 us
    ppermute x2, waiting for transfers between devices, shards(): arrived = lax.ppermute(result, 'pipe', following)  5.94 us
    ppermute x1, waiting for transfers between devices, shards(): top = lax.ppermute(waited[0], 'pipe', turned_across)  5.66 us
    unnamed x24, local copies, waits for them, and re-layouts  5.49 us
  transfers between devices with their start and end apart: 8, of which 5 were waited for; matrix products, arithmetic and copies ran while one was open for 0% of the time, Pallas kernels for 0%

profile of v9, /device:TPU:71, one launch (start us, length us, event | category | flops | bytes accessed | tf_op | source)
XLA Modules:
  0.0 177.3 jit_solution(14788858744810589940)
XLA Ops:
  0.6 0.0 copy-start
  0.6 1.7 copy-done
  2.3 0.9 copy-done.4
  3.2 0.7 copy-done.10
  3.9 0.8 project.3
  4.8 0.0 copy-start.8
  4.8 26.9 %all_to_all.30.got_ref = bf16[8,32,3328]{2,1,0:T(8,128)(2,1)S(1)} all-to-all(bf16[8,32,3328]{2,1,0:T(8,128)(2,1)S(1)} %project.3), channel_id=1, replica_groups=mesh['pipe'=64,'tp'=8] {'tp'}, dimensions={0} | all-to-all | bytes 3407872 | tf_op jit(solution)/shard_map/all_to_all | solution.py:148
  31.7 0.0 copy-done.8
  31.7 0.8 attend.3
  32.5 0.0 copy-start.2
  32.5 18.2 %all_to_all.31 = bf16[8,32,2048]{2,1,0:T(8,128)(2,1)S(1)} all-to-all(bf16[8,32,2048]{2,1,0:T(8,128)(2,1)S(1)} %attend.3), channel_id=1, replica_groups=mesh['pipe'=64,'tp'=8] {'tp'}, dimensions={0} | all-to-all | bytes 2097152 | tf_op jit(solution)/shard_map/all_to_all | solution.py:148
  50.7 0.0 copy-done.5
  50.7 0.0 copy-done.2
  50.7 0.0 copy-start.11
  50.7 0.7 project_out.3
  51.4 6.8 %collective-permute-start = (bf16[256,512]{1,0:T(8,128)(2,1)S(1)}, bf16[256,512]{1,0:T(8,128)(2,1)S(1)}, u32[]{:S(2)}, u32[]{:S(2)}) collective-permute-start(bf16[256,512]{1,0:T(8,128)(2,1)S(1)} %project_out.3), channel_id=1, source_target_pairs={{0,8},{8,16},{16,24},{24,32},{32,40},{40,48},{48,56},{56,64},{64,7... | collective-permute-start | bytes 786440 | tf_op jit(solution)/shard_map/ppermute | solution.py:192
  58.3 3.3 %collective-permute-done.refs_0_ = bf16[256,512]{1,0:T(8,128)(2,1)S(1)} collective-permute-done((bf16[256,512]{1,0:T(8,128)(2,1)S(1)}, bf16[256,512]{1,0:T(8,128)(2,1)S(1)}, u32[]{:S(2)}, u32[]{:S(2)}) %collective-permute-start) | collective-permute-done | bytes 262176 | tf_op jit(solution)/shard_map/ppermute | solution.py:192
  61.6 0.0 copy-done.1
  61.6 0.0 copy-done.6
  61.6 0.0 copy-done.11
  61.6 0.9 project.4
  62.4 24.8 %all_to_all.32.got_ref = bf16[8,32,3328]{2,1,0:T(8,128)(2,1)S(1)} all-to-all(bf16[8,32,3328]{2,1,0:T(8,128)(2,1)S(1)} %get-tuple-element.9), channel_id=1, replica_groups=mesh['pipe'=64,'tp'=8] {'tp'}, dimensions={0} | all-to-all | bytes 3407872 | tf_op jit(solution)/shard_map/all_to_all | solution.py:148
  87.3 0.8 attend.4
  88.1 18.2 %all_to_all.33 = bf16[8,32,2048]{2,1,0:T(8,128)(2,1)S(1)} all-to-all(bf16[8,32,2048]{2,1,0:T(8,128)(2,1)S(1)} %attend.4), channel_id=1, replica_groups=mesh['pipe'=64,'tp'=8] {'tp'}, dimensions={0} | all-to-all | bytes 2097152 | tf_op jit(solution)/shard_map/all_to_all | solution.py:148
  106.3 0.7 project_out.4
  107.0 9.1 %collective-permute-start.1 = (bf16[256,512]{1,0:T(8,128)(2,1)S(1)}, bf16[256,512]{1,0:T(8,128)(2,1)S(1)}, u32[]{:S(2)}, u32[]{:S(2)}) collective-permute-start(bf16[256,512]{1,0:T(8,128)(2,1)S(1)} %project_out.4), channel_id=1, source_target_pairs={{0,8},{8,16},{16,24},{24,32},{32,40},{40,48},{48,56},{56,64},{64,7... | collective-permute-start | bytes 786440 | tf_op jit(solution)/shard_map/ppermute | solution.py:192
  116.8 2.6 %collective-permute-done.1.refs_3_ = bf16[256,512]{1,0:T(8,128)(2,1)S(1)} collective-permute-done((bf16[256,512]{1,0:T(8,128)(2,1)S(1)}, bf16[256,512]{1,0:T(8,128)(2,1)S(1)}, u32[]{:S(2)}, u32[]{:S(2)}) %collective-permute-start.1) | collective-permute-done | bytes 262176 | tf_op jit(solution)/shard_map/ppermute | solution.py:192
  119.4 0.9 project.5
  120.4 0.0 copy-start.7
  120.4 1.2 copy-done.7
  121.5 6.9 %all-to-all-start.4 = ((bf16[8,32,3328]{2,1,0:T(8,128)(2,1)}), bf16[8,32,3328]{2,1,0:T(8,128)(2,1)}, u32[]{:S(2)}, u32[]{:S(2)}) async-start(bf16[8,32,3328]{2,1,0:T(8,128)(2,1)} %copy-done.7), calls=%async_computation.4 | async-start | bytes 3407872 | tf_op jit(solution)/shard_map/all_to_all | solution.py:148
  128.5 1.3 collective-permute-start.2
  129.8 0.7 collective-permute-start.3
  130.4 19.6 %collective-permute-done.2.refs_0_ = bf16[128,512]{1,0:T(8,128)(2,1)S(1)} collective-permute-done((bf16[128,512]{1,0:T(8,128)(2,1)S(1)}, bf16[128,512]{1,0:T(8,128)(2,1)S(1)}, u32[]{:S(2)}, u32[]{:S(2)}) %collective-permute-start.2) | collective-permute-done | bytes 131104 | tf_op jit(solution)/shard_map/ppermute | solution.py:214
  150.1 0.0 collective-permute-done.3.refs_1_
  150.1 0.0 all-to-all-done.4.got_ref
  150.1 2.3 %attend.5 = bf16[8,32,2048]{2,1,0:T(8,128)(2,1)S(1)} custom-call(s32[66,256]{1,0:T(8,128)S(1)} %copy-done.8, bf16[8,32,3328]{2,1,0:T(8,128)(2,1)} %all-to-all-done.4.got_ref, bf16[128,512]{1,0:T(8,128)(2,1)S(1)} %collective-permute-done.2.refs_0_, bf16[128,512]{1,0:T(8,128)(2,1)S(1)} %collective-permute-done.3.refs_1_), custom_call_target="tpu_custom_call" | custom-call | tf_op jit(solution)/shard_map/attend/pallas_call | solution.py:153
  152.4 0.0 copy-start.3
  152.4 1.0 copy-done.3
  153.4 0.0 copy-done.9
  153.4 6.7 %all-to-all-start.5 = ((bf16[8,32,2048]{2,1,0:T(8,128)(2,1)}), bf16[8,32,2048]{2,1,0:T(8,128)(2,1)S(1)}, u32[]{:S(2)}, u32[]{:S(2)}) async-start(bf16[8,32,2048]{2,1,0:T(8,128)(2,1)} %copy-done.3), calls=%async_computation.5 | async-start | bytes 2097152 | tf_op jit(solution)/shard_map/all_to_all | solution.py:148
  160.1 7.9 %collective-permute-start.4 = (bf16[128,512]{1,0:T(8,128)(2,1)S(1)}, bf16[128,512]{1,0:T(8,128)(2,1)S(1)}, u32[]{:S(2)}, u32[]{:S(2)}) collective-permute-start(bf16[128,512]{1,0:T(8,128)(2,1)S(1)} %collective-permute-done.2.refs_0_), channel_id=1, source_target_pairs={{256,504},{264,496},{272,488},{280,480},{288,472},{296,464},{304,4... | collective-permute-start | bytes 393224 | tf_op jit(solution)/shard_map/ppermute | solution.py:217
  168.0 1.3 collective-permute-start.5
  169.3 5.7 %collective-permute-done.4 = bf16[128,512]{1,0:T(8,128)(2,1)S(1)} collective-permute-done((bf16[128,512]{1,0:T(8,128)(2,1)S(1)}, bf16[128,512]{1,0:T(8,128)(2,1)S(1)}, u32[]{:S(2)}, u32[]{:S(2)}) %collective-permute-start.4) | collective-permute-done | bytes 131104 | tf_op jit(solution)/shard_map/ppermute | solution.py:217
  175.0 0.2 collective-permute-done.5
  175.2 0.7 maximum_bitcast_fusion
  175.9 0.0 all-to-all-done.5
  175.9 1.4 project_out.5
  (7 shorter events, 0.0 us)
Async XLA Ops:
  0.6 1.7 copy-start
  2.3 0.9 copy-start.4
  3.2 0.7 copy-start.10
  4.8 26.9 %copy-start.8 = (s32[66,256]{1,0:T(8,128)S(1)}, s32[66,256]{1,0:T(8,128)}, u32[]{:S(2)}) copy-start(s32[66,256]{1,0:T(8,128)} %segments_ref.5) | copy-start | bytes 202756
  31.7 19.0 %copy-start.5 = (bf16[1,256,512]{2,1,0:T(8,128)(2,1)S(1)}, bf16[1,256,512]{2,1,0:T(8,128)(2,1)}, u32[]{:S(2)}) copy-start(bf16[1,256,512]{2,1,0:T(8,128)(2,1)} %param.7) | copy-start | bytes 786436
  32.5 18.2 %copy-start.2 = (bf16[1,2048,512]{2,1,0:T(8,128)(2,1)S(1)}, bf16[1,2048,512]{2,1,0:T(8,128)(2,1)}, u32[]{:S(2)}) copy-start(bf16[1,2048,512]{2,1,0:T(8,128)(2,1)} %param.11) | copy-start | bytes 6291460
  50.7 10.9 %copy-start.1 = (bf16[1,512,2304]{2,1,0:T(8,128)(2,1)S(1)}, bf16[1,512,2304]{2,1,0:T(8,128)(2,1)}, u32[]{:S(2)}) copy-start(bf16[1,512,2304]{2,1,0:T(8,128)(2,1)} %param.10) | copy-start | bytes 7077892
  50.7 10.9 %copy-start.6 = (bf16[2,256,512]{2,1,0:T(8,128)(2,1)S(1)}, bf16[2,256,512]{2,1,0:T(8,128)(2,1)}, u32[]{:S(2)}) copy-start(bf16[2,256,512]{2,1,0:T(8,128)(2,1)} %refs_4_.1) | copy-start | bytes 1572868
  50.7 10.9 %copy-start.11 = (bf16[1,512]{1,0:T(2,128)(2,1)S(1)}, bf16[1,512]{1,0:T(2,128)(2,1)}, u32[]{:S(2)}) copy-start(bf16[1,512]{1,0:T(2,128)(2,1)} %refs_5_.1) | copy-start | bytes 3076
  51.4 10.1 %collective-permute-start = (bf16[256,512]{1,0:T(8,128)(2,1)S(1)}, bf16[256,512]{1,0:T(8,128)(2,1)S(1)}, u32[]{:S(2)}, u32[]{:S(2)}) collective-permute-start(bf16[256,512]{1,0:T(8,128)(2,1)S(1)} %project_out.3), channel_id=1, source_target_pairs={{0,8},{8,16},{16,24},{24,32},{32,40},{40,48},{48,56},{56,64},{64,7... | collective-permute-start | bytes 786440 | tf_op jit(solution)/shard_map/ppermute | solution.py:192
  107.0 12.4 %collective-permute-start.1 = (bf16[256,512]{1,0:T(8,128)(2,1)S(1)}, bf16[256,512]{1,0:T(8,128)(2,1)S(1)}, u32[]{:S(2)}, u32[]{:S(2)}) collective-permute-start(bf16[256,512]{1,0:T(8,128)(2,1)S(1)} %project_out.4), channel_id=1, source_target_pairs={{0,8},{8,16},{16,24},{24,32},{32,40},{40,48},{48,56},{56,64},{64,7... | collective-permute-start | bytes 786440 | tf_op jit(solution)/shard_map/ppermute | solution.py:192
  120.4 1.2 copy-start.7
  121.5 28.5 %all-to-all-start.4 = ((bf16[8,32,3328]{2,1,0:T(8,128)(2,1)}), bf16[8,32,3328]{2,1,0:T(8,128)(2,1)}, u32[]{:S(2)}, u32[]{:S(2)}) async-start(bf16[8,32,3328]{2,1,0:T(8,128)(2,1)} %copy-done.7), calls=%async_computation.4 | async-start | bytes 3407872 | tf_op jit(solution)/shard_map/all_to_all | solution.py:148
  128.5 21.6 %collective-permute-start.2 = (bf16[128,512]{1,0:T(8,128)(2,1)S(1)}, bf16[128,512]{1,0:T(8,128)(2,1)S(1)}, u32[]{:S(2)}, u32[]{:S(2)}) collective-permute-start(bf16[128,512]{1,0:T(8,128)(2,1)S(1)} %get-tuple-element.12), channel_id=1, source_target_pairs={{0,256},{8,264},{16,272},{24,280},{32,288},{40,296},{48,304},{56,3... | collective-permute-start | bytes 393224 | tf_op jit(solution)/shard_map/ppermute | solution.py:214
  129.8 20.3 %collective-permute-start.3 = (bf16[128,512]{1,0:T(8,128)(2,1)S(1)}, bf16[128,512]{1,0:T(8,128)(2,1)S(1)}, u32[]{:S(2)}, u32[]{:S(2)}) collective-permute-start(bf16[128,512]{1,0:T(8,128)(2,1)S(1)} %get-tuple-element.13), channel_id=1, source_target_pairs={{0,248},{8,240},{16,232},{24,224},{32,216},{40,208},{48,200},{56,1... | collective-permute-start | bytes 393224 | tf_op jit(solution)/shard_map/ppermute | solution.py:214
  150.1 3.3 %copy-start.9 = (bf16[128,512]{1,0:T(8,128)(2,1)}, bf16[128,512]{1,0:T(8,128)(2,1)S(1)}, u32[]{:S(2)}) copy-start(bf16[128,512]{1,0:T(8,128)(2,1)S(1)} %collective-permute-done.3.refs_1_) | copy-start | bytes 393220
  152.4 1.0 copy-start.3
  153.4 22.5 %all-to-all-start.5 = ((bf16[8,32,2048]{2,1,0:T(8,128)(2,1)}), bf16[8,32,2048]{2,1,0:T(8,128)(2,1)S(1)}, u32[]{:S(2)}, u32[]{:S(2)}) async-start(bf16[8,32,2048]{2,1,0:T(8,128)(2,1)} %copy-done.3), calls=%async_computation.5 | async-start | bytes 2097152 | tf_op jit(solution)/shard_map/all_to_all | solution.py:148
  160.1 14.9 %collective-permute-start.4 = (bf16[128,512]{1,0:T(8,128)(2,1)S(1)}, bf16[128,512]{1,0:T(8,128)(2,1)S(1)}, u32[]{:S(2)}, u32[]{:S(2)}) collective-permute-start(bf16[128,512]{1,0:T(8,128)(2,1)S(1)} %collective-permute-done.2.refs_0_), channel_id=1, source_target_pairs={{256,504},{264,496},{272,488},{280,480},{288,472},{296,464},{304,4... | collective-permute-start | bytes 393224 | tf_op jit(solution)/shard_map/ppermute | solution.py:217
  168.0 7.1 %collective-permute-start.5 = (bf16[128,512]{1,0:T(8,128)(2,1)}, bf16[128,512]{1,0:T(8,128)(2,1)S(1)}, u32[]{:S(2)}, u32[]{:S(2)}) collective-permute-start(bf16[128,512]{1,0:T(8,128)(2,1)} %copy-done.9), channel_id=1, source_target_pairs={{0,256},{8,264},{16,272},{24,280},{32,288},{40,296},{48,304},{56,3... | collective-permute-start | bytes 393224 | tf_op jit(solution)/shard_map/ppermute | solution.py:218
